TPU v7x, 512 devices: a whole 4x8x8 slice. The times are simulated.
512 devices in a mesh: row: 16 (over z_hi, x, core), col: 32 (over y, z_lo).
Axes of the slice: x: 4, y: 8, z: 8 (z_hi: 2, z_lo: 4; z = z_hi * 4 + z_lo), core: 2. Of those that a mesh axis runs over, the one named last changes fastest.
Arguments:
- vectors: bfloat16 [16, 32, 4096], P(None, 'row', 'col')
- tile_values: bfloat16 [16, 2048, 64, 128], P('row', 'col'), may hold values from -0.09375 to 0.09375
- tile_coords: int32 [2, 16, 4096], P(None, 'row', 'col'), may hold values from 0 to 2047, as said below
- tile_counts: int32 [16, 32], P('row', 'col'), may hold values from 32 to 128, as said below
- energies: float32 [32, 4096], P('row', 'col'), may hold values from 0.3 to 3
Outputs:
- residual: bfloat16 [16, 32, 4096], P(None, 'row', 'col')
- image: float32 [16, 32, 4096], P(None, 'row', 'col')
Inputs may be any that keep to these rules, and one draw needn't show every extreme that they name: `tile_coords`: every slot of device (r, c) holds a tile row i with ((i // 2) % 32) // 2 == r and a tile column j with (j // 2) % 32 == c. The slots below the device's count hold distinct tiles with i <= j; later slots hold tiles of the same device's region and are not part of the Hamiltonian. `tile_counts`: devices (r, c) with c // 2 == r hold exactly 128 live slots; one other device holds exactly 32.
All inputs are finite; a program needn't handle non-finite values.
Results may differ from a plain program's by a relative error of at most 0.0075.
Values may be sent and summed in bfloat16 or wider, within the bound.
No kernel may reach another device: no remote copies, remote signals or barrier semaphores. Data moves between devices by JAX's collectives and lax.ppermute only.
A program may use at most 64 MiB of HBM per device.

v0:
```python
import jax
import jax.numpy as jnp
from jax import lax
from jax.sharding import PartitionSpec as P


def broadcast(value, axis, source):
    kept = jnp.where(lax.axis_index(axis) == source, value, 0).astype(value.dtype)
    return lax.psum(kept, axis)


def rayleigh_solve(gram_vectors, gram_product):
    factor = jnp.linalg.cholesky(gram_vectors)
    halfway = lax.linalg.triangular_solve(factor, gram_product, left_side=True, lower=True)
    return lax.linalg.triangular_solve(
        factor, halfway, left_side=True, lower=True, transpose_a=True
    )


def slot_sums(partial_value, packed, row_slots, col_slots, live_mask, row_tiles, column_tiles):
    forward_sum, backward_sum = partial_value
    columns, row_total, tile_size = row_tiles.shape
    slot_total = row_slots.shape[0]
    pair_count = slot_total // 2
    x_column = jnp.take(column_tiles, col_slots, axis=1).reshape(columns, pair_count, 2, tile_size)
    x_row = jnp.take(row_tiles, row_slots, axis=1).reshape(columns, pair_count, 2, tile_size)
    forward = jnp.einsum("hatb,khtb->khta", packed, x_column, preferred_element_type=jnp.float32)
    backward = jnp.einsum("hatb,khta->khtb", packed, x_row, preferred_element_type=jnp.float32)
    forward = jnp.where(
        live_mask[None, :, None], forward.reshape(columns, slot_total, tile_size), 0.0
    )
    backward = jnp.where(
        live_mask[None, :, None], backward.reshape(columns, slot_total, tile_size), 0.0
    )
    forward_sum = forward_sum.at[:, row_slots, :].add(forward)
    backward_sum = backward_sum.at[:, col_slots, :].add(backward)
    return (forward_sum, backward_sum)


def apply_hamiltonian(vector_block, packed, local_row, local_col, live_count, energies):
    columns, piece_rows, pair_rows = vector_block.shape
    tile_size = pair_rows // 2
    row_count = lax.axis_size("row")
    span_blocks = lax.axis_size("col") // row_count
    blocks = piece_rows * row_count
    row_index = lax.axis_index("row")
    column = lax.all_gather(vector_block, "row", axis=1, tiled=True)
    pieces = []
    for offset in range(span_blocks):
        received = broadcast(column, "col", row_index * span_blocks + offset)
        pieces.append(received.reshape(columns, row_count, piece_rows, pair_rows))
    row_field = jnp.stack(pieces, axis=2)
    row_tiles = row_field.reshape(columns, 2 * blocks * span_blocks, tile_size)
    column_tiles = column.reshape(columns, 2 * blocks, tile_size)
    slot_total = local_row.shape[0]
    initial = (
        jnp.zeros((columns, 2 * blocks * span_blocks, tile_size), jnp.float32),
        jnp.zeros((columns, 2 * blocks, tile_size), jnp.float32),
    )
    live_mask = jnp.arange(slot_total, dtype=jnp.int32) < live_count
    forward_sum, backward_sum = slot_sums(
        initial, packed, local_row, local_col, live_mask, row_tiles, column_tiles
    )
    forward_grid = forward_sum.reshape(columns, row_count, span_blocks, piece_rows, pair_rows)
    moved_sums = lax.all_to_all(
        lax.all_to_all(
            forward_grid.astype(jnp.bfloat16), "row", split_axis=1, concat_axis=2, tiled=True
        ),
        "col",
        split_axis=2,
        concat_axis=1,
        tiled=True,
    ).astype(forward_grid.dtype)
    column_part = lax.psum_scatter(
        backward_sum.reshape(columns, blocks, pair_rows), "row", scatter_dimension=1, tiled=True
    )
    forward_part = jnp.sum(moved_sums, axis=1).reshape(columns, piece_rows, pair_rows)
    return forward_part + column_part + energies[None] * vector_block.astype(jnp.float32)


def shards(vectors, tile_values, tile_coords, tile_counts, energies):
    columns, piece_rows, pair_rows = vectors.shape
    tile_size = pair_rows // 2
    slot_total = tile_coords.shape[2]
    col_groups = lax.axis_size("col")
    span_blocks = col_groups // lax.axis_size("row")
    tile_row = tile_coords[0, 0]
    tile_col = tile_coords[1, 0]
    row_pair = tile_row // 2
    block_offset = row_pair % col_groups - lax.axis_index("row") * span_blocks
    row_major = row_pair // col_groups
    local_row = (
        (row_major // piece_rows * span_blocks + block_offset) * piece_rows + row_major % piece_rows
    ) * 2 + tile_row % 2
    local_col = tile_col // 2 // col_groups * 2 + tile_col % 2
    packed = tile_values[0].reshape(slot_total // 2, tile_size, 2, tile_size)
    live_count = tile_counts[0, 0]
    product = apply_hamiltonian(vectors, packed, local_row, local_col, live_count, energies)
    flat_vectors = vectors.reshape(columns, -1)
    flat_product = product.reshape(columns, -1)
    gram_vectors = jnp.dot(flat_vectors, flat_vectors.T, preferred_element_type=jnp.float32)
    gram_product = jnp.dot(
        flat_vectors.astype(jnp.float32), flat_product.T, precision=lax.Precision.HIGHEST
    )
    gram_vectors, gram_product = lax.psum((gram_vectors, gram_product), ("row", "col"))
    rayleigh = rayleigh_solve(gram_vectors, gram_product)
    shifted = jnp.dot(rayleigh.T, flat_vectors.astype(jnp.float32), precision=lax.Precision.HIGHEST)
    residual = (flat_product - shifted).astype(jnp.bfloat16).reshape(vectors.shape)
    image = apply_hamiltonian(residual, packed, local_row, local_col, live_count, energies)
    return (residual, image)


def solution(mesh):
    in_specs = (
        P(None, "row", "col"),
        P("row", "col", None, None),
        P(None, "row", "col"),
        P("row", "col"),
        P("row", "col"),
    )
    out_specs = (P(None, "row", "col"), P(None, "row", "col"))
    return jax.shard_map(shards, mesh=mesh, in_specs=in_specs, out_specs=out_specs, check_vma=False)
```

profile of v0, /device:TPU:6, one launch (start us, length us, event | category | flops | bytes accessed | tf_op | source)
XLA Modules:
  0.0 1060.7 jit_solution(17080266460261790020)
XLA Ops:
  7.2 0.8 copy.163
  8.0 27.0 %all_gather.6 = bf16[16,32,128]{2,0,1:T(8,128)(2,1)S(1)} all-gather(bf16[16,2,128]{2,0,1:T(8,128)(2,1)S(1)} %copy.163), channel_id=1, replica_groups=mesh['row'=16,'col'=32] {'row'}, dimensions={1}, use_global_device_ids=true | all-gather | bytes 139264 | tf_op jit(solution)/shard_map/all_gather | solution.py:47
  35.0 0.8 copy.172
  35.8 0.8 copy.173
  36.6 0.7 compare_and_fusion
  37.3 0.9 reshape_squeeze.3
  39.2 0.7 gather_fusion
  39.9 0.2 broadcast_select_fusion.3
  40.1 1.2 fusion.6
  41.4 307.1 %all-reduce.8.cloned.1.call-done = (bf16[16,16,1,2,128]{4,3,2,1,0:T(2,128)(2,1)}, bf16[16,16,1,2,128]{4,3,2,1,0:T(2,128)(2,1)}) async-done(((bf16[16,16,1,2,128]{4,3,2,1,0:T(2,128)(2,1)}, bf16[16,16,1,2,128]{4,3,2,1,0:T(2,128)(2,1)}), (bf16[16,16,1,2,128]{4,3,2,1,0:T(2,128)(2,1)}, bf16[16,16,1,2,128]{4,3,2,1,0:T(2,128)(2,1)})) %all-reduce.8.cloned.1.call-update) | async-done | bytes 262160 | tf_op jit(solution)/shard_map/psum | solution.py:9
  348.4 1.3 pad_maximum_fusion
  349.8 1.1 reshape.540
  350.8 2.2 copy.174
  353.0 2.5 gather_fusion.1
  355.6 1.2 broadcast_select_fusion.1
  356.8 0.6 fusion.4
  357.5 1.7 bitcast_select_fusion.2
  359.2 10.5 scatter_fusion
  369.7 0.4 copy.167
  370.2 0.3 copy.168
  370.5 0.3 convert_element_type.53
  370.7 0.2 copy.169
  371.0 18.8 %all_to_all.42 = bf16[16,16,2,2,128]{4,3,2,0,1:T(2,128)(2,1)S(1)} all-to-all(bf16[16,16,2,2,128]{4,3,2,0,1:T(2,128)(2,1)S(1)} %copy.169), channel_id=1, replica_groups=mesh['row'=16,'col'=32] {'row'}, dimensions={1} | all-to-all | bytes 524288 | tf_op jit(solution)/shard_map/all_to_all | solution.py:66
  389.8 0.9 copy.171
  390.7 7.1 all-to-all-start.1
  398.0 10.5 scatter_fusion.1
  408.8 0.8 copy.177
  409.9 2.1 all-to-all-done.1
  412.0 0.2 convert_reduce_fusion.1
  412.2 80.0 %reduce-scatter.3.cloned.1.call-done = f32[16,2,128]{2,0,1:T(8,128)} async-done(((f32[16,32,128]{2,0,1:T(8,128)}), f32[16,2,128]{2,0,1:T(8,128)}) %reduce-scatter.3.cloned.1.call-update) | async-done | bytes 16400 | tf_op jit(solution)/shard_map/reduce_scatter | solution.py:74
  492.2 0.7 fusion.11
  493.1 94.6 %all-reduce = (f32[16,16]{0,1:T(8,128)S(1)}, f32[16,16]{0,1:T(8,128)S(1)}) all-reduce(f32[16,16]{0,1:T(8,128)S(1)} %convolution_bitcast_fusion, f32[16,16]{0,1:T(8,128)S(1)} %convolution_bitcast_fusion.1), channel_id=1, replica_groups=mesh['row'=16,'col'=32] {'row','col'}, use_global_device_ids=true, to_apply=%region_9.12 | all-reduce | flops 512 | bytes 4096 | tf_op jit(solution)/shard_map/psum | solution.py:105
  587.8 1.5 cholesky.16
  589.2 0.6 compare_reduce_fusion
  589.9 0.6 fusion.12
  590.5 1.2 custom-call.8
  591.8 0.2 fusion.17
  592.3 23.7 %all_gather.7 = bf16[16,32,128]{2,0,1:T(8,128)(2,1)S(1)} all-gather(bf16[16,2,128]{2,0,1:T(8,128)(2,1)S(1)} %copy_bitcast_fusion), channel_id=1, replica_groups=mesh['row'=16,'col'=32] {'row'}, dimensions={1}, use_global_device_ids=true | all-gather | bytes 139264 | tf_op jit(solution)/shard_map/all_gather | solution.py:47
  616.0 0.8 copy.194
  616.8 0.8 copy.195
  617.9 1.5 gather_fusion.2
  619.4 304.7 %all-reduce.6.cloned.1.call-done = (bf16[16,16,1,2,128]{4,3,2,1,0:T(2,128)(2,1)}, bf16[16,16,1,2,128]{4,3,2,1,0:T(2,128)(2,1)}) async-done(((bf16[16,16,1,2,128]{4,3,2,1,0:T(2,128)(2,1)}, bf16[16,16,1,2,128]{4,3,2,1,0:T(2,128)(2,1)}), (bf16[16,16,1,2,128]{4,3,2,1,0:T(2,128)(2,1)}, bf16[16,16,1,2,128]{4,3,2,1,0:T(2,128)(2,1)})) %all-reduce.6.cloned.1.call-update) | async-done | bytes 262160 | tf_op jit(solution)/shard_map/psum | solution.py:9
  924.1 1.3 pad_maximum_fusion.1
  925.5 0.2 reshape.550
  925.7 0.3 copy.196
  926.1 0.7 gather_fusion.3
  926.8 1.6 broadcast_select_fusion
  928.4 1.2 fusion.2
  929.5 0.7 fusion
  930.2 0.2 bitcast_select_fusion
  930.5 5.2 scatter_fusion.2
  935.7 0.4 copy.189
  936.1 0.3 copy.190
  936.4 0.3 convert_element_type.58
  936.7 0.2 copy.191
  936.9 18.8 %all_to_all.43 = bf16[16,16,2,2,128]{4,3,2,0,1:T(2,128)(2,1)S(1)} all-to-all(bf16[16,16,2,2,128]{4,3,2,0,1:T(2,128)(2,1)S(1)} %copy.191), channel_id=1, replica_groups=mesh['row'=16,'col'=32] {'row'}, dimensions={1} | all-to-all | bytes 524288 | tf_op jit(solution)/shard_map/all_to_all | solution.py:66
  955.8 0.9 copy.193
  956.7 7.1 all-to-all-start.3
  963.9 5.2 scatter_fusion.3
  969.5 0.9 copy.199
  970.4 7.5 all-to-all-done.3
  977.9 0.2 convert_reduce_fusion
  978.1 74.7 %reduce-scatter.5.cloned.1.call-done = f32[16,2,128]{2,0,1:T(8,128)} async-done(((f32[16,32,128]{2,0,1:T(8,128)}), f32[16,2,128]{2,0,1:T(8,128)}) %reduce-scatter.5.cloned.1.call-update) | async-done | bytes 16400 | tf_op jit(solution)/shard_map/reduce_scatter | solution.py:74
  1052.8 1.3 fusion.9
  (49 shorter events, 2.6 us)
Async XLA Ops:
  7.2 30.2 %copy-start = (bf16[1,64,64,128]{3,2,1,0:T(8,128)(2,1)S(1)}, bf16[1,64,64,128]{3,2,1,0:T(8,128)(2,1)}, u32[]{:S(2)}) copy-start(bf16[1,64,64,128]{3,2,1,0:T(8,128)(2,1)} %param.10) | copy-start | bytes 3145732
  7.2 341.3 %all-reduce.8.cloned.1.call-start = ((), (), s32[]{:S(2)}) async-start(), calls=%async_computation.9 | async-start | bytes 524288 | tf_op jit(solution)/shard_map/psum | solution.py:9
  40.1 1.2 copy-start.4
  390.7 21.2 %all-to-all-start.1 = ((bf16[16,1,32,2,128]{4,3,0,1,2:T(2,128)(2,1)}), bf16[16,1,32,2,128]{4,3,0,1,2:T(2,128)(2,1)S(1)}, u32[]{:S(2)}, u32[]{:S(2)}) async-start(bf16[16,1,32,2,128]{4,3,0,1,2:T(2,128)(2,1)} %copy.171), calls=%async_computation.1 | async-start | bytes 524288 | tf_op jit(solution)/shard_map/all_to_all | solution.py:65
  397.9 94.3 %reduce-scatter.3.cloned.1.call-start = ((), (), s32[]{:S(2)}) async-start(), calls=%async_computation.6 | async-start | bytes 278528 | tf_op jit(solution)/shard_map/reduce_scatter | solution.py:74
  408.5 1.3 copy-start.1
  408.5 83.7 %copy-start.3 = (f32[2,128]{1,0:T(2,128)S(1)}, f32[2,128]{1,0:T(2,128)}, u32[]{:S(2)}) copy-start(f32[2,128]{1,0:T(2,128)} %param.13) | copy-start | bytes 3076
  409.7 514.4 %all-reduce.6.cloned.1.call-start = ((), (), s32[]{:S(2)}) async-start(), calls=%async_computation.8 | async-start | bytes 524288 | tf_op jit(solution)/shard_map/psum | solution.py:9
  956.7 21.2 %all-to-all-start.3 = ((bf16[16,1,32,2,128]{4,3,0,1,2:T(2,128)(2,1)}), bf16[16,1,32,2,128]{4,3,0,1,2:T(2,128)(2,1)S(1)}, u32[]{:S(2)}, u32[]{:S(2)}) async-start(bf16[16,1,32,2,128]{4,3,0,1,2:T(2,128)(2,1)} %copy.193), calls=%async_computation.4 | async-start | bytes 524288 | tf_op jit(solution)/shard_map/all_to_all | solution.py:65
  963.8 89.0 %reduce-scatter.5.cloned.1.call-start = ((), (), s32[]{:S(2)}) async-start(), calls=%async_computation.7 | async-start | bytes 278528 | tf_op jit(solution)/shard_map/reduce_scatter | solution.py:74
  970.4 83.8 %copy-start.2 = (bf16[16,2,128]{2,1,0:T(2,128)(2,1)}, bf16[16,2,128]{2,1,0:T(2,128)(2,1)S(1)}, u32[]{:S(2)}) copy-start(bf16[16,2,128]{2,1,0:T(2,128)(2,1)S(1)} %reshape.546) | copy-start | bytes 24580
Sparse Core Ops, SparseCore 0:
  36.7 311.7 all-reduce.7
  409.8 82.3 reduce-scatter.2
  617.7 306.4 all-reduce.5
  970.5 82.3 reduce-scatter.4
where the time goes:
time: 1060 us
  waiting for transfers between devices  776 us (73%)
  blocking collectives  183 us (17%)
  other arithmetic  46.4 us (4%)
  local copies, waits for them, and re-layouts  21.5 us (2%)
  between operations  14.8 us (1%)
  starting transfers between devices  14.4 us (1%)
    psum x2, waiting for transfers between devices, broadcast(): return lax.psum(kept, axis)  612 us
    reduce_scatter x2, waiting for transfers between devices, apply_hamiltonian(): lax.psum_scatter(backward_sum.reshape(columns, blocks, pair_rows), 'row',...  155 us
    psum x1, blocking collectives, shards(): lax.psum((gram_vectors, gram_product), ('row', 'col'))  94.6 us
    all_gather x2, blocking collectives, apply_hamiltonian(): column = lax.all_gather(vector_block, 'row', axis=1, tiled=True)  50.6 us
    all_to_all x2, blocking collectives, apply_hamiltonian(): lax.all_to_all(forward_grid.astype(jnp.bfloat16), 'row', split_axis=1, co...  37.6 us
  transfers between devices with their start and end apart: 6, of which 6 were waited for; matrix products, arithmetic and copies ran while one was open for 2% of the time, Pallas kernels for 0%

commit v1 on v0

v1 whole, which is shorter than its diff:
```python
import functools

import jax
import jax.numpy as jnp
from jax import lax
from jax.experimental import pallas as pl
from jax.experimental.pallas import tpu as pltpu
from jax.sharding import PartitionSpec as P

F32 = jnp.float32
BF16 = jnp.bfloat16
VECS = 16
LANES = 128
HALF = 64
NR = 16
NC = 32
GROUP = 6
PAIRS = NR * GROUP
SLOTS = 128
DEAD = 2 * PAIRS
VMEM = pl.BlockSpec(memory_space=pltpu.VMEM)
SMEM = pl.BlockSpec(memory_space=pltpu.SMEM)
NT_DIMS = (((1,), (1,)), ((), ()))


def shape(*dims, dtype=BF16):
    return jax.ShapeDtypeStruct(dims, dtype)


def call(kernel, outs, n_in, scratch=(), smem_first=False, limit=None):
    specs = [VMEM] * n_in
    if smem_first:
        specs[0] = SMEM
    return pl.pallas_call(
        kernel,
        out_shape=outs,
        in_specs=specs,
        out_specs=jax.tree.map(lambda _: VMEM, outs),
        scratch_shapes=list(scratch),
        compiler_params=pltpu.CompilerParams(vmem_limit_bytes=limit or 32 * 1024 * 1024),
    )


def lane_index():
    return lax.broadcasted_iota(jnp.int32, (VECS, LANES), 1)


def split3(value):
    high = value.astype(BF16)
    rest = value - high.astype(F32)
    middle = rest.astype(BF16)
    low = (rest - middle.astype(F32)).astype(BF16)
    return high, middle, low


def spread_kernel(x_ref, out_ref):
    for k in range(NC):
        out_ref[k] = x_ref[...]


def regroup_kernel(own_ref, in_ref, out_ref):
    for r in range(NR):
        for s in range(2):
            for j in range(2):
                out_ref[r, 2 * s + j] = in_ref[2 * r + s, j]
        for j in range(2):
            out_ref[r, 4 + j] = own_ref[j]


def tiles_kernel(with_gram, *refs):
    if with_gram:
        idx_ref, x_ref, w_ref, own_ref, e_ref, out_ref, field, acc_row, acc_col = refs
    else:
        idx_ref, x_ref, w_ref, out_ref, field, acc_row, acc_col = refs
    lane = lane_index()
    low_half = lane < HALF
    zero = jnp.zeros((VECS, LANES), F32)
    half_mask = [low_half, jnp.logical_not(low_half)]
    half_one = [jnp.where(m, 1.0, 0.0).astype(BF16) for m in half_mask]

    def duplicate(r, carry):
        for g in range(GROUP):
            value = x_ref[r, g].astype(F32)
            turned = pltpu.roll(value, HALF, 1)
            field[(r * GROUP + g) * 2] = jnp.where(low_half, value, turned).astype(BF16)
            field[(r * GROUP + g) * 2 + 1] = jnp.where(low_half, turned, value).astype(BF16)
            for h in range(2):
                acc_row[(r * GROUP + g) * 2 + h] = zero
                acc_col[(r * GROUP + g) * 2 + h] = zero
        return carry

    lax.fori_loop(0, NR, duplicate, 0)
    field[DEAD] = zero.astype(BF16)
    acc_row[DEAD] = zero
    acc_col[DEAD] = zero

    def group(q, carry):
        rows, cols = [], []
        for k in range(4):
            rows.append(idx_ref[0, q * 4 + k])
            cols.append(idx_ref[1, q * 4 + k])
        w = w_ref[pl.ds(2 * q, 2)].reshape(2 * HALF, LANES)
        left_f = jnp.concatenate([field[cols[k]] * half_one[k % 2] for k in range(4)], axis=0)
        left_b = jnp.concatenate([field[rows[k]] * half_one[k // 2] for k in range(4)], axis=0)
        forward = lax.dot_general(left_f, w, NT_DIMS, preferred_element_type=F32)
        backward = jnp.dot(left_b, w, preferred_element_type=F32)
        for k in range(4):
            piece = slice(k * VECS, (k + 1) * VECS)
            acc_row[rows[k]] += jnp.where(half_mask[k // 2], forward[piece], 0.0)
            acc_col[cols[k]] += jnp.where(half_mask[k % 2], backward[piece], 0.0)
        return carry

    lax.fori_loop(0, SLOTS // 4, group, 0)

    def fold(acc, p):
        first, second = acc[2 * p], acc[2 * p + 1]
        return jnp.where(low_half, first, second) + pltpu.roll(
            jnp.where(low_half, second, first), HALF, 1
        )

    def pack(r, carry):
        for g in range(4):
            out_ref[r, g] = fold(acc_row, r * GROUP + g).astype(BF16)
        for g in range(4, GROUP):
            total = fold(acc_col, r * GROUP + g)
            out_ref[r, g] = total.astype(BF16)
            if with_gram:
                x = x_ref[r, g]
                for part in split3(total):
                    carry = carry + lax.dot_general(x, part, NT_DIMS, preferred_element_type=F32)
        return carry

    if not with_gram:
        lax.fori_loop(0, NR, pack, 0)
        return
    cross = lax.fori_loop(0, NR, pack, jnp.zeros((VECS, VECS), F32))
    gram = jnp.zeros((VECS, VECS), F32)
    for j in range(2):
        own = own_ref[j]
        gram = gram + lax.dot_general(own, own, NT_DIMS, preferred_element_type=F32)
        weighted = own.astype(F32) * (0.5 * e_ref[j : j + 1, :])
        for part in split3(weighted):
            cross = cross + lax.dot_general(own, part, NT_DIMS, preferred_element_type=F32)
    message = gram_message(gram, cross)
    for r in range(NR):
        out_ref[r, GROUP] = message


def widen(value):
    return jnp.concatenate([value, jnp.zeros((VECS, LANES - VECS), F32)], axis=1)


def message_of(gram, cross):
    total = jnp.zeros((VECS, LANES), F32)
    for base, value in ((0, gram), (HALF, cross)):
        for n, part in enumerate(split3(value)):
            part = part.astype(F32)
            total = total + (pltpu.roll(part, base + n * VECS, 1) if base + n else part)
    return total.astype(BF16)


def gram_message(gram, cross):
    return message_of(widen(gram), widen(cross))


def read_message(total):
    keep = lane_index() < VECS
    found = []
    for base in (0, HALF):
        value = jnp.zeros((VECS, LANES), F32)
        for n in (2, 1, 0):
            shift = base + n * VECS
            value = value + (pltpu.roll(total, LANES - shift, 1) if shift else total)
        found.append(jnp.where(keep, value, 0.0))
    return found


def collect_kernel(with_gram, in_ref, out_ref, back_ref):
    for r in range(NR):
        for s in range(2):
            for j in range(2):
                out_ref[2 * r + s, j] = in_ref[r, 2 * s + j]
    for j in range(2):
        total = in_ref[0, 4 + j].astype(F32)
        for r in range(1, NR):
            total = total + in_ref[r, 4 + j].astype(F32)
        back_ref[j] = total
    if with_gram:
        total = in_ref[0, GROUP].astype(F32)
        for r in range(1, NR):
            total = total + in_ref[r, GROUP].astype(F32)
        message = message_of(*read_message(total))
        for c in range(NC):
            out_ref[c, 2] = message


def solve_kernel(in_ref, back_ref, own_ref, e_ref, out_ref, residual_ref):
    def total_of(g):
        total = in_ref[0, g].astype(F32)
        for c in range(1, NC):
            total = total + in_ref[c, g].astype(F32)
        return total

    gram, cross = read_message(total_of(2))
    wide = jnp.concatenate([cross, jnp.zeros((LANES - VECS, LANES), F32)], axis=0)
    cross = cross + jnp.transpose(wide)[:VECS]
    state = jnp.concatenate([gram, cross], axis=0)
    lane = lax.broadcasted_iota(jnp.int32, (2 * VECS, LANES), 1)
    for p in range(VECS):
        column = state[:, p : p + 1]
        pivot = state[p : p + 1, :]
        scaled = pivot / state[p : p + 1, p : p + 1]
        scaled = jnp.where(lane[:1] == p, 0.0, scaled)
        own_column = column / state[p : p + 1, p : p + 1]
        state = jnp.where(lane == p, own_column, state - column * scaled)
    mix = state[VECS:]
    for j in range(2):
        v = own_ref[j].astype(F32)
        product = total_of(j) + back_ref[j] + e_ref[j : j + 1, :] * v
        shifted = jnp.zeros((VECS, LANES), F32)
        for k in range(VECS):
            shifted = shifted + mix[:, k : k + 1] * v[k : k + 1, :]
        value = (product - shifted).astype(BF16)
        residual_ref[j] = value
        for c in range(NC):
            out_ref[c, j] = value


def finish_kernel(in_ref, back_ref, own_ref, e_ref, out_ref):
    for j in range(2):
        total = in_ref[0, j].astype(F32)
        for c in range(1, NC):
            total = total + in_ref[c, j].astype(F32)
        out_ref[j] = total + back_ref[j] + e_ref[j : j + 1, :] * own_ref[j].astype(F32)


def exchange(value, axis):
    return lax.all_to_all(value, axis, split_axis=0, concat_axis=0, tiled=True)


def apply_tiles(own, spread, index, tiles, energies, with_gram):
    by_block = exchange(spread, "col")
    grouped = call(regroup_kernel, shape(NR, GROUP, VECS, LANES), 2)(own, by_block)
    fields = exchange(grouped, "row")
    scratch = [
        pltpu.VMEM((DEAD + 1, VECS, LANES), BF16),
        pltpu.VMEM((DEAD + 1, VECS, LANES), F32),
        pltpu.VMEM((DEAD + 1, VECS, LANES), F32),
    ]
    extra = 1 if with_gram else 0
    args = (index, fields, tiles) + ((own, energies) if with_gram else ())
    partial = call(
        functools.partial(tiles_kernel, with_gram),
        shape(NR, GROUP + extra, VECS, LANES),
        len(args),
        scratch,
        smem_first=True,
    )(*args)
    moved = exchange(partial, "row")
    by_block, back = call(
        functools.partial(collect_kernel, with_gram),
        (shape(NC, 2 + extra, VECS, LANES), shape(2, VECS, LANES, dtype=F32)),
        1,
    )(moved)
    return exchange(by_block, "col"), back


def shards(vectors, tile_values, tile_coords, tile_counts, energies):
    tiles = tile_values[0]
    coords = tile_coords[:, 0]
    pair = coords // 2
    major = pair // NC
    within = jnp.stack([(pair[0] % 2) * 2 + major[0] % 2, 4 + major[1] % 2])
    index = ((major // 2) * GROUP + within) * 2 + coords % 2
    live = jnp.arange(SLOTS, dtype=jnp.int32) < tile_counts[0, 0]
    index = jnp.where(live[None], index, DEAD)

    own = jnp.transpose(vectors, (1, 0, 2))
    spread = call(spread_kernel, shape(NC, 2, VECS, LANES), 1)(own)
    forward, back = apply_tiles(own, spread, index, tiles, energies, True)
    spread, residual = call(
        solve_kernel, (shape(NC, 2, VECS, LANES), shape(2, VECS, LANES)), 4
    )(forward, back, own, energies)
    forward, back = apply_tiles(residual, spread, index, tiles, energies, False)
    image = call(finish_kernel, shape(2, VECS, LANES, dtype=F32), 4)(
        forward, back, residual, energies
    )
    return jnp.transpose(residual, (1, 0, 2)), jnp.transpose(image, (1, 0, 2))


def solution(mesh):
    in_specs = (
        P(None, "row", "col"),
        P("row", "col", None, None),
        P(None, "row", "col"),
        P("row", "col"),
        P("row", "col"),
    )
    out_specs = (P(None, "row", "col"), P(None, "row", "col"))
    return jax.shard_map(shards, mesh=mesh, in_specs=in_specs, out_specs=out_specs, check_vma=False)
```

time: 1060 us -> 193 us (0.18)
  waiting for transfers between devices: 776 us -> 38.4 us
  blocking collectives: 183 us -> 93.2 us
  other arithmetic: 46.4 us -> 0.05 us
  Pallas kernels: 0 us -> 23.1 us
  local copies, waits for them, and re-layouts: 21.5 us -> 2.6 us
  starting transfers between devices: 14.4 us -> 33.2 us
  between operations: 14.8 us -> 1.36 us
    psum x2 -> x0, waiting for transfers between devices: 612 us -> none  [broadcast(): return lax.psum(kept, axis)]
    reduce_scatter x2 -> x0, waiting for transfers between devices: 155 us -> none  [apply_hamiltonian(): lax.psum_scatter(backward_sum.reshape(columns, blocks, pair_rows), 'row',...]
    psum x1 -> x0, blocking collectives: 94.6 us -> none  [shards(): lax.psum((gram_vectors, gram_product), ('row', 'col'))]
    all_to_all x2 -> x5, blocking collectives: 37.6 us -> 93.2 us  [exchange(): return lax.all_to_all(value, axis, split_axis=0, concat_axis=0, tiled=True)]
    all_gather x2 -> x0, blocking collectives: 50.6 us -> none  [apply_hamiltonian(): column = lax.all_gather(vector_block, 'row', axis=1, tiled=True)]
    scatter-add x4 -> x0, other arithmetic: 31.4 us -> none  [the longest x2 15.7 us: slot_sums(): backward_sum = backward_sum.at[:, col_slots, :].add(backward)]
    all_to_all x2 -> x3, waiting for transfers between devices: 9.59 us -> 38.4 us  [exchange(): return lax.all_to_all(value, axis, split_axis=0, concat_axis=0, tiled=True)]
    pallas_call x0 -> x9, Pallas kernels: none -> 23.1 us  [the longest x2 19 us: apply_tiles(): call(functools.partial(tiles_kernel, with_gram), shape(NR, GROUP + extra,...]
  transfers between devices with their start and end apart: 6 -> 3, of which waited for: 6 -> 3; matrix products, arithmetic and copies ran while one was open for 2% -> 0% of each run, Pallas kernels for 0% -> 0%
where the time goes in v1:
time: 193 us; the launch traced here: 192 us
  blocking collectives  93.2 us (48%)
  waiting for transfers between devices  38.4 us (20%)
  starting transfers between devices  33.2 us (17%)
  Pallas kernels  23.1 us (12%)
  local copies, waits for them, and re-layouts  2.6 us (1%)
    all_to_all x5, blocking collectives, exchange(): return lax.all_to_all(value, axis, split_axis=0, concat_axis=0, tiled=True)  93.2 us
    all_to_all x3, waiting for transfers between devices, exchange(): return lax.all_to_all(value, axis, split_axis=0, concat_axis=0, tiled=True)  38.4 us
    all_to_all x3, starting transfers between devices, exchange(): return lax.all_to_all(value, axis, split_axis=0, concat_axis=0, tiled=True)  33.2 us
    pallas_call x2, Pallas kernels, apply_tiles(): call(functools.partial(tiles_kernel, with_gram), shape(NR, GROUP + extra,...  19 us
  transfers between devices with their start and end apart: 3, of which 3 were waited for; matrix products, arithmetic and copies ran while one was open for 0% of the time, Pallas kernels for 0%

profile of v1, /device:TPU:6, one launch (start us, length us, event | category | flops | bytes accessed | tf_op | source)
XLA Modules:
  0.0 192.0 jit_solution(18419413077624534863)
XLA Ops:
  0.6 0.7 copy.11
  1.3 0.7 shard_map.68
  2.1 0.0 copy-start
  2.1 13.0 %all-to-all-start = ((bf16[32,2,16,128]{3,2,1,0:T(8,128)(2,1)}), bf16[32,2,16,128]{3,2,1,0:T(8,128)(2,1)S(1)}, u32[]{:S(2)}, u32[]{:S(2)}) async-start(bf16[32,2,16,128]{3,2,1,0:T(8,128)(2,1)} %shard_map.68), calls=%async_computation | async-start | bytes 524288 | tf_op jit(solution)/shard_map/all_to_all | solution.py:238
  15.8 12.6 %all-to-all-done.in_ref = bf16[32,2,16,128]{3,2,1,0:T(8,128)(2,1)S(1)} async-done(((bf16[32,2,16,128]{3,2,1,0:T(8,128)(2,1)}), bf16[32,2,16,128]{3,2,1,0:T(8,128)(2,1)S(1)}, u32[]{:S(2)}, u32[]{:S(2)}) %all-to-all-start) | async-done | bytes 262176 | tf_op jit(solution)/shard_map/all_to_all | solution.py:238
  28.4 0.8 shard_map.69
  29.2 10.5 %all-to-all-start.1 = ((bf16[16,6,16,128]{3,2,1,0:T(8,128)(2,1)}), bf16[16,6,16,128]{3,2,1,0:T(8,128)(2,1)S(1)}, u32[]{:S(2)}, u32[]{:S(2)}) async-start(bf16[16,6,16,128]{3,2,1,0:T(8,128)(2,1)} %shard_map.69), calls=%async_computation.1 | async-start | bytes 786432 | tf_op jit(solution)/shard_map/all_to_all | solution.py:238
  39.7 0.0 copy-start.2
  39.7 0.7 copy-done.2
  40.5 0.0 copy-start.1
  40.5 12.6 %all-to-all-done.1.refs_1_ = bf16[16,6,16,128]{3,2,1,0:T(8,128)(2,1)S(1)} async-done(((bf16[16,6,16,128]{3,2,1,0:T(8,128)(2,1)}), bf16[16,6,16,128]{3,2,1,0:T(8,128)(2,1)S(1)}, u32[]{:S(2)}, u32[]{:S(2)}) %all-to-all-start.1) | async-done | bytes 393248 | tf_op jit(solution)/shard_map/all_to_all | solution.py:238
  53.1 0.0 copy-done
  53.1 0.0 copy-done.1
  53.1 10.6 %shard_map.70 = bf16[16,7,16,128]{3,2,1,0:T(8,128)(2,1)S(1)} custom-call(s32[2,128]{1,0:T(2,128)S(1)} %broadcast_select_fusion.refs_0_, bf16[16,6,16,128]{3,2,1,0:T(8,128)(2,1)S(1)} %all-to-all-done.1.refs_1_, bf16[64,64,128]{2,1,0:T(8,128)(2,1)S(1)} %bitcast.9, bf16[2,16,128]{2,1,0:T(8,128)(2,1)S(1)} %bitcast.13, f32[2,128]{1,0:T(2,128)S(1)} %copy-done.1), custom_call_target="tpu_custom_call" | custom-call | tf_op jit(solution)/shard_map/pallas_call | solution.py:252
  63.7 16.6 %all_to_all.40.in_ref = bf16[16,7,16,128]{3,2,1,0:T(8,128)(2,1)S(1)} all-to-all(bf16[16,7,16,128]{3,2,1,0:T(8,128)(2,1)S(1)} %shard_map.70), channel_id=1, replica_groups=mesh['row'=16,'col'=32] {'row'}, dimensions={0} | all-to-all | bytes 917504 | tf_op jit(solution)/shard_map/all_to_all | solution.py:238
  80.3 0.2 shard_map.71
  80.5 26.3 %all_to_all.41.in_ref = bf16[32,3,16,128]{3,2,1,0:T(8,128)(2,1)S(1)} all-to-all(bf16[32,3,16,128]{3,2,1,0:T(8,128)(2,1)S(1)} %get-tuple-element.8), channel_id=1, replica_groups=mesh['row'=16,'col'=32] {'col'}, dimensions={0} | all-to-all | bytes 786432 | tf_op jit(solution)/shard_map/all_to_all | solution.py:238
  106.8 1.6 shard_map.72
  108.5 16.6 %all_to_all.42.in_ref = bf16[32,2,16,128]{3,2,1,0:T(8,128)(2,1)S(1)} all-to-all(bf16[32,2,16,128]{3,2,1,0:T(8,128)(2,1)S(1)} %get-tuple-element.11), channel_id=1, replica_groups=mesh['row'=16,'col'=32] {'col'}, dimensions={0} | all-to-all | bytes 524288 | tf_op jit(solution)/shard_map/all_to_all | solution.py:238
  125.2 17.7 %all_to_all.43.refs_1_ = bf16[16,6,16,128]{3,2,1,0:T(8,128)(2,1)S(1)} all-to-all(bf16[16,6,16,128]{3,2,1,0:T(8,128)(2,1)S(1)} %shard_map.73), channel_id=1, replica_groups=mesh['row'=16,'col'=32] {'row'}, dimensions={0} | all-to-all | bytes 786432 | tf_op jit(solution)/shard_map/all_to_all | solution.py:238
  142.9 8.4 %shard_map.74 = bf16[16,6,16,128]{3,2,1,0:T(8,128)(2,1)S(1)} custom-call(s32[2,128]{1,0:T(2,128)S(1)} %broadcast_select_fusion.refs_0_, bf16[16,6,16,128]{3,2,1,0:T(8,128)(2,1)S(1)} %all_to_all.43.refs_1_, bf16[64,64,128]{2,1,0:T(8,128)(2,1)S(1)} %bitcast.10), custom_call_target="tpu_custom_call" | custom-call | tf_op jit(solution)/shard_map/pallas_call | solution.py:252
  151.2 15.9 %all_to_all.44.in_ref = bf16[16,6,16,128]{3,2,1,0:T(8,128)(2,1)S(1)} all-to-all(bf16[16,6,16,128]{3,2,1,0:T(8,128)(2,1)S(1)} %shard_map.74), channel_id=1, replica_groups=mesh['row'=16,'col'=32] {'row'}, dimensions={0} | all-to-all | bytes 786432 | tf_op jit(solution)/shard_map/all_to_all | solution.py:238
  167.1 0.7 shard_map.75
  167.9 9.6 %all-to-all-start.7 = ((bf16[32,2,16,128]{3,2,1,0:T(8,128)(2,1)}), bf16[32,2,16,128]{3,2,1,0:T(8,128)(2,1)S(1)}, u32[]{:S(2)}, u32[]{:S(2)}) async-start(bf16[32,2,16,128]{3,2,1,0:T(8,128)(2,1)} %get-tuple-element.12), calls=%async_computation.7 | async-start | bytes 524288 | tf_op jit(solution)/shard_map/all_to_all | solution.py:238
  177.5 0.6 copy.8
  178.1 13.2 %all-to-all-done.7.in_ref = bf16[32,2,16,128]{3,2,1,0:T(8,128)(2,1)S(1)} async-done(((bf16[32,2,16,128]{3,2,1,0:T(8,128)(2,1)}), bf16[32,2,16,128]{3,2,1,0:T(8,128)(2,1)S(1)}, u32[]{:S(2)}, u32[]{:S(2)}) %all-to-all-start.7) | async-done | bytes 262176 | tf_op jit(solution)/shard_map/all_to_all | solution.py:238
  191.3 0.1 shard_map.76
  191.4 0.6 copy.9
  (5 shorter events, 0.1 us)
Async XLA Ops:
  2.1 51.0 %copy-start = (bf16[1,64,64,128]{3,2,1,0:T(8,128)(2,1)S(1)}, bf16[1,64,64,128]{3,2,1,0:T(8,128)(2,1)}, u32[]{:S(2)}) copy-start(bf16[1,64,64,128]{3,2,1,0:T(8,128)(2,1)} %param.6) | copy-start | bytes 3145732
  2.1 26.3 %all-to-all-start = ((bf16[32,2,16,128]{3,2,1,0:T(8,128)(2,1)}), bf16[32,2,16,128]{3,2,1,0:T(8,128)(2,1)S(1)}, u32[]{:S(2)}, u32[]{:S(2)}) async-start(bf16[32,2,16,128]{3,2,1,0:T(8,128)(2,1)} %shard_map.68), calls=%async_computation | async-start | bytes 524288 | tf_op jit(solution)/shard_map/all_to_all | solution.py:238
  29.2 23.9 %all-to-all-start.1 = ((bf16[16,6,16,128]{3,2,1,0:T(8,128)(2,1)}), bf16[16,6,16,128]{3,2,1,0:T(8,128)(2,1)S(1)}, u32[]{:S(2)}, u32[]{:S(2)}) async-start(bf16[16,6,16,128]{3,2,1,0:T(8,128)(2,1)} %shard_map.69), calls=%async_computation.1 | async-start | bytes 786432 | tf_op jit(solution)/shard_map/all_to_all | solution.py:238
  39.7 0.7 copy-start.2
  40.5 12.6 %copy-start.1 = (f32[2,128]{1,0:T(2,128)S(1)}, f32[2,128]{1,0:T(2,128)}, u32[]{:S(2)}) copy-start(f32[2,128]{1,0:T(2,128)} %e_ref.3) | copy-start | bytes 3076
  167.9 23.4 %all-to-all-start.7 = ((bf16[32,2,16,128]{3,2,1,0:T(8,128)(2,1)}), bf16[32,2,16,128]{3,2,1,0:T(8,128)(2,1)S(1)}, u32[]{:S(2)}, u32[]{:S(2)}) async-start(bf16[32,2,16,128]{3,2,1,0:T(8,128)(2,1)} %get-tuple-element.12), calls=%async_computation.7 | async-start | bytes 524288 | tf_op jit(solution)/shard_map/all_to_all | solution.py:238

commit v2 on v1

v2 whole, which is shorter than its diff:
```python
import functools

import jax
import jax.numpy as jnp
from jax import lax
from jax.experimental import pallas as pl
from jax.experimental.pallas import tpu as pltpu
from jax.sharding import PartitionSpec as P

F32 = jnp.float32
BF16 = jnp.bfloat16
VECS = 16
LANES = 128
HALF = 64
NR = 16
NC = 32
GROUP = 6
SLOTS = 128
UNROLL = 8
ROW_DEAD = NR * 8
COL_DEAD = NR * 4
VMEM = pl.BlockSpec(memory_space=pltpu.VMEM)
SMEM = pl.BlockSpec(memory_space=pltpu.SMEM)
NT_DIMS = (((1,), (1,)), ((), ()))


def shape(*dims, dtype=BF16):
    return jax.ShapeDtypeStruct(dims, dtype)


def call(kernel, outs, n_in, scratch=(), smem_first=False, limit=None):
    specs = [VMEM] * n_in
    if smem_first:
        specs[0] = SMEM
    return pl.pallas_call(
        kernel,
        out_shape=outs,
        in_specs=specs,
        out_specs=jax.tree.map(lambda _: VMEM, outs),
        scratch_shapes=list(scratch),
        compiler_params=pltpu.CompilerParams(vmem_limit_bytes=limit or 32 * 1024 * 1024),
    )


def lane_index():
    return lax.broadcasted_iota(jnp.int32, (VECS, LANES), 1)


def split3(value):
    high = value.astype(BF16)
    rest = value - high.astype(F32)
    middle = rest.astype(BF16)
    low = (rest - middle.astype(F32)).astype(BF16)
    return high, middle, low


def spread_kernel(x_ref, out_ref, own_ref):
    for j in range(2):
        value = x_ref[:, j, :]
        own_ref[j] = value
        for c in range(NC):
            out_ref[c, j * VECS : (j + 1) * VECS] = value


def regroup_kernel(own_ref, in_ref, out_ref):
    wide = 2 * VECS
    for r in range(NR):
        for s in range(2):
            out_ref[r, s * wide : (s + 1) * wide] = in_ref[2 * r + s, :wide]
        for j in range(2):
            out_ref[r, 2 * wide + j * VECS : 2 * wide + (j + 1) * VECS] = own_ref[j]


def tiles_kernel(with_gram, *refs):
    if with_gram:
        idx_ref, x_ref, w_ref, own_ref, e_ref, out_ref, *scratch = refs
    else:
        idx_ref, x_ref, w_ref, out_ref, *scratch = refs
    field_row, field_col, acc_row, acc_col = scratch[:4]
    low_half = lane_index() < HALF
    zero = jnp.zeros((VECS, LANES), F32)
    half_mask = [low_half, jnp.logical_not(low_half)]
    half_one = [jnp.where(m, 1.0, 0.0).astype(BF16) for m in half_mask]

    def part(g):
        return slice(g * VECS, (g + 1) * VECS)

    def place(r, g):
        if g < 4:
            return field_row, acc_row, r * 8 + g * 2
        return field_col, acc_col, r * 4 + (g - 4) * 2

    def duplicate(r, carry):
        for g in range(GROUP):
            value = x_ref[r, part(g)].astype(F32)
            turned = pltpu.roll(value, HALF, 1)
            field, acc, at = place(r, g)
            field[at] = jnp.where(low_half, value, turned).astype(BF16)
            field[at + 1] = jnp.where(low_half, turned, value).astype(BF16)
            acc[at] = zero
            acc[at + 1] = zero
        return carry

    lax.fori_loop(0, NR, duplicate, 0, unroll=4)
    for field, acc, dead in ((field_row, acc_row, ROW_DEAD), (field_col, acc_col, COL_DEAD)):
        field[dead] = zero.astype(BF16)
        acc[dead] = zero

    def block(b, carry):
        work = []
        for u in range(UNROLL):
            q = b * UNROLL + u
            rows = [idx_ref[0, q * 4 + k] for k in range(4)]
            cols = [idx_ref[1, q * 4 + k] for k in range(4)]
            w = w_ref[pl.ds(2 * q, 2)].reshape(2 * HALF, LANES)
            left_f = jnp.concatenate([field_col[cols[k]] * half_one[k % 2] for k in range(4)], axis=0)
            left_b = jnp.concatenate([field_row[rows[k]] * half_one[k // 2] for k in range(4)], axis=0)
            forward = lax.dot_general(left_f, w, NT_DIMS, preferred_element_type=F32)
            backward = jnp.dot(left_b, w, preferred_element_type=F32)
            work.append((rows, cols, forward, backward))
        for rows, cols, forward, backward in work:
            for k in range(4):
                acc_row[rows[k]] += jnp.where(half_mask[k // 2], forward[part(k)], 0.0)
                acc_col[cols[k]] += jnp.where(half_mask[k % 2], backward[part(k)], 0.0)
        return carry

    lax.fori_loop(0, SLOTS // 4 // UNROLL, block, 0)

    def pack(r, carry):
        for g in range(GROUP):
            _, acc, at = place(r, g)
            first, second = acc[at], acc[at + 1]
            total = jnp.where(low_half, first, second) + pltpu.roll(
                jnp.where(low_half, second, first), HALF, 1
            )
            out_ref[r, part(g)] = total.astype(BF16)
            if with_gram and g >= 4:
                for n, term in enumerate(split3(total)):
                    scratch[4][n, r * 2 + g - 4] = term
        return carry

    lax.fori_loop(0, NR, pack, 0, unroll=4)
    if not with_gram:
        return
    terms = scratch[4]
    left = jnp.concatenate(
        [jnp.concatenate([terms[n, p] for p in range(2 * NR)], axis=1) for n in range(3)], axis=0
    )
    right = jnp.concatenate([x_ref[r, part(g)] for r in range(NR) for g in (4, 5)], axis=1)
    crosses = lax.dot_general(left, right, NT_DIMS, preferred_element_type=F32)
    cross = crosses[:VECS] + crosses[VECS : 2 * VECS] + crosses[2 * VECS :]
    gram = jnp.zeros((VECS, VECS), F32)
    for j in range(2):
        own = own_ref[j]
        gram = gram + lax.dot_general(own, own, NT_DIMS, preferred_element_type=F32)
        weighted = own.astype(F32) * (0.5 * e_ref[j : j + 1, :])
        for term in split3(weighted):
            cross = cross + lax.dot_general(term, own, NT_DIMS, preferred_element_type=F32)
    message = message_of(widen(gram), widen(cross))
    for r in range(NR):
        out_ref[r, part(GROUP)] = message


def widen(value):
    return jnp.concatenate([value, jnp.zeros((VECS, LANES - VECS), F32)], axis=1)


def message_of(gram, cross):
    total = jnp.zeros((VECS, LANES), F32)
    for base, value in ((0, gram), (HALF, cross)):
        for n, part in enumerate(split3(value)):
            part = part.astype(F32)
            total = total + (pltpu.roll(part, base + n * VECS, 1) if base + n else part)
    return total.astype(BF16)


def read_message(total):
    keep = lane_index() < VECS
    found = []
    for base in (0, HALF):
        value = jnp.zeros((VECS, LANES), F32)
        for n in (2, 1, 0):
            shift = base + n * VECS
            value = value + (pltpu.roll(total, LANES - shift, 1) if shift else total)
        found.append(jnp.where(keep, value, 0.0))
    return found


def collect_kernel(with_gram, in_ref, out_ref, back_ref):
    wide = 2 * VECS
    for r in range(NR):
        for s in range(2):
            out_ref[2 * r + s, :wide] = in_ref[r, s * wide : (s + 1) * wide]

    def total_of(g):
        part = slice(g * VECS, (g + 1) * VECS)
        total = in_ref[0, part].astype(F32)
        for r in range(1, NR):
            total = total + in_ref[r, part].astype(F32)
        return total

    for j in range(2):
        back_ref[j] = total_of(4 + j)
    if with_gram:
        message = message_of(*read_message(total_of(GROUP)))
        for c in range(NC):
            out_ref[c, wide:] = message


def sum_over(in_ref, g):
    part = slice(g * VECS, (g + 1) * VECS)
    total = in_ref[0, part].astype(F32)
    for c in range(1, NC):
        total = total + in_ref[c, part].astype(F32)
    return total


def solve_kernel(in_ref, back_ref, own_ref, e_ref, out_ref, residual_ref, result_ref):
    gram, cross = read_message(sum_over(in_ref, 2))
    wide = jnp.concatenate([cross, jnp.zeros((LANES - VECS, LANES), F32)], axis=0)
    cross = cross + jnp.transpose(wide)[:VECS]
    state = jnp.concatenate([gram, cross], axis=0)
    lane = lax.broadcasted_iota(jnp.int32, (2 * VECS, LANES), 1)
    for p in range(VECS):
        column = state[:, p : p + 1]
        pivot = state[p : p + 1, :]
        scaled = pivot / state[p : p + 1, p : p + 1]
        scaled = jnp.where(lane[:1] == p, 0.0, scaled)
        own_column = column / state[p : p + 1, p : p + 1]
        state = jnp.where(lane == p, own_column, state - column * scaled)
    mix = state[VECS:]
    for j in range(2):
        v = own_ref[j].astype(F32)
        product = sum_over(in_ref, j) + back_ref[j] + e_ref[j : j + 1, :] * v
        shifted = jnp.zeros((VECS, LANES), F32)
        for k in range(VECS):
            shifted = shifted + mix[:, k : k + 1] * v[k : k + 1, :]
        value = (product - shifted).astype(BF16)
        residual_ref[j] = value
        result_ref[:, j, :] = value
        for c in range(NC):
            out_ref[c, j * VECS : (j + 1) * VECS] = value


def finish_kernel(in_ref, back_ref, own_ref, e_ref, out_ref):
    for j in range(2):
        total = sum_over(in_ref, j) + back_ref[j]
        out_ref[:, j, :] = total + e_ref[j : j + 1, :] * own_ref[j].astype(F32)


def exchange(value, axis):
    return lax.all_to_all(value, axis, split_axis=0, concat_axis=0, tiled=True)


def apply_tiles(own, spread, index, tiles, energies, with_gram):
    by_block = exchange(spread, "col")
    grouped = call(regroup_kernel, shape(NR, GROUP * VECS, LANES), 2)(own, by_block)
    fields = exchange(grouped, "row")
    scratch = [
        pltpu.VMEM((ROW_DEAD + 1, VECS, LANES), BF16),
        pltpu.VMEM((COL_DEAD + 1, VECS, LANES), BF16),
        pltpu.VMEM((ROW_DEAD + 1, VECS, LANES), F32),
        pltpu.VMEM((COL_DEAD + 1, VECS, LANES), F32),
    ]
    extra = 0
    args = (index, fields, tiles)
    if with_gram:
        extra = 1
        args = args + (own, energies)
        scratch.append(pltpu.VMEM((3, 2 * NR, VECS, LANES), BF16))
    partial = call(
        functools.partial(tiles_kernel, with_gram),
        shape(NR, (GROUP + extra) * VECS, LANES),
        len(args),
        scratch,
        smem_first=True,
    )(*args)
    moved = exchange(partial, "row")
    by_block, back = call(
        functools.partial(collect_kernel, with_gram),
        (shape(NC, (2 + extra) * VECS, LANES), shape(2, VECS, LANES, dtype=F32)),
        1,
    )(moved)
    return exchange(by_block, "col"), back


def shards(vectors, tile_values, tile_coords, tile_counts, energies):
    tiles = tile_values[0]
    coords = tile_coords[:, 0]
    pair = coords // 2
    major = pair // NC
    rows = (major[0] // 2 * 4 + pair[0] % 2 * 2 + major[0] % 2) * 2 + coords[0] % 2
    cols = major[1] * 2 + coords[1] % 2
    live = jnp.arange(SLOTS, dtype=jnp.int32) < tile_counts[0, 0]
    index = jnp.stack([jnp.where(live, rows, ROW_DEAD), jnp.where(live, cols, COL_DEAD)])
    vectors, index = lax.optimization_barrier((vectors, index))

    spread, own = call(
        spread_kernel, (shape(NC, 2 * VECS, LANES), shape(2, VECS, LANES)), 1
    )(vectors)
    forward, back = apply_tiles(own, spread, index, tiles, energies, True)
    spread, residual, result = call(
        solve_kernel,
        (shape(NC, 2 * VECS, LANES), shape(2, VECS, LANES), shape(VECS, 2, LANES)),
        4,
    )(forward, back, own, energies)
    forward, back = apply_tiles(residual, spread, index, tiles, energies, False)
    image = call(finish_kernel, shape(VECS, 2, LANES, dtype=F32), 4)(
        forward, back, residual, energies
    )
    return result, image


def solution(mesh):
    in_specs = (
        P(None, "row", "col"),
        P("row", "col", None, None),
        P(None, "row", "col"),
        P("row", "col"),
        P("row", "col"),
    )
    out_specs = (P(None, "row", "col"), P(None, "row", "col"))
    return jax.shard_map(shards, mesh=mesh, in_specs=in_specs, out_specs=out_specs, check_vma=False)
```

time: 193 us -> 180 us (0.933)
  blocking collectives: 93.2 us -> 166 us
  waiting for transfers between devices: 38.4 us -> 0 us
  starting transfers between devices: 33.2 us -> 0 us
  Pallas kernels: 23.1 us -> 9.56 us
    all_to_all x5 -> x8, blocking collectives: 93.2 us -> 166 us  [exchange(): return lax.all_to_all(value, axis, split_axis=0, concat_axis=0, tiled=True)]
    all_to_all x3 -> x0, waiting for transfers between devices: 38.4 us -> none  [exchange(): return lax.all_to_all(value, axis, split_axis=0, concat_axis=0, tiled=True)]
    all_to_all x3 -> x0, starting transfers between devices: 33.2 us -> none  [exchange(): return lax.all_to_all(value, axis, split_axis=0, concat_axis=0, tiled=True)]
    pallas_call x9, Pallas kernels: 23.1 us -> 9.56 us  [the longest x2 6.25 us: apply_tiles(): call(functools.partial(tiles_kernel, with_gram), shape(NR, (GROUP + extra...]
  transfers between devices with their start and end apart: 3 -> 0, of which waited for: 3 -> 0; matrix products, arithmetic and copies ran while one was open for 0% -> 0% of each run, Pallas kernels for 0% -> 0%
where the time goes in v2:
time: 180 us; the launch traced here: 179 us
  blocking collectives  166 us (92%)
  Pallas kernels  9.56 us (5%)
    all_to_all x8, blocking collectives, exchange(): return lax.all_to_all(value, axis, split_axis=0, concat_axis=0, tiled=True)  166 us
    pallas_call x2, Pallas kernels, apply_tiles(): call(functools.partial(tiles_kernel, with_gram), shape(NR, (GROUP + extra...  6.25 us

profile of v2, /device:TPU:6, one launch (start us, length us, event | category | flops | bytes accessed | tf_op | source)
XLA Modules:
  0.0 178.8 jit_solution(786239454489346433)
XLA Ops:
  0.6 0.0 copy-start.2
  0.6 0.0 copy-start
  1.4 0.7 and_select_fusion.5
  2.1 0.7 compare_select_fusion.10
  2.8 0.0 copy-done.2
  2.8 0.1 shard_map.68
  2.9 26.0 %all_to_all.40.in_ref = bf16[32,32,128]{2,1,0:T(8,128)(2,1)S(1)} all-to-all(bf16[32,32,128]{2,1,0:T(8,128)(2,1)S(1)} %get-tuple-element.16), channel_id=1, replica_groups=mesh['row'=16,'col'=32] {'col'}, dimensions={0} | all-to-all | bytes 524288 | tf_op jit(solution)/shard_map/all_to_all | solution.py:252
  28.9 23.7 %all_to_all.41.refs_1_ = bf16[16,96,128]{2,1,0:T(8,128)(2,1)S(1)} all-to-all(bf16[16,96,128]{2,1,0:T(8,128)(2,1)S(1)} %shard_map.69), channel_id=1, replica_groups=mesh['row'=16,'col'=32] {'row'}, dimensions={0} | all-to-all | bytes 786432 | tf_op jit(solution)/shard_map/all_to_all | solution.py:252
  52.6 0.0 copy-start.1
  52.6 0.0 copy-done
  52.6 0.7 copy-done.1
  53.3 3.3 %shard_map.70 = bf16[16,112,128]{2,1,0:T(8,128)(2,1)S(1)} custom-call(s32[2,128]{1,0:T(2,128)S(1)} %pad_add_fusion.refs_0_, bf16[16,96,128]{2,1,0:T(8,128)(2,1)S(1)} %all_to_all.41.refs_1_, bf16[64,64,128]{2,1,0:T(8,128)(2,1)S(1)} %bitcast.12, bf16[2,16,128]{2,1,0:T(8,128)(2,1)S(1)} %get-tuple-element.15.own_ref.refs_3_, f32[2,128]{1,0:T(2,128)S(1)} %copy-done.1), custom_call_target="tpu_custom_call" | custom-call | tf_op jit(solution)/shard_map/pallas_call | solution.py:271
  56.6 16.6 %all_to_all.42.in_ref = bf16[16,112,128]{2,1,0:T(8,128)(2,1)S(1)} all-to-all(bf16[16,112,128]{2,1,0:T(8,128)(2,1)S(1)} %shard_map.70), channel_id=1, replica_groups=mesh['row'=16,'col'=32] {'row'}, dimensions={0} | all-to-all | bytes 917504 | tf_op jit(solution)/shard_map/all_to_all | solution.py:252
  73.2 0.2 shard_map.71
  73.4 26.1 %all_to_all.43.in_ref = bf16[32,48,128]{2,1,0:T(8,128)(2,1)S(1)} all-to-all(bf16[32,48,128]{2,1,0:T(8,128)(2,1)S(1)} %get-tuple-element.17), channel_id=1, replica_groups=mesh['row'=16,'col'=32] {'col'}, dimensions={0} | all-to-all | bytes 786432 | tf_op jit(solution)/shard_map/all_to_all | solution.py:252
  99.5 2.3 %shard_map.72 = (bf16[32,32,128]{2,1,0:T(8,128)(2,1)S(1)}, bf16[2,16,128]{2,1,0:T(8,128)(2,1)S(1)}, bf16[16,2,128]{2,1,0:T(2,128)(2,1)}) custom-call(bf16[32,48,128]{2,1,0:T(8,128)(2,1)S(1)} %all_to_all.43.in_ref, f32[2,16,128]{2,1,0:T(8,128)S(1)} %get-tuple-element.18.back_ref, bf16[2,16,128]{2,1,0:T(8,128)(2,1)S(1)} %get-tuple-element.15.own_ref.refs_3_, ...), custom_call_target="tpu_custom_call" | custom-call | tf_op jit(solution)/shard_map/pallas_call | solution.py:302
  101.8 16.6 %all_to_all.44.in_ref = bf16[32,32,128]{2,1,0:T(8,128)(2,1)S(1)} all-to-all(bf16[32,32,128]{2,1,0:T(8,128)(2,1)S(1)} %get-tuple-element.21), channel_id=1, replica_groups=mesh['row'=16,'col'=32] {'col'}, dimensions={0} | all-to-all | bytes 524288 | tf_op jit(solution)/shard_map/all_to_all | solution.py:252
  118.5 17.7 %all_to_all.45.refs_1_ = bf16[16,96,128]{2,1,0:T(8,128)(2,1)S(1)} all-to-all(bf16[16,96,128]{2,1,0:T(8,128)(2,1)S(1)} %shard_map.73), channel_id=1, replica_groups=mesh['row'=16,'col'=32] {'row'}, dimensions={0} | all-to-all | bytes 786432 | tf_op jit(solution)/shard_map/all_to_all | solution.py:252
  136.2 2.9 %shard_map.74 = bf16[16,96,128]{2,1,0:T(8,128)(2,1)S(1)} custom-call(s32[2,128]{1,0:T(2,128)S(1)} %pad_add_fusion.refs_0_, bf16[16,96,128]{2,1,0:T(8,128)(2,1)S(1)} %all_to_all.45.refs_1_, bf16[64,64,128]{2,1,0:T(8,128)(2,1)S(1)} %bitcast.13), custom_call_target="tpu_custom_call" | custom-call | tf_op jit(solution)/shard_map/pallas_call | solution.py:271
  139.1 15.9 %all_to_all.46.in_ref = bf16[16,96,128]{2,1,0:T(8,128)(2,1)S(1)} all-to-all(bf16[16,96,128]{2,1,0:T(8,128)(2,1)S(1)} %shard_map.74), channel_id=1, replica_groups=mesh['row'=16,'col'=32] {'row'}, dimensions={0} | all-to-all | bytes 786432 | tf_op jit(solution)/shard_map/all_to_all | solution.py:252
  155.0 23.1 %all_to_all.47.in_ref = bf16[32,32,128]{2,1,0:T(8,128)(2,1)S(1)} all-to-all(bf16[32,32,128]{2,1,0:T(8,128)(2,1)S(1)} %get-tuple-element.22), channel_id=1, replica_groups=mesh['row'=16,'col'=32] {'col'}, dimensions={0} | all-to-all | bytes 524288 | tf_op jit(solution)/shard_map/all_to_all | solution.py:252
  178.1 0.7 shard_map.76
  (4 shorter events, 0.1 us)
Async XLA Ops:
  0.6 2.2 %copy-start.2 = (bf16[16,2,128]{2,1,0:T(2,128)(2,1)S(1)}, bf16[16,2,128]{2,1,0:T(2,128)(2,1)}, u32[]{:S(2)}) copy-start(bf16[16,2,128]{2,1,0:T(2,128)(2,1)} %x_ref) | copy-start | bytes 24580
  0.6 52.0 %copy-start = (bf16[1,64,64,128]{3,2,1,0:T(8,128)(2,1)S(1)}, bf16[1,64,64,128]{3,2,1,0:T(8,128)(2,1)}, u32[]{:S(2)}) copy-start(bf16[1,64,64,128]{3,2,1,0:T(8,128)(2,1)} %param.6) | copy-start | bytes 3145732
  52.6 0.7 copy-start.1

commit v3 on v2

--- a/solution.py
+++ b/solution.py
@@ -2,6 +2,7 @@
 
 import jax
 import jax.numpy as jnp
+import numpy as np
 from jax import lax
 from jax.experimental import pallas as pl
 from jax.experimental.pallas import tpu as pltpu
@@ -16,29 +17,37 @@
 NC = 32
 GROUP = 6
 SLOTS = 128
-UNROLL = 8
+UNROLL = 16
 ROW_DEAD = NR * 8
 COL_DEAD = NR * 4
+ROW = ("x", "core", "zh")
+COL = ("zl", "y")
 VMEM = pl.BlockSpec(memory_space=pltpu.VMEM)
 SMEM = pl.BlockSpec(memory_space=pltpu.SMEM)
 NT_DIMS = (((1,), (1,)), ((), ()))
 
 
+def row_at(r):
+    return (r % 8) * 2 + r // 8
+
+
+def col_at(c):
+    return (c % 4) * 8 + c // 4
+
+
 def shape(*dims, dtype=BF16):
     return jax.ShapeDtypeStruct(dims, dtype)
 
 
-def call(kernel, outs, n_in, scratch=(), smem_first=False, limit=None):
-    specs = [VMEM] * n_in
-    if smem_first:
-        specs[0] = SMEM
+def call(kernel, outs, n_in, scratch=(), scalars=(), first=VMEM, limit=32):
+    specs = [SMEM if n in scalars else first for n in range(n_in)]
     return pl.pallas_call(
         kernel,
         out_shape=outs,
         in_specs=specs,
         out_specs=jax.tree.map(lambda _: VMEM, outs),
         scratch_shapes=list(scratch),
-        compiler_params=pltpu.CompilerParams(vmem_limit_bytes=limit or 32 * 1024 * 1024),
+        compiler_params=pltpu.CompilerParams(vmem_limit_bytes=limit * 1024 * 1024),
     )
 
 
@@ -54,21 +63,40 @@
     return high, middle, low
 
 
-def spread_kernel(x_ref, out_ref, own_ref):
+def spread_kernel(
+    x_hbm, coords_hbm, counts_hbm, e_hbm, out_ref, own_ref, index_ref, energy_ref, x_ref, coords_ref, counts_ref, sems
+):
+    pairs = ((x_hbm, x_ref), (coords_hbm, coords_ref), (counts_hbm, counts_ref), (e_hbm, energy_ref))
+    copies = [pltpu.make_async_copy(a, b, sems.at[n]) for n, (a, b) in enumerate(pairs)]
+    for copy in copies:
+        copy.start()
+    for copy in copies:
+        copy.wait()
     for j in range(2):
         value = x_ref[:, j, :]
         own_ref[j] = value
         for c in range(NC):
             out_ref[c, j * VECS : (j + 1) * VECS] = value
+    live = lax.broadcasted_iota(jnp.int32, (1, SLOTS), 1) < counts_ref[0, 0]
+    for n, dead in ((0, ROW_DEAD), (1, COL_DEAD)):
+        coords = coords_ref[n]
+        major = coords >> 6
+        source = major >> 1
+        group = ((source & 7) << 1) + (source >> 3)
+        if n == 0:
+            group = group * 2 + ((coords >> 1) & 1)
+        tile = (group * 2 + (major & 1)) * 2 + (coords & 1)
+        index_ref[n : n + 1] = jnp.where(live, tile, dead)
 
 
 def regroup_kernel(own_ref, in_ref, out_ref):
     wide = 2 * VECS
     for r in range(NR):
+        at = row_at(r)
         for s in range(2):
-            out_ref[r, s * wide : (s + 1) * wide] = in_ref[2 * r + s, :wide]
+            out_ref[at, s * wide : (s + 1) * wide] = in_ref[col_at(2 * r + s), :wide]
         for j in range(2):
-            out_ref[r, 2 * wide + j * VECS : 2 * wide + (j + 1) * VECS] = own_ref[j]
+            out_ref[at, 2 * wide + j * VECS : 2 * wide + (j + 1) * VECS] = own_ref[j]
 
 
 def tiles_kernel(with_gram, *refs):
@@ -190,7 +218,7 @@
     wide = 2 * VECS
     for r in range(NR):
         for s in range(2):
-            out_ref[2 * r + s, :wide] = in_ref[r, s * wide : (s + 1) * wide]
+            out_ref[col_at(2 * r + s), :wide] = in_ref[row_at(r), s * wide : (s + 1) * wide]
 
     def total_of(g):
         part = slice(g * VECS, (g + 1) * VECS)
@@ -221,13 +249,15 @@
     cross = cross + jnp.transpose(wide)[:VECS]
     state = jnp.concatenate([gram, cross], axis=0)
     lane = lax.broadcasted_iota(jnp.int32, (2 * VECS, LANES), 1)
-    for p in range(VECS):
-        column = state[:, p : p + 1]
-        pivot = state[p : p + 1, :]
-        scaled = pivot / state[p : p + 1, p : p + 1]
-        scaled = jnp.where(lane[:1] == p, 0.0, scaled)
-        own_column = column / state[p : p + 1, p : p + 1]
-        state = jnp.where(lane == p, own_column, state - column * scaled)
+    for p in range(0, VECS, 2):
+        first, second = state[:, p : p + 1], state[:, p + 1 : p + 2]
+        a, b = first[p : p + 1], second[p : p + 1]
+        c, d = first[p + 1 : p + 2], second[p + 1 : p + 2]
+        scale = 1.0 / (a * d - b * c)
+        new_first = (first * d - second * c) * scale
+        new_second = (second * a - first * b) * scale
+        rest = state - new_first * state[p : p + 1] - new_second * state[p + 1 : p + 2]
+        state = jnp.where(lane == p, new_first, jnp.where(lane == p + 1, new_second, rest))
     mix = state[VECS:]
     for j in range(2):
         v = own_ref[j].astype(F32)
@@ -253,9 +283,9 @@
 
 
 def apply_tiles(own, spread, index, tiles, energies, with_gram):
-    by_block = exchange(spread, "col")
+    by_block = exchange(spread, COL)
     grouped = call(regroup_kernel, shape(NR, GROUP * VECS, LANES), 2)(own, by_block)
-    fields = exchange(grouped, "row")
+    fields = exchange(grouped, ROW)
     scratch = [
         pltpu.VMEM((ROW_DEAD + 1, VECS, LANES), BF16),
         pltpu.VMEM((COL_DEAD + 1, VECS, LANES), BF16),
@@ -273,31 +303,37 @@
         shape(NR, (GROUP + extra) * VECS, LANES),
         len(args),
         scratch,
-        smem_first=True,
+        scalars=(0,),
     )(*args)
-    moved = exchange(partial, "row")
+    moved = exchange(partial, ROW)
     by_block, back = call(
         functools.partial(collect_kernel, with_gram),
         (shape(NC, (2 + extra) * VECS, LANES), shape(2, VECS, LANES, dtype=F32)),
         1,
     )(moved)
-    return exchange(by_block, "col"), back
+    return exchange(by_block, COL), back
 
 
 def shards(vectors, tile_values, tile_coords, tile_counts, energies):
     tiles = tile_values[0]
-    coords = tile_coords[:, 0]
-    pair = coords // 2
-    major = pair // NC
-    rows = (major[0] // 2 * 4 + pair[0] % 2 * 2 + major[0] % 2) * 2 + coords[0] % 2
-    cols = major[1] * 2 + coords[1] % 2
-    live = jnp.arange(SLOTS, dtype=jnp.int32) < tile_counts[0, 0]
-    index = jnp.stack([jnp.where(live, rows, ROW_DEAD), jnp.where(live, cols, COL_DEAD)])
-    vectors, index = lax.optimization_barrier((vectors, index))
-
-    spread, own = call(
-        spread_kernel, (shape(NC, 2 * VECS, LANES), shape(2, VECS, LANES)), 1
-    )(vectors)
+    spread, own, index, energies = call(
+        spread_kernel,
+        (
+            shape(NC, 2 * VECS, LANES),
+            shape(2, VECS, LANES),
+            shape(2, SLOTS, dtype=jnp.int32),
+            shape(2, LANES, dtype=F32),
+        ),
+        4,
+        [
+            pltpu.VMEM((VECS, 2, LANES), BF16),
+            pltpu.VMEM((2, 1, SLOTS), jnp.int32),
+            pltpu.SMEM((1, 1), jnp.int32),
+            pltpu.SemaphoreType.DMA((4,)),
+        ],
+        first=pl.BlockSpec(memory_space=pl.ANY),
+        limit=60,
+    )(vectors, tile_coords, tile_counts, energies)
     forward, back = apply_tiles(own, spread, index, tiles, energies, True)
     spread, residual, result = call(
         solve_kernel,
@@ -312,12 +348,15 @@
 
 
 def solution(mesh):
+    devices = np.asarray(mesh.devices).reshape(2, 4, 2, 8, 4)
+    fine = jax.sharding.Mesh(devices, ("zh", "x", "core", "y", "zl"))
+    row, col = ("zh", "x", "core"), ("y", "zl")
     in_specs = (
-        P(None, "row", "col"),
-        P("row", "col", None, None),
-        P(None, "row", "col"),
-        P("row", "col"),
-        P("row", "col"),
+        P(None, row, col),
+        P(row, col, None, None),
+        P(None, row, col),
+        P(row, col),
+        P(row, col),
     )
-    out_specs = (P(None, "row", "col"), P(None, "row", "col"))
-    return jax.shard_map(shards, mesh=mesh, in_specs=in_specs, out_specs=out_specs, check_vma=False)
+    out_specs = (P(None, row, col), P(None, row, col))
+    return jax.shard_map(shards, mesh=fine, in_specs=in_specs, out_specs=out_specs, check_vma=False)

time: 180 us -> 178 us (0.989)
  blocking collectives: 166 us -> 162 us
    all_to_all x8, blocking collectives: 166 us -> 162 us  [exchange(): return lax.all_to_all(value, axis, split_axis=0, concat_axis=0, tiled=True)]
where the time goes in v3:
time: 178 us; the launch traced here: 176 us
  blocking collectives  162 us (91%)
  Pallas kernels  11.3 us (6%)
    all_to_all x8, blocking collectives, exchange(): return lax.all_to_all(value, axis, split_axis=0, concat_axis=0, tiled=True)  162 us
    pallas_call x2, Pallas kernels, apply_tiles(): call(functools.partial(tiles_kernel, with_gram), shape(NR, (GROUP + extra...  5.62 us

profile of v3, /device:TPU:6, one launch (start us, length us, event | category | flops | bytes accessed | tf_op | source)
XLA Modules:
  0.0 176.3 jit_solution(3466198023861039176)
XLA Ops:
  0.6 0.0 copy-start
  1.4 1.5 shard_map.68
  2.9 25.5 %all_to_all.40.in_ref = bf16[32,32,128]{2,1,0:T(8,128)(2,1)S(1)} all-to-all(bf16[32,32,128]{2,1,0:T(8,128)(2,1)} %get-tuple-element.15), channel_id=1, replica_groups=mesh['zh'=2,'x'=4,'core'=2,'y'=8,'zl'=4] {'zl','y'}, dimensions={0} | all-to-all | bytes 524288 | tf_op jit(solution)/shard_map/all_to_all | solution.py:282
  28.4 0.0 copy-start.1
  28.4 0.7 copy-done.1
  29.1 0.0 copy-start.4
  29.1 22.8 %all_to_all.41.refs_1_ = bf16[16,96,128]{2,1,0:T(8,128)(2,1)S(1)} all-to-all(bf16[16,96,128]{2,1,0:T(8,128)(2,1)S(1)} %shard_map.69), channel_id=1, replica_groups=mesh['zh'=2,'x'=4,'core'=2,'y'=8,'zl'=4] {'x','core','zh'}, dimensions={0} | all-to-all | bytes 786432 | tf_op jit(solution)/shard_map/all_to_all | solution.py:282
  51.9 0.0 copy-start.3
  51.9 0.0 copy-done
  51.9 0.0 copy-done.4
  51.9 0.6 copy-done.3
  52.5 3.0 %shard_map.70 = bf16[16,112,128]{2,1,0:T(8,128)(2,1)S(1)} custom-call(s32[2,128]{1,0:T(2,128)S(1)} %copy-done.4, bf16[16,96,128]{2,1,0:T(8,128)(2,1)S(1)} %all_to_all.41.refs_1_, bf16[64,64,128]{2,1,0:T(8,128)(2,1)S(1)} %bitcast.1, bf16[2,16,128]{2,1,0:T(8,128)(2,1)S(1)} %copy-done.1, f32[2,128]{1,0:T(2,128)S(1)} %copy-done.3), custom_call_target="tpu_custom_call" | custom-call | tf_op jit(solution)/shard_map/pallas_call | solution.py:301
  55.5 16.5 %all_to_all.42.in_ref = bf16[16,112,128]{2,1,0:T(8,128)(2,1)S(1)} all-to-all(bf16[16,112,128]{2,1,0:T(8,128)(2,1)S(1)} %shard_map.70), channel_id=1, replica_groups=mesh['zh'=2,'x'=4,'core'=2,'y'=8,'zl'=4] {'x','core','zh'}, dimensions={0} | all-to-all | bytes 917504 | tf_op jit(solution)/shard_map/all_to_all | solution.py:282
  72.0 0.2 shard_map.71
  72.2 0.0 copy-start.2
  72.2 24.9 %all_to_all.43.in_ref = bf16[32,48,128]{2,1,0:T(8,128)(2,1)S(1)} all-to-all(bf16[32,48,128]{2,1,0:T(8,128)(2,1)S(1)} %get-tuple-element.17), channel_id=1, replica_groups=mesh['zh'=2,'x'=4,'core'=2,'y'=8,'zl'=4] {'zl','y'}, dimensions={0} | all-to-all | bytes 786432 | tf_op jit(solution)/shard_map/all_to_all | solution.py:282
  97.1 0.0 copy-done.2
  97.1 3.2 %shard_map.72 = (bf16[32,32,128]{2,1,0:T(8,128)(2,1)S(1)}, bf16[2,16,128]{2,1,0:T(8,128)(2,1)S(1)}, bf16[16,2,128]{2,1,0:T(2,128)(2,1)}) custom-call(bf16[32,48,128]{2,1,0:T(8,128)(2,1)S(1)} %all_to_all.43.in_ref, f32[2,16,128]{2,1,0:T(8,128)S(1)} %get-tuple-element.18.back_ref, bf16[2,16,128]{2,1,0:T(8,128)(2,1)S(1)} %copy-done.2, f32[2,128]{1,0:T(2,128)S(1)} %copy-done.3), custom_call_target="tpu_custom_call" | custom-call | tf_op jit(solution)/shard_map/pallas_call | solution.py:338
  100.3 17.5 %all_to_all.44.in_ref = bf16[32,32,128]{2,1,0:T(8,128)(2,1)S(1)} all-to-all(bf16[32,32,128]{2,1,0:T(8,128)(2,1)S(1)} %get-tuple-element.21), channel_id=1, replica_groups=mesh['zh'=2,'x'=4,'core'=2,'y'=8,'zl'=4] {'zl','y'}, dimensions={0} | all-to-all | bytes 524288 | tf_op jit(solution)/shard_map/all_to_all | solution.py:282
  117.8 16.8 %all_to_all.45.refs_1_ = bf16[16,96,128]{2,1,0:T(8,128)(2,1)S(1)} all-to-all(bf16[16,96,128]{2,1,0:T(8,128)(2,1)S(1)} %shard_map.73), channel_id=1, replica_groups=mesh['zh'=2,'x'=4,'core'=2,'y'=8,'zl'=4] {'x','core','zh'}, dimensions={0} | all-to-all | bytes 786432 | tf_op jit(solution)/shard_map/all_to_all | solution.py:282
  134.6 2.6 %shard_map.74 = bf16[16,96,128]{2,1,0:T(8,128)(2,1)S(1)} custom-call(s32[2,128]{1,0:T(2,128)S(1)} %copy-done.4, bf16[16,96,128]{2,1,0:T(8,128)(2,1)S(1)} %all_to_all.45.refs_1_, bf16[64,64,128]{2,1,0:T(8,128)(2,1)S(1)} %bitcast.2), custom_call_target="tpu_custom_call" | custom-call | tf_op jit(solution)/shard_map/pallas_call | solution.py:301
  137.2 15.6 %all_to_all.46.in_ref = bf16[16,96,128]{2,1,0:T(8,128)(2,1)S(1)} all-to-all(bf16[16,96,128]{2,1,0:T(8,128)(2,1)S(1)} %shard_map.74), channel_id=1, replica_groups=mesh['zh'=2,'x'=4,'core'=2,'y'=8,'zl'=4] {'x','core','zh'}, dimensions={0} | all-to-all | bytes 786432 | tf_op jit(solution)/shard_map/all_to_all | solution.py:282
  152.8 22.9 %all_to_all.47.in_ref = bf16[32,32,128]{2,1,0:T(8,128)(2,1)S(1)} all-to-all(bf16[32,32,128]{2,1,0:T(8,128)(2,1)S(1)} %get-tuple-element.22), channel_id=1, replica_groups=mesh['zh'=2,'x'=4,'core'=2,'y'=8,'zl'=4] {'zl','y'}, dimensions={0} | all-to-all | bytes 524288 | tf_op jit(solution)/shard_map/all_to_all | solution.py:282
  175.7 0.7 shard_map.76
  (3 shorter events, 0.1 us)
Async XLA Ops:
  0.6 51.3 %copy-start = (bf16[1,64,64,128]{3,2,1,0:T(8,128)(2,1)S(1)}, bf16[1,64,64,128]{3,2,1,0:T(8,128)(2,1)}, u32[]{:S(2)}) copy-start(bf16[1,64,64,128]{3,2,1,0:T(8,128)(2,1)} %param.6) | copy-start | bytes 3145732
  28.4 0.7 copy-start.1
  29.1 22.8 %copy-start.4 = (s32[2,128]{1,0:T(2,128)S(1)}, s32[2,128]{1,0:T(2,128)}, u32[]{:S(2)}) copy-start(s32[2,128]{1,0:T(2,128)} %get-tuple-element.13.refs_0_) | copy-start | bytes 3076
  51.9 0.6 copy-start.3
  72.2 24.9 %copy-start.2 = (bf16[2,16,128]{2,1,0:T(8,128)(2,1)S(1)}, bf16[2,16,128]{2,1,0:T(8,128)(2,1)}, u32[]{:S(2)}) copy-start(bf16[2,16,128]{2,1,0:T(8,128)(2,1)} %get-tuple-element.14.own_ref.refs_3_) | copy-start | bytes 24580

commit v4 on v3

--- a/solution.py
+++ b/solution.py
@@ -13,6 +13,7 @@
 VECS = 16
 LANES = 128
 HALF = 64
+MESSAGE = 8
 NR = 16
 NC = 32
 GROUP = 6
@@ -55,6 +56,11 @@
     return lax.broadcasted_iota(jnp.int32, (VECS, LANES), 1)
 
 
+def split2(value):
+    high = value.astype(BF16)
+    return high, (value - high.astype(F32)).astype(BF16)
+
+
 def split3(value):
     high = value.astype(BF16)
     rest = value - high.astype(F32)
@@ -64,7 +70,7 @@
 
 
 def spread_kernel(
-    x_hbm, coords_hbm, counts_hbm, e_hbm, out_ref, own_ref, index_ref, energy_ref, x_ref, coords_ref, counts_ref, sems
+    x_hbm, coords_hbm, counts_hbm, e_hbm, out_ref, index_ref, energy_ref, x_ref, coords_ref, counts_ref, sems
 ):
     pairs = ((x_hbm, x_ref), (coords_hbm, coords_ref), (counts_hbm, counts_ref), (e_hbm, energy_ref))
     copies = [pltpu.make_async_copy(a, b, sems.at[n]) for n, (a, b) in enumerate(pairs)]
@@ -74,7 +80,6 @@
         copy.wait()
     for j in range(2):
         value = x_ref[:, j, :]
-        own_ref[j] = value
         for c in range(NC):
             out_ref[c, j * VECS : (j + 1) * VECS] = value
     live = lax.broadcasted_iota(jnp.int32, (1, SLOTS), 1) < counts_ref[0, 0]
@@ -89,14 +94,16 @@
         index_ref[n : n + 1] = jnp.where(live, tile, dead)
 
 
-def regroup_kernel(own_ref, in_ref, out_ref):
+def regroup_kernel(in_ref, out_ref, own_ref):
     wide = 2 * VECS
+    own = in_ref[lax.axis_index("zl") * 8 + lax.axis_index("y")]
+    for j in range(2):
+        own_ref[j] = own[j * VECS : (j + 1) * VECS]
     for r in range(NR):
         at = row_at(r)
         for s in range(2):
-            out_ref[at, s * wide : (s + 1) * wide] = in_ref[col_at(2 * r + s), :wide]
-        for j in range(2):
-            out_ref[at, 2 * wide + j * VECS : 2 * wide + (j + 1) * VECS] = own_ref[j]
+            out_ref[at, s * wide : (s + 1) * wide] = in_ref[col_at(2 * r + s)]
+        out_ref[at, 2 * wide :] = own
 
 
 def tiles_kernel(with_gram, *refs):
@@ -186,7 +193,7 @@
             cross = cross + lax.dot_general(term, own, NT_DIMS, preferred_element_type=F32)
     message = message_of(widen(gram), widen(cross))
     for r in range(NR):
-        out_ref[r, part(GROUP)] = message
+        out_ref[r, GROUP * VECS :] = message
 
 
 def widen(value):
@@ -195,23 +202,28 @@
 
 def message_of(gram, cross):
     total = jnp.zeros((VECS, LANES), F32)
-    for base, value in ((0, gram), (HALF, cross)):
-        for n, part in enumerate(split3(value)):
-            part = part.astype(F32)
-            total = total + (pltpu.roll(part, base + n * VECS, 1) if base + n else part)
-    return total.astype(BF16)
+    for n, part in enumerate(split2(gram) + split2(cross)):
+        part = part.astype(F32)
+        total = total + (pltpu.roll(part, n * VECS, 1) if n else part)
+    return (total[:MESSAGE] + pltpu.roll(total[MESSAGE:], HALF, 1)).astype(BF16)
 
 
 def read_message(total):
+    total = jnp.concatenate([total, pltpu.roll(total, HALF, 1)], axis=0)
     keep = lane_index() < VECS
     found = []
-    for base in (0, HALF):
-        value = jnp.zeros((VECS, LANES), F32)
-        for n in (2, 1, 0):
-            shift = base + n * VECS
-            value = value + (pltpu.roll(total, LANES - shift, 1) if shift else total)
-        found.append(jnp.where(keep, value, 0.0))
+    for n in (0, 2):
+        high = pltpu.roll(total, LANES - n * VECS, 1) if n else total
+        low = pltpu.roll(total, LANES - (n + 1) * VECS, 1)
+        found.append(jnp.where(keep, high + low, 0.0))
     return found
+
+
+def sum_over(in_ref, start, rows):
+    total = in_ref[0, start : start + rows].astype(F32)
+    for n in range(1, in_ref.shape[0]):
+        total = total + in_ref[n, start : start + rows].astype(F32)
+    return total
 
 
 def collect_kernel(with_gram, in_ref, out_ref, back_ref):
@@ -220,53 +232,31 @@
         for s in range(2):
             out_ref[col_at(2 * r + s), :wide] = in_ref[row_at(r), s * wide : (s + 1) * wide]
 
-    def total_of(g):
-        part = slice(g * VECS, (g + 1) * VECS)
-        total = in_ref[0, part].astype(F32)
-        for r in range(1, NR):
-            total = total + in_ref[r, part].astype(F32)
-        return total
-
-    for j in range(2):
-        back_ref[j] = total_of(4 + j)
+    for j in range(2):
+        back_ref[j] = sum_over(in_ref, (4 + j) * VECS, VECS)
     if with_gram:
-        message = message_of(*read_message(total_of(GROUP)))
+        message = message_of(*read_message(sum_over(in_ref, GROUP * VECS, MESSAGE)))
         for c in range(NC):
             out_ref[c, wide:] = message
 
 
-def sum_over(in_ref, g):
-    part = slice(g * VECS, (g + 1) * VECS)
-    total = in_ref[0, part].astype(F32)
-    for c in range(1, NC):
-        total = total + in_ref[c, part].astype(F32)
-    return total
-
-
-def solve_kernel(in_ref, back_ref, own_ref, e_ref, out_ref, residual_ref, result_ref):
-    gram, cross = read_message(sum_over(in_ref, 2))
+def solve_kernel(in_ref, back_ref, own_ref, e_ref, out_ref, result_ref):
+    gram, cross = read_message(sum_over(in_ref, 2 * VECS, MESSAGE))
     wide = jnp.concatenate([cross, jnp.zeros((LANES - VECS, LANES), F32)], axis=0)
     cross = cross + jnp.transpose(wide)[:VECS]
     state = jnp.concatenate([gram, cross], axis=0)
     lane = lax.broadcasted_iota(jnp.int32, (2 * VECS, LANES), 1)
-    for p in range(0, VECS, 2):
-        first, second = state[:, p : p + 1], state[:, p + 1 : p + 2]
-        a, b = first[p : p + 1], second[p : p + 1]
-        c, d = first[p + 1 : p + 2], second[p + 1 : p + 2]
-        scale = 1.0 / (a * d - b * c)
-        new_first = (first * d - second * c) * scale
-        new_second = (second * a - first * b) * scale
-        rest = state - new_first * state[p : p + 1] - new_second * state[p + 1 : p + 2]
-        state = jnp.where(lane == p, new_first, jnp.where(lane == p + 1, new_second, rest))
+    for p in range(VECS):
+        column = state[:, p : p + 1] * (1.0 / state[p : p + 1, p : p + 1])
+        state = jnp.where(lane == p, column, state - column * state[p : p + 1])
     mix = state[VECS:]
     for j in range(2):
         v = own_ref[j].astype(F32)
-        product = sum_over(in_ref, j) + back_ref[j] + e_ref[j : j + 1, :] * v
+        product = sum_over(in_ref, j * VECS, VECS) + back_ref[j] + e_ref[j : j + 1, :] * v
         shifted = jnp.zeros((VECS, LANES), F32)
         for k in range(VECS):
             shifted = shifted + mix[:, k : k + 1] * v[k : k + 1, :]
         value = (product - shifted).astype(BF16)
-        residual_ref[j] = value
         result_ref[:, j, :] = value
         for c in range(NC):
             out_ref[c, j * VECS : (j + 1) * VECS] = value
@@ -274,7 +264,7 @@
 
 def finish_kernel(in_ref, back_ref, own_ref, e_ref, out_ref):
     for j in range(2):
-        total = sum_over(in_ref, j) + back_ref[j]
+        total = sum_over(in_ref, j * VECS, VECS) + back_ref[j]
         out_ref[:, j, :] = total + e_ref[j : j + 1, :] * own_ref[j].astype(F32)
 
 
@@ -282,9 +272,11 @@
     return lax.all_to_all(value, axis, split_axis=0, concat_axis=0, tiled=True)
 
 
-def apply_tiles(own, spread, index, tiles, energies, with_gram):
+def apply_tiles(spread, index, tiles, energies, with_gram):
     by_block = exchange(spread, COL)
-    grouped = call(regroup_kernel, shape(NR, GROUP * VECS, LANES), 2)(own, by_block)
+    grouped, own = call(
+        regroup_kernel, (shape(NR, GROUP * VECS, LANES), shape(2, VECS, LANES)), 1
+    )(by_block)
     fields = exchange(grouped, ROW)
     scratch = [
         pltpu.VMEM((ROW_DEAD + 1, VECS, LANES), BF16),
@@ -292,15 +284,15 @@
         pltpu.VMEM((ROW_DEAD + 1, VECS, LANES), F32),
         pltpu.VMEM((COL_DEAD + 1, VECS, LANES), F32),
     ]
-    extra = 0
+    message = 0
     args = (index, fields, tiles)
     if with_gram:
-        extra = 1
+        message = MESSAGE
         args = args + (own, energies)
         scratch.append(pltpu.VMEM((3, 2 * NR, VECS, LANES), BF16))
     partial = call(
         functools.partial(tiles_kernel, with_gram),
-        shape(NR, (GROUP + extra) * VECS, LANES),
+        shape(NR, GROUP * VECS + message, LANES),
         len(args),
         scratch,
         scalars=(0,),
@@ -308,19 +300,18 @@
     moved = exchange(partial, ROW)
     by_block, back = call(
         functools.partial(collect_kernel, with_gram),
-        (shape(NC, (2 + extra) * VECS, LANES), shape(2, VECS, LANES, dtype=F32)),
+        (shape(NC, 2 * VECS + message, LANES), shape(2, VECS, LANES, dtype=F32)),
         1,
     )(moved)
-    return exchange(by_block, COL), back
+    return exchange(by_block, COL), back, own
 
 
 def shards(vectors, tile_values, tile_coords, tile_counts, energies):
     tiles = tile_values[0]
-    spread, own, index, energies = call(
+    spread, index, energies = call(
         spread_kernel,
         (
             shape(NC, 2 * VECS, LANES),
-            shape(2, VECS, LANES),
             shape(2, SLOTS, dtype=jnp.int32),
             shape(2, LANES, dtype=F32),
         ),
@@ -334,13 +325,11 @@
         first=pl.BlockSpec(memory_space=pl.ANY),
         limit=60,
     )(vectors, tile_coords, tile_counts, energies)
-    forward, back = apply_tiles(own, spread, index, tiles, energies, True)
-    spread, residual, result = call(
-        solve_kernel,
-        (shape(NC, 2 * VECS, LANES), shape(2, VECS, LANES), shape(VECS, 2, LANES)),
-        4,
+    forward, back, own = apply_tiles(spread, index, tiles, energies, True)
+    spread, result = call(
+        solve_kernel, (shape(NC, 2 * VECS, LANES), shape(VECS, 2, LANES)), 4
     )(forward, back, own, energies)
-    forward, back = apply_tiles(residual, spread, index, tiles, energies, False)
+    forward, back, residual = apply_tiles(spread, index, tiles, energies, False)
     image = call(finish_kernel, shape(VECS, 2, LANES, dtype=F32), 4)(
         forward, back, residual, energies
     )

time: 178 us -> 175 us (0.983)
  blocking collectives: 162 us -> 160 us
    all_to_all x8, blocking collectives: 162 us -> 160 us  [exchange(): return lax.all_to_all(value, axis, split_axis=0, concat_axis=0, tiled=True)]
where the time goes in v4:
time: 175 us; the launch traced here: 173 us
  blocking collectives  160 us (91%)
  Pallas kernels  10.6 us (6%)
    all_to_all x8, blocking collectives, exchange(): return lax.all_to_all(value, axis, split_axis=0, concat_axis=0, tiled=True)  160 us
    pallas_call x2, Pallas kernels, apply_tiles(): call(functools.partial(tiles_kernel, with_gram), shape(NR, GROUP * VECS +...  5.79 us

profile of v4, /device:TPU:6, one launch (start us, length us, event | category | flops | bytes accessed | tf_op | source)
XLA Modules:
  0.0 172.7 jit_solution(5020589629789051018)
XLA Ops:
  0.6 0.0 copy-start
  1.4 1.5 shard_map.68
  2.9 25.5 %all_to_all.40.in_ref = bf16[32,32,128]{2,1,0:T(8,128)(2,1)S(1)} all-to-all(bf16[32,32,128]{2,1,0:T(8,128)(2,1)} %get-tuple-element.16), channel_id=1, replica_groups=mesh['zh'=2,'x'=4,'core'=2,'y'=8,'zl'=4] {'zl','y'}, dimensions={0} | all-to-all | bytes 524288 | tf_op jit(solution)/shard_map/all_to_all | solution.py:272
  28.4 0.0 copy-start.2
  28.4 22.8 %all_to_all.41.refs_1_ = bf16[16,96,128]{2,1,0:T(8,128)(2,1)S(1)} all-to-all(bf16[16,96,128]{2,1,0:T(8,128)(2,1)S(1)} %get-tuple-element.17), channel_id=1, replica_groups=mesh['zh'=2,'x'=4,'core'=2,'y'=8,'zl'=4] {'x','core','zh'}, dimensions={0} | all-to-all | bytes 786432 | tf_op jit(solution)/shard_map/all_to_all | solution.py:272
  51.2 0.0 copy-start.1
  51.2 0.0 copy-done
  51.2 0.0 copy-done.2
  51.2 0.7 copy-done.1
  51.9 3.1 %shard_map.70 = bf16[16,104,128]{2,1,0:T(8,128)(2,1)S(1)} custom-call(s32[2,128]{1,0:T(2,128)S(1)} %copy-done.2, bf16[16,96,128]{2,1,0:T(8,128)(2,1)S(1)} %all_to_all.41.refs_1_, bf16[64,64,128]{2,1,0:T(8,128)(2,1)S(1)} %bitcast.1, bf16[2,16,128]{2,1,0:T(8,128)(2,1)S(1)} %get-tuple-element.18.refs_3_.own_ref, f32[2,128]{1,0:T(2,128)S(1)} %copy-done.1), custom_call_target="tpu_custom_call" | custom-call | tf_op jit(solution)/shard_map/pallas_call | solution.py:293
  55.0 16.1 %all_to_all.42.in_ref = bf16[16,104,128]{2,1,0:T(8,128)(2,1)S(1)} all-to-all(bf16[16,104,128]{2,1,0:T(8,128)(2,1)S(1)} %shard_map.70), channel_id=1, replica_groups=mesh['zh'=2,'x'=4,'core'=2,'y'=8,'zl'=4] {'x','core','zh'}, dimensions={0} | all-to-all | bytes 851968 | tf_op jit(solution)/shard_map/all_to_all | solution.py:272
  71.1 0.3 shard_map.71
  71.4 23.5 %all_to_all.43.in_ref = bf16[32,40,128]{2,1,0:T(8,128)(2,1)S(1)} all-to-all(bf16[32,40,128]{2,1,0:T(8,128)(2,1)S(1)} %get-tuple-element.20), channel_id=1, replica_groups=mesh['zh'=2,'x'=4,'core'=2,'y'=8,'zl'=4] {'zl','y'}, dimensions={0} | all-to-all | bytes 655360 | tf_op jit(solution)/shard_map/all_to_all | solution.py:272
  94.9 2.2 %shard_map.72 = (bf16[32,32,128]{2,1,0:T(8,128)(2,1)S(1)}, bf16[16,2,128]{2,1,0:T(2,128)(2,1)}) custom-call(bf16[32,40,128]{2,1,0:T(8,128)(2,1)S(1)} %all_to_all.43.in_ref, f32[2,16,128]{2,1,0:T(8,128)S(1)} %get-tuple-element.21.back_ref, bf16[2,16,128]{2,1,0:T(8,128)(2,1)S(1)} %get-tuple-element.18.refs_3_.own_ref, f32[2,128]{1,0:T(2,128)S(1)} %copy-done.1), custom_call_target="tpu_custom_call" | custom-call | tf_op jit(solution)/shard_map/pallas_call | solution.py:329
  97.1 17.1 %all_to_all.44.in_ref = bf16[32,32,128]{2,1,0:T(8,128)(2,1)S(1)} all-to-all(bf16[32,32,128]{2,1,0:T(8,128)(2,1)S(1)} %get-tuple-element.23), channel_id=1, replica_groups=mesh['zh'=2,'x'=4,'core'=2,'y'=8,'zl'=4] {'zl','y'}, dimensions={0} | all-to-all | bytes 524288 | tf_op jit(solution)/shard_map/all_to_all | solution.py:272
  114.2 17.2 %all_to_all.45.refs_1_ = bf16[16,96,128]{2,1,0:T(8,128)(2,1)S(1)} all-to-all(bf16[16,96,128]{2,1,0:T(8,128)(2,1)S(1)} %get-tuple-element.24), channel_id=1, replica_groups=mesh['zh'=2,'x'=4,'core'=2,'y'=8,'zl'=4] {'x','core','zh'}, dimensions={0} | all-to-all | bytes 786432 | tf_op jit(solution)/shard_map/all_to_all | solution.py:272
  131.4 2.7 %shard_map.74 = bf16[16,96,128]{2,1,0:T(8,128)(2,1)S(1)} custom-call(s32[2,128]{1,0:T(2,128)S(1)} %copy-done.2, bf16[16,96,128]{2,1,0:T(8,128)(2,1)S(1)} %all_to_all.45.refs_1_, bf16[64,64,128]{2,1,0:T(8,128)(2,1)S(1)} %bitcast.2), custom_call_target="tpu_custom_call" | custom-call | tf_op jit(solution)/shard_map/pallas_call | solution.py:293
  134.1 15.8 %all_to_all.46.in_ref = bf16[16,96,128]{2,1,0:T(8,128)(2,1)S(1)} all-to-all(bf16[16,96,128]{2,1,0:T(8,128)(2,1)S(1)} %shard_map.74), channel_id=1, replica_groups=mesh['zh'=2,'x'=4,'core'=2,'y'=8,'zl'=4] {'x','core','zh'}, dimensions={0} | all-to-all | bytes 786432 | tf_op jit(solution)/shard_map/all_to_all | solution.py:272
  149.9 22.1 %all_to_all.47.in_ref = bf16[32,32,128]{2,1,0:T(8,128)(2,1)S(1)} all-to-all(bf16[32,32,128]{2,1,0:T(8,128)(2,1)S(1)} %get-tuple-element.25), channel_id=1, replica_groups=mesh['zh'=2,'x'=4,'core'=2,'y'=8,'zl'=4] {'zl','y'}, dimensions={0} | all-to-all | bytes 524288 | tf_op jit(solution)/shard_map/all_to_all | solution.py:272
  172.0 0.7 shard_map.76
  (3 shorter events, 0.1 us)
Async XLA Ops:
  0.6 50.6 %copy-start = (bf16[1,64,64,128]{3,2,1,0:T(8,128)(2,1)S(1)}, bf16[1,64,64,128]{3,2,1,0:T(8,128)(2,1)}, u32[]{:S(2)}) copy-start(bf16[1,64,64,128]{3,2,1,0:T(8,128)(2,1)} %param.6) | copy-start | bytes 3145732
  28.4 22.8 %copy-start.2 = (s32[2,128]{1,0:T(2,128)S(1)}, s32[2,128]{1,0:T(2,128)}, u32[]{:S(2)}) copy-start(s32[2,128]{1,0:T(2,128)} %get-tuple-element.15.refs_0_) | copy-start | bytes 3076
  51.2 0.7 copy-start.1

commit v5 on v4

v5 whole, which is shorter than its diff:
```python
import functools

import jax
import jax.numpy as jnp
import numpy as np
from jax import lax
from jax.experimental import pallas as pl
from jax.experimental.pallas import tpu as pltpu
from jax.sharding import PartitionSpec as P

F32 = jnp.float32
BF16 = jnp.bfloat16
VECS = 16
LANES = 128
HALF = 64
MESSAGE = 8
NR = 16
NC = 32
GROUP = 6
PIECES = 32
SLOTS = 128
UNROLL = 16
ROW_DEAD = NR * 8
COL_DEAD = NR * 4
ROW = ("x", "core", "zh")
COL = ("zl", "y")
PIECE = ("x", "zh", "zl")
OWNER = ("y", "core")
VMEM = pl.BlockSpec(memory_space=pltpu.VMEM)
SMEM = pl.BlockSpec(memory_space=pltpu.SMEM)
NT_DIMS = (((1,), (1,)), ((), ()))


def row_at(r):
    return (r % 8) * 2 + r // 8


def col_at(c):
    return (c % 4) * 8 + c // 4


def shape(*dims, dtype=BF16):
    return jax.ShapeDtypeStruct(dims, dtype)


def call(kernel, outs, n_in, scratch=(), scalars=(), first=VMEM, limit=32):
    specs = [SMEM if n in scalars else first for n in range(n_in)]
    return pl.pallas_call(
        kernel,
        out_shape=outs,
        in_specs=specs,
        out_specs=jax.tree.map(lambda _: VMEM, outs),
        scratch_shapes=list(scratch),
        compiler_params=pltpu.CompilerParams(vmem_limit_bytes=limit * 1024 * 1024),
    )


def lane_index():
    return lax.broadcasted_iota(jnp.int32, (VECS, LANES), 1)


def split2(value):
    high = value.astype(BF16)
    return high, (value - high.astype(F32)).astype(BF16)


def split3(value):
    high = value.astype(BF16)
    rest = value - high.astype(F32)
    middle = rest.astype(BF16)
    low = (rest - middle.astype(F32)).astype(BF16)
    return high, middle, low


def piece_at(x, zh, core, j):
    return x * 8 + zh * 4 + core * 2 + j


def locate(by_row, x, zh, core, j, slot):
    if by_row:
        place = slot * 2 + j if slot < 2 else 4 + j
        return x * 4 + core * 2 + zh, slice(place * VECS, (place + 1) * VECS)
    return piece_at(x, zh, core, j), slice(slot * VECS, (slot + 1) * VECS)


INNER = [(zh, core, j) for zh in range(2) for core in range(2) for j in range(2)]


def spread_kernel(
    x_hbm, coords_hbm, counts_hbm, e_hbm, out_ref, index_ref, energy_ref, x_ref, coords_ref, counts_ref, sems
):
    pairs = ((x_hbm, x_ref), (coords_hbm, coords_ref), (counts_hbm, counts_ref), (e_hbm, energy_ref))
    copies = [pltpu.make_async_copy(a, b, sems.at[n]) for n, (a, b) in enumerate(pairs)]
    for copy in copies:
        copy.start()
    for copy in copies:
        copy.wait()
    for j in range(2):
        value = x_ref[:, j, :]
        for c in range(NC):
            out_ref[c, j * VECS : (j + 1) * VECS] = value
    live = lax.broadcasted_iota(jnp.int32, (1, SLOTS), 1) < counts_ref[0, 0]
    for n, dead in ((0, ROW_DEAD), (1, COL_DEAD)):
        coords = coords_ref[n]
        major = coords >> 6
        piece = ((major >> 2) & 3) * 8 + (major >> 4) * 4 + (major & 3)
        if n == 0:
            piece = piece * 2 + ((coords >> 1) & 1)
        index_ref[n : n + 1] = jnp.where(live, piece * 2 + (coords & 1), dead)


def regroup_kernel(in_ref, out_ref, own_ref, kept_ref, sent_ref):
    wide = 2 * VECS
    y, zl, core = lax.axis_index("y"), lax.axis_index("zl"), lax.axis_index("core")
    own = in_ref[zl * 8 + y]
    half = lax.rem(zl, 2) == 0
    for j in range(2):
        own_ref[j] = own[j * VECS : (j + 1) * VECS]
        for target, side in ((kept_ref, core), (sent_ref, 1 - core)):
            value = in_ref[(side * 2 + j) * 8 + y]
            target[j] = jnp.where(half, value[:VECS], value[VECS:])
    for r in range(NR):
        at = row_at(r)
        for s in range(2):
            out_ref[at, s * wide : (s + 1) * wide] = in_ref[col_at(2 * r + s)]
        out_ref[at, 2 * wide :] = own


def regroup_back_kernel(in_ref, out_ref):
    y, core = lax.axis_index("y"), lax.axis_index("core")
    for zl in range(4):
        column = in_ref[y * 2 + zl // 2, (zl % 2) * VECS : (zl % 2 + 1) * VECS]
        for block in range(8):
            zh, x = block // 4, block % 4
            at = (x * 2 + zh) * 4 + zl
            out_ref[at, : 2 * VECS] = in_ref[block * 2 + core]
            out_ref[at, 2 * VECS :] = column


def tiles_kernel(first, *refs):
    if first:
        idx_ref, x_ref, w_ref, own_ref, e_ref, out_ref, *scratch = refs
    else:
        idx_ref, x_ref, w_ref, out_ref, own_ref, *scratch = refs
    field_row, field_col, acc_row, acc_col = scratch[:4]
    low_half = lane_index() < HALF
    zero = jnp.zeros((VECS, LANES), F32)
    half_mask = [low_half, jnp.logical_not(low_half)]
    half_one = [jnp.where(m, 1.0, 0.0).astype(BF16) for m in half_mask]
    own_piece = piece_at(lax.axis_index("x"), lax.axis_index("zh"), lax.axis_index("core"), 0)

    def part(g):
        return slice(g * VECS, (g + 1) * VECS)

    def place(piece, slot):
        if slot < 2:
            return field_row, acc_row, (piece * 2 + slot) * 2
        return field_col, acc_col, piece * 2

    def duplicate(x, carry):
        for zh, core, j in INNER:
            for slot in range(3):
                chunk, rows = locate(first, x, zh, core, j, slot)
                value = x_ref[chunk, rows].astype(F32)
                turned = pltpu.roll(value, HALF, 1)
                field, acc, at = place(piece_at(x, zh, core, j), slot)
                field[at] = jnp.where(low_half, value, turned).astype(BF16)
                field[at + 1] = jnp.where(low_half, turned, value).astype(BF16)
                acc[at] = zero
                acc[at + 1] = zero
        return carry

    lax.fori_loop(0, 4, duplicate, 0)
    for field, acc, dead in ((field_row, acc_row, ROW_DEAD), (field_col, acc_col, COL_DEAD)):
        field[dead] = zero.astype(BF16)
        acc[dead] = zero

    def block(b, carry):
        work = []
        for u in range(UNROLL):
            q = b * UNROLL + u
            rows = [idx_ref[0, q * 4 + k] for k in range(4)]
            cols = [idx_ref[1, q * 4 + k] for k in range(4)]
            w = w_ref[pl.ds(2 * q, 2)].reshape(2 * HALF, LANES)
            left_f = jnp.concatenate([field_col[cols[k]] * half_one[k % 2] for k in range(4)], axis=0)
            left_b = jnp.concatenate([field_row[rows[k]] * half_one[k // 2] for k in range(4)], axis=0)
            forward = lax.dot_general(left_f, w, NT_DIMS, preferred_element_type=F32)
            backward = jnp.dot(left_b, w, preferred_element_type=F32)
            work.append((rows, cols, forward, backward))
        for rows, cols, forward, backward in work:
            for k in range(4):
                acc_row[rows[k]] += jnp.where(half_mask[k // 2], forward[part(k)], 0.0)
                acc_col[cols[k]] += jnp.where(half_mask[k % 2], backward[part(k)], 0.0)
        return carry

    lax.fori_loop(0, SLOTS // 4 // UNROLL, block, 0)

    def add_energies(j):
        value = own_ref[j].astype(F32) * (0.5 * e_ref[j : j + 1, :])
        at = (own_piece + j) * 2
        for h in range(2):
            acc_col[at + h] += jnp.where(half_mask[h], value, 0.0)

    def folded(piece, slot):
        _, acc, at = place(piece, slot)
        one, two = acc[at], acc[at + 1]
        return jnp.where(low_half, one, two) + pltpu.roll(jnp.where(low_half, two, one), HALF, 1)

    def pack(x, carry):
        for zh, core, j in INNER:
            piece = piece_at(x, zh, core, j)
            for slot in range(3):
                total = folded(piece, slot)
                chunk, rows = locate(not first, x, zh, core, j, slot)
                out_ref[chunk, rows] = total.astype(BF16)
                if first and slot == 2:
                    for n, term in enumerate(split3(total)):
                        scratch[4][n, piece] = term
        return carry

    if not first:
        lax.fori_loop(0, 4, pack, 0)
        for j in range(2):
            own_ref[j] = x_ref[own_piece + j, part(2)]
        return

    for j in range(2):
        add_energies(j)
    lax.fori_loop(0, 4, pack, 0)
    terms = scratch[4]
    left = jnp.concatenate(
        [jnp.concatenate([terms[n, p] for p in range(PIECES)], axis=1) for n in range(3)], axis=0
    )
    pieces = []
    for x in range(4):
        for zh, core, j in INNER:
            chunk, rows = locate(True, x, zh, core, j, 2)
            pieces.append(x_ref[chunk, rows])
    crosses = lax.dot_general(
        left, jnp.concatenate(pieces, axis=1), NT_DIMS, preferred_element_type=F32
    )
    cross = crosses[:VECS] + crosses[VECS : 2 * VECS] + crosses[2 * VECS :]
    gram = jnp.zeros((VECS, VECS), F32)
    for j in range(2):
        own = own_ref[j]
        gram = gram + lax.dot_general(own, own, NT_DIMS, preferred_element_type=F32)
        add_energies(j)
        out_ref[own_piece + j, part(2)] = folded(own_piece + j, 2).astype(BF16)
    message = message_of(widen(gram), widen(cross))
    for p in range(PIECES):
        out_ref[p, 3 * VECS :] = message


def widen(value):
    return jnp.concatenate([value, jnp.zeros((VECS, LANES - VECS), F32)], axis=1)


def message_of(gram, cross):
    total = jnp.zeros((VECS, LANES), F32)
    for n, part in enumerate(split2(gram) + split2(cross)):
        part = part.astype(F32)
        total = total + (pltpu.roll(part, n * VECS, 1) if n else part)
    return (total[:MESSAGE] + pltpu.roll(total[MESSAGE:], HALF, 1)).astype(BF16)


def read_message(total):
    total = jnp.concatenate([total, pltpu.roll(total, HALF, 1)], axis=0)
    keep = lane_index() < VECS
    found = []
    for n in (0, 2):
        high = pltpu.roll(total, LANES - n * VECS, 1) if n else total
        low = pltpu.roll(total, LANES - (n + 1) * VECS, 1)
        found.append(jnp.where(keep, high + low, 0.0))
    return found


def sum_over(in_ref, start, rows, chunks=None):
    total = None
    for n in range(in_ref.shape[0]) if chunks is None else chunks:
        value = in_ref[n, start : start + rows].astype(F32)
        total = value if total is None else total + value
    return total


def collect_owner_kernel(in_ref, out_ref, back_ref):
    wide = 2 * VECS
    y, core = lax.axis_index("y"), lax.axis_index("core")
    nothing = jnp.zeros((wide, LANES), BF16)
    for block in range(8):
        zh, x = block // 4, block % 4
        chunks = [(x * 2 + zh) * 4 + zl for zl in range(4)]
        out_ref[block * 2 + core, :wide] = sum_over(in_ref, 0, wide, chunks).astype(BF16)
        out_ref[block * 2 + 1 - core, :wide] = nothing
    sums = []
    for zl in range(4):
        sums.append(sum_over(in_ref, wide, VECS, [n * 4 + zl for n in range(8)]))
    for s in range(2):
        same = core == 0
        back_ref[s] = jnp.where(same, sums[s], sums[2 + s])
        other = jnp.where(same, sums[2 + s], sums[s])
        out_ref[y * 2 + 1 - core, s * VECS : (s + 1) * VECS] = other.astype(BF16)
    message = message_of(*read_message(sum_over(in_ref, 3 * VECS, MESSAGE)))
    for n in range(2 * 8):
        out_ref[n, wide:] = message


def solve_kernel(in_ref, back_ref, kept_ref, received_ref, out_ref):
    gram, cross = read_message(sum_over(in_ref, 2 * VECS, MESSAGE))
    wide = jnp.concatenate([cross, jnp.zeros((LANES - VECS, LANES), F32)], axis=0)
    cross = cross + jnp.transpose(wide)[:VECS]
    state = jnp.concatenate([gram, cross], axis=0)
    lane = lax.broadcasted_iota(jnp.int32, (2 * VECS, LANES), 1)
    for p in range(VECS):
        column = state[:, p : p + 1] * (1.0 / state[p : p + 1, p : p + 1])
        state = jnp.where(lane == p, column, state - column * state[p : p + 1])
    mix = state[VECS:]
    mine = lax.div(lax.axis_index("zl"), 2) == lax.axis_index("core")
    for s in range(2):
        v = jnp.where(mine, kept_ref[s].astype(F32), received_ref[s].astype(F32))
        product = sum_over(in_ref, s * VECS, VECS) + back_ref[s]
        shifted = jnp.zeros((VECS, LANES), F32)
        for k in range(VECS):
            shifted = shifted + mix[:, k : k + 1] * v[k : k + 1, :]
        value = (product - shifted).astype(BF16)
        for n in range(2 * 8):
            out_ref[n, s * VECS : (s + 1) * VECS] = value


def collect_kernel(in_ref, out_ref, back_ref):
    wide = 2 * VECS
    for r in range(NR):
        for s in range(2):
            out_ref[col_at(2 * r + s)] = in_ref[row_at(r), s * wide : (s + 1) * wide]
    for j in range(2):
        back_ref[j] = sum_over(in_ref, (4 + j) * VECS, VECS)


def finish_kernel(in_ref, back_ref, own_ref, e_ref, residual_ref, out_ref):
    for j in range(2):
        own = own_ref[j]
        total = sum_over(in_ref, j * VECS, VECS) + back_ref[j]
        residual_ref[:, j, :] = own
        out_ref[:, j, :] = total + e_ref[j : j + 1, :] * own.astype(F32)


def exchange(value, axis):
    return lax.all_to_all(value, axis, split_axis=0, concat_axis=0, tiled=True)


def shards(vectors, tile_values, tile_coords, tile_counts, energies):
    tiles = tile_values[0]
    piece = shape(2, VECS, LANES)
    scratch = [
        pltpu.VMEM((ROW_DEAD + 1, VECS, LANES), BF16),
        pltpu.VMEM((COL_DEAD + 1, VECS, LANES), BF16),
        pltpu.VMEM((ROW_DEAD + 1, VECS, LANES), F32),
        pltpu.VMEM((COL_DEAD + 1, VECS, LANES), F32),
    ]
    spread, index, energies = call(
        spread_kernel,
        (
            shape(NC, 2 * VECS, LANES),
            shape(2, SLOTS, dtype=jnp.int32),
            shape(2, LANES, dtype=F32),
        ),
        4,
        [
            pltpu.VMEM((VECS, 2, LANES), BF16),
            pltpu.VMEM((2, 1, SLOTS), jnp.int32),
            pltpu.SMEM((1, 1), jnp.int32),
            pltpu.SemaphoreType.DMA((4,)),
        ],
        first=pl.BlockSpec(memory_space=pl.ANY),
        limit=60,
    )(vectors, tile_coords, tile_counts, energies)

    slab = exchange(spread, COL)
    grouped, own, kept, sent = call(
        regroup_kernel, (shape(NR, GROUP * VECS, LANES), piece, piece, piece), 1
    )(slab)
    received = lax.ppermute(sent, "core", [(0, 1), (1, 0)])
    fields = exchange(grouped, ROW)
    partial = call(
        functools.partial(tiles_kernel, True),
        shape(PIECES, 3 * VECS + MESSAGE, LANES),
        5,
        scratch + [pltpu.VMEM((3, PIECES, VECS, LANES), BF16)],
        scalars=(0,),
    )(index, fields, tiles, own, energies)
    by_owner, back = call(
        collect_owner_kernel,
        (shape(NR, 2 * VECS + MESSAGE, LANES), shape(2, VECS, LANES, dtype=F32)),
        1,
    )(exchange(partial, PIECE))
    residual = call(solve_kernel, shape(NR, 2 * VECS, LANES), 4)(
        exchange(by_owner, OWNER), back, kept, received
    )

    grouped = call(regroup_back_kernel, shape(PIECES, 3 * VECS, LANES), 1)(exchange(residual, OWNER))
    partial, own = call(
        functools.partial(tiles_kernel, False),
        (shape(NR, GROUP * VECS, LANES), piece),
        3,
        scratch,
        scalars=(0,),
    )(index, exchange(grouped, PIECE), tiles)
    by_block, back = call(
        collect_kernel, (shape(NC, 2 * VECS, LANES), shape(2, VECS, LANES, dtype=F32)), 1
    )(exchange(partial, ROW))
    return call(
        finish_kernel, (shape(VECS, 2, LANES), shape(VECS, 2, LANES, dtype=F32)), 4
    )(exchange(by_block, COL), back, own, energies)


def solution(mesh):
    devices = np.asarray(mesh.devices).reshape(2, 4, 2, 8, 4)
    fine = jax.sharding.Mesh(devices, ("zh", "x", "core", "y", "zl"))
    row, col = ("zh", "x", "core"), ("y", "zl")
    in_specs = (
        P(None, row, col),
        P(row, col, None, None),
        P(None, row, col),
        P(row, col),
        P(row, col),
    )
    out_specs = (P(None, row, col), P(None, row, col))
    return jax.shard_map(shards, mesh=fine, in_specs=in_specs, out_specs=out_specs, check_vma=False)
```

time: 175 us -> 168 us (0.960)
  blocking collectives: 160 us -> 140 us
  waiting for transfers between devices: 0 us -> 6.98 us
  starting transfers between devices: 0 us -> 5.7 us
    all_to_all x8 -> x7, blocking collectives: 160 us -> 140 us  [exchange(): return lax.all_to_all(value, axis, split_axis=0, concat_axis=0, tiled=True)]
    all_to_all x0 -> x1, waiting for transfers between devices: none -> 6.11 us  [exchange(): return lax.all_to_all(value, axis, split_axis=0, concat_axis=0, tiled=True)]
    all_to_all x0 -> x1, starting transfers between devices: none -> 3.52 us  [exchange(): return lax.all_to_all(value, axis, split_axis=0, concat_axis=0, tiled=True)]
    ppermute x0 -> x1, starting transfers between devices: none -> 2.19 us  [shards(): received = lax.ppermute(sent, 'core', [(0, 1), (1, 0)])]
  transfers between devices with their start and end apart: 0 -> 2, of which waited for: 0 -> 2; matrix products, arithmetic and copies ran while one was open for 0% -> 0% of each run, Pallas kernels for 0% -> 0%
where the time goes in v5:
time: 168 us; the launch traced here: 166 us
  blocking collectives  140 us (83%)
  Pallas kernels  10.7 us (6%)
  waiting for transfers between devices  6.98 us (4%)
  starting transfers between devices  5.7 us (3%)
    all_to_all x7, blocking collectives, exchange(): return lax.all_to_all(value, axis, split_axis=0, concat_axis=0, tiled=True)  140 us
    all_to_all x1, waiting for transfers between devices, exchange(): return lax.all_to_all(value, axis, split_axis=0, concat_axis=0, tiled=True)  6.11 us
    all_to_all x1, starting transfers between devices, exchange(): return lax.all_to_all(value, axis, split_axis=0, concat_axis=0, tiled=True)  3.52 us
  transfers between devices with their start and end apart: 2, of which 2 were waited for; matrix products, arithmetic and copies ran while one was open for 0% of the time, Pallas kernels for 0%

profile of v5, /device:TPU:6, one launch (start us, length us, event | category | flops | bytes accessed | tf_op | source)
XLA Modules:
  0.0 165.8 jit_solution(3120735631431280923)
XLA Ops:
  0.6 0.0 copy-start
  1.4 1.5 shard_map.68
  2.9 25.5 %all_to_all.40.in_ref = bf16[32,32,128]{2,1,0:T(8,128)(2,1)S(1)} all-to-all(bf16[32,32,128]{2,1,0:T(8,128)(2,1)} %get-tuple-element.16), channel_id=1, replica_groups=mesh['zh'=2,'x'=4,'core'=2,'y'=8,'zl'=4] {'zl','y'}, dimensions={0} | all-to-all | bytes 524288 | tf_op jit(solution)/shard_map/all_to_all | solution.py:347
  28.4 0.0 copy-start.2
  28.4 22.8 %all_to_all.41.refs_1_ = bf16[16,96,128]{2,1,0:T(8,128)(2,1)S(1)} all-to-all(bf16[16,96,128]{2,1,0:T(8,128)(2,1)S(1)} %get-tuple-element.17), channel_id=1, replica_groups=mesh['zh'=2,'x'=4,'core'=2,'y'=8,'zl'=4] {'x','core','zh'}, dimensions={0} | all-to-all | bytes 786432 | tf_op jit(solution)/shard_map/all_to_all | solution.py:347
  51.2 0.0 copy-start.1
  51.2 0.0 copy-done
  51.2 0.0 copy-done.2
  51.2 0.7 copy-done.1
  51.9 3.2 %shard_map.70 = bf16[32,56,128]{2,1,0:T(8,128)(2,1)S(1)} custom-call(s32[2,128]{1,0:T(2,128)S(1)} %copy-done.2, bf16[16,96,128]{2,1,0:T(8,128)(2,1)S(1)} %all_to_all.41.refs_1_, bf16[64,64,128]{2,1,0:T(8,128)(2,1)S(1)} %bitcast.1, bf16[2,16,128]{2,1,0:T(8,128)(2,1)S(1)} %get-tuple-element.18.refs_3_, f32[2,128]{1,0:T(2,128)S(1)} %copy-done.1), custom_call_target="tpu_custom_call" | custom-call | tf_op jit(solution)/shard_map/pallas_call | solution.py:383
  55.0 22.3 %all_to_all.42.in_ref = bf16[32,56,128]{2,1,0:T(8,128)(2,1)S(1)} all-to-all(bf16[32,56,128]{2,1,0:T(8,128)(2,1)S(1)} %shard_map.70), channel_id=1, replica_groups=mesh['zh'=2,'x'=4,'core'=2,'y'=8,'zl'=4] {'x','zh','zl'}, dimensions={0} | all-to-all | bytes 917504 | tf_op jit(solution)/shard_map/all_to_all | solution.py:347
  77.3 1.0 shard_map.71
  78.3 3.5 %all-to-all-start.3 = ((bf16[16,40,128]{2,1,0:T(8,128)(2,1)}), bf16[16,40,128]{2,1,0:T(8,128)(2,1)S(1)}, u32[]{:S(2)}, u32[]{:S(2)}) async-start(bf16[16,40,128]{2,1,0:T(8,128)(2,1)} %get-tuple-element.20), calls=%async_computation.3 | async-start | bytes 327680 | tf_op jit(solution)/shard_map/all_to_all | solution.py:347
  81.8 2.2 %collective-permute-start = (bf16[2,16,128]{2,1,0:T(8,128)(2,1)S(1)}, bf16[2,16,128]{2,1,0:T(8,128)(2,1)S(1)}, u32[]{:S(2)}, u32[]{:S(2)}) collective-permute-start(bf16[2,16,128]{2,1,0:T(8,128)(2,1)S(1)} %get-tuple-element.23), channel_id=1, source_target_pairs={{0,32},{32,0},{1,33},{33,1},{2,34},{34,2},{3,35},{35,3},{4,36},{36... | collective-permute-start | bytes 24584 | tf_op jit(solution)/shard_map/ppermute | solution.py:381
  84.0 0.9 collective-permute-done.received_ref
  84.9 6.1 %all-to-all-done.3.in_ref = bf16[16,40,128]{2,1,0:T(8,128)(2,1)S(1)} async-done(((bf16[16,40,128]{2,1,0:T(8,128)(2,1)}), bf16[16,40,128]{2,1,0:T(8,128)(2,1)S(1)}, u32[]{:S(2)}, u32[]{:S(2)}) %all-to-all-start.3) | async-done | bytes 163872 | tf_op jit(solution)/shard_map/all_to_all | solution.py:347
  91.0 1.5 shard_map.72
  92.5 11.8 %all_to_all.43.in_ref = bf16[16,32,128]{2,1,0:T(8,128)(2,1)S(1)} all-to-all(bf16[16,32,128]{2,1,0:T(8,128)(2,1)S(1)} %shard_map.72), channel_id=1, replica_groups=mesh['zh'=2,'x'=4,'core'=2,'y'=8,'zl'=4] {'y','core'}, dimensions={0} | all-to-all | bytes 262144 | tf_op jit(solution)/shard_map/all_to_all | solution.py:347
  104.3 0.1 shard_map.73
  104.3 20.1 %all_to_all.44.refs_1_ = bf16[32,48,128]{2,1,0:T(8,128)(2,1)S(1)} all-to-all(bf16[32,48,128]{2,1,0:T(8,128)(2,1)S(1)} %shard_map.73), channel_id=1, replica_groups=mesh['zh'=2,'x'=4,'core'=2,'y'=8,'zl'=4] {'x','zh','zl'}, dimensions={0} | all-to-all | bytes 786432 | tf_op jit(solution)/shard_map/all_to_all | solution.py:347
  124.4 2.7 %shard_map.74 = (bf16[16,96,128]{2,1,0:T(8,128)(2,1)S(1)}, bf16[2,16,128]{2,1,0:T(8,128)(2,1)S(1)}) custom-call(s32[2,128]{1,0:T(2,128)S(1)} %copy-done.2, bf16[32,48,128]{2,1,0:T(8,128)(2,1)S(1)} %all_to_all.44.refs_1_, bf16[64,64,128]{2,1,0:T(8,128)(2,1)S(1)} %bitcast.2), custom_call_target="tpu_custom_call" | custom-call | tf_op jit(solution)/shard_map/pallas_call | solution.py:400
  127.2 17.5 %all_to_all.45.in_ref = bf16[16,96,128]{2,1,0:T(8,128)(2,1)S(1)} all-to-all(bf16[16,96,128]{2,1,0:T(8,128)(2,1)S(1)} %get-tuple-element.24), channel_id=1, replica_groups=mesh['zh'=2,'x'=4,'core'=2,'y'=8,'zl'=4] {'x','core','zh'}, dimensions={0} | all-to-all | bytes 786432 | tf_op jit(solution)/shard_map/all_to_all | solution.py:347
  144.7 20.4 %all_to_all.46.in_ref = bf16[32,32,128]{2,1,0:T(8,128)(2,1)S(1)} all-to-all(bf16[32,32,128]{2,1,0:T(8,128)(2,1)S(1)} %get-tuple-element.25), channel_id=1, replica_groups=mesh['zh'=2,'x'=4,'core'=2,'y'=8,'zl'=4] {'zl','y'}, dimensions={0} | all-to-all | bytes 524288 | tf_op jit(solution)/shard_map/all_to_all | solution.py:347
  165.1 0.7 shard_map.76
  (2 shorter events, 0.1 us)
Async XLA Ops:
  0.6 50.6 %copy-start = (bf16[1,64,64,128]{3,2,1,0:T(8,128)(2,1)S(1)}, bf16[1,64,64,128]{3,2,1,0:T(8,128)(2,1)}, u32[]{:S(2)}) copy-start(bf16[1,64,64,128]{3,2,1,0:T(8,128)(2,1)} %param.6) | copy-start | bytes 3145732
  28.4 22.8 %copy-start.2 = (s32[2,128]{1,0:T(2,128)S(1)}, s32[2,128]{1,0:T(2,128)}, u32[]{:S(2)}) copy-start(s32[2,128]{1,0:T(2,128)} %get-tuple-element.15.refs_0_) | copy-start | bytes 3076
  51.2 0.7 copy-start.1
  78.3 12.7 %all-to-all-start.3 = ((bf16[16,40,128]{2,1,0:T(8,128)(2,1)}), bf16[16,40,128]{2,1,0:T(8,128)(2,1)S(1)}, u32[]{:S(2)}, u32[]{:S(2)}) async-start(bf16[16,40,128]{2,1,0:T(8,128)(2,1)} %get-tuple-element.20), calls=%async_computation.3 | async-start | bytes 327680 | tf_op jit(solution)/shard_map/all_to_all | solution.py:347
  81.8 3.1 %collective-permute-start = (bf16[2,16,128]{2,1,0:T(8,128)(2,1)S(1)}, bf16[2,16,128]{2,1,0:T(8,128)(2,1)S(1)}, u32[]{:S(2)}, u32[]{:S(2)}) collective-permute-start(bf16[2,16,128]{2,1,0:T(8,128)(2,1)S(1)} %get-tuple-element.23), channel_id=1, source_target_pairs={{0,32},{32,0},{1,33},{33,1},{2,34},{34,2},{3,35},{35,3},{4,36},{36... | collective-permute-start | bytes 24584 | tf_op jit(solution)/shard_map/ppermute | solution.py:381

commit v6 on v5

--- a/solution.py
+++ b/solution.py
@@ -87,8 +87,9 @@
 
 
 def spread_kernel(
-    x_hbm, coords_hbm, counts_hbm, e_hbm, out_ref, index_ref, energy_ref, x_ref, coords_ref, counts_ref, sems
+    x_hbm, coords_hbm, counts_hbm, e_hbm, out_ref, index_ref, energy_ref, *refs
 ):
+    messages, (x_ref, coords_ref, counts_ref, sems) = refs[:2], refs[2:]
     pairs = ((x_hbm, x_ref), (coords_hbm, coords_ref), (counts_hbm, counts_ref), (e_hbm, energy_ref))
     copies = [pltpu.make_async_copy(a, b, sems.at[n]) for n, (a, b) in enumerate(pairs)]
     for copy in copies:
@@ -99,6 +100,14 @@
         value = x_ref[:, j, :]
         for c in range(NC):
             out_ref[c, j * VECS : (j + 1) * VECS] = value
+    odd = lax.rem(lax.axis_index("zl"), 2)
+    row = lax.broadcasted_iota(jnp.int32, (VECS, LANES), 0)
+    for k, message in enumerate(messages):
+        message[:VECS] = jnp.where(odd == k, x_ref[:, 0, :], x_ref[:, 1, :])
+        terms = jnp.zeros((VECS, LANES), F32)
+        for n, term in enumerate(split3(jnp.where(odd == k, energy_ref[0:1], energy_ref[1:2]))):
+            terms = jnp.where(row == n, term.astype(F32), terms)
+        message[VECS:] = terms.astype(BF16)
     live = lax.broadcasted_iota(jnp.int32, (1, SLOTS), 1) < counts_ref[0, 0]
     for n, dead in ((0, ROW_DEAD), (1, COL_DEAD)):
         coords = coords_ref[n]
@@ -109,16 +118,17 @@
         index_ref[n : n + 1] = jnp.where(live, piece * 2 + (coords & 1), dead)
 
 
-def regroup_kernel(in_ref, out_ref, own_ref, kept_ref, sent_ref):
+def regroup_kernel(in_ref, even_ref, odd_ref, out_ref, own_ref, owned_ref, energy_ref):
     wide = 2 * VECS
-    y, zl, core = lax.axis_index("y"), lax.axis_index("zl"), lax.axis_index("core")
+    y, zl = lax.axis_index("y"), lax.axis_index("zl")
     own = in_ref[zl * 8 + y]
-    half = lax.rem(zl, 2) == 0
+    odd = lax.rem(zl, 2)
     for j in range(2):
         own_ref[j] = own[j * VECS : (j + 1) * VECS]
-        for target, side in ((kept_ref, core), (sent_ref, 1 - core)):
-            value = in_ref[(side * 2 + j) * 8 + y]
-            target[j] = jnp.where(half, value[:VECS], value[VECS:])
+        message = jnp.where(odd == j, even_ref[...], odd_ref[...])
+        owned_ref[j] = message[:VECS]
+        terms = message[VECS:].astype(F32)
+        energy_ref[j : j + 1] = terms[0:1] + terms[1:2] + terms[2:3]
     for r in range(NR):
         at = row_at(r)
         for s in range(2):
@@ -195,12 +205,6 @@
 
     lax.fori_loop(0, SLOTS // 4 // UNROLL, block, 0)
 
-    def add_energies(j):
-        value = own_ref[j].astype(F32) * (0.5 * e_ref[j : j + 1, :])
-        at = (own_piece + j) * 2
-        for h in range(2):
-            acc_col[at + h] += jnp.where(half_mask[h], value, 0.0)
-
     def folded(piece, slot):
         _, acc, at = place(piece, slot)
         one, two = acc[at], acc[at + 1]
@@ -224,8 +228,6 @@
             own_ref[j] = x_ref[own_piece + j, part(2)]
         return
 
-    for j in range(2):
-        add_energies(j)
     lax.fori_loop(0, 4, pack, 0)
     terms = scratch[4]
     left = jnp.concatenate(
@@ -244,8 +246,8 @@
     for j in range(2):
         own = own_ref[j]
         gram = gram + lax.dot_general(own, own, NT_DIMS, preferred_element_type=F32)
-        add_energies(j)
-        out_ref[own_piece + j, part(2)] = folded(own_piece + j, 2).astype(BF16)
+        for term in split3(own.astype(F32) * (0.5 * e_ref[j : j + 1, :])):
+            cross = cross + lax.dot_general(term, own, NT_DIMS, preferred_element_type=F32)
     message = message_of(widen(gram), widen(cross))
     for p in range(PIECES):
         out_ref[p, 3 * VECS :] = message
@@ -304,7 +306,7 @@
         out_ref[n, wide:] = message
 
 
-def solve_kernel(in_ref, back_ref, kept_ref, received_ref, out_ref):
+def solve_kernel(in_ref, back_ref, owned_ref, e_ref, out_ref):
     gram, cross = read_message(sum_over(in_ref, 2 * VECS, MESSAGE))
     wide = jnp.concatenate([cross, jnp.zeros((LANES - VECS, LANES), F32)], axis=0)
     cross = cross + jnp.transpose(wide)[:VECS]
@@ -314,10 +316,9 @@
         column = state[:, p : p + 1] * (1.0 / state[p : p + 1, p : p + 1])
         state = jnp.where(lane == p, column, state - column * state[p : p + 1])
     mix = state[VECS:]
-    mine = lax.div(lax.axis_index("zl"), 2) == lax.axis_index("core")
     for s in range(2):
-        v = jnp.where(mine, kept_ref[s].astype(F32), received_ref[s].astype(F32))
-        product = sum_over(in_ref, s * VECS, VECS) + back_ref[s]
+        v = owned_ref[s].astype(F32)
+        product = sum_over(in_ref, s * VECS, VECS) + back_ref[s] + e_ref[s : s + 1, :] * v
         shifted = jnp.zeros((VECS, LANES), F32)
         for k in range(VECS):
             shifted = shifted + mix[:, k : k + 1] * v[k : k + 1, :]
@@ -341,6 +342,11 @@
         total = sum_over(in_ref, j * VECS, VECS) + back_ref[j]
         residual_ref[:, j, :] = own
         out_ref[:, j, :] = total + e_ref[j : j + 1, :] * own.astype(F32)
+
+
+def owner_of(n, k):
+    core, zl = n // 4, n % 4
+    return n, zl // 2 * 4 + core * 2 + (zl % 2 ^ k)
 
 
 def exchange(value, axis):
@@ -356,12 +362,14 @@
         pltpu.VMEM((ROW_DEAD + 1, VECS, LANES), F32),
         pltpu.VMEM((COL_DEAD + 1, VECS, LANES), F32),
     ]
-    spread, index, energies = call(
+    spread, index, energies, *messages = call(
         spread_kernel,
         (
             shape(NC, 2 * VECS, LANES),
             shape(2, SLOTS, dtype=jnp.int32),
             shape(2, LANES, dtype=F32),
+            shape(2 * VECS, LANES),
+            shape(2 * VECS, LANES),
         ),
         4,
         [
@@ -374,11 +382,16 @@
         limit=60,
     )(vectors, tile_coords, tile_counts, energies)
 
+    received = [
+        lax.ppermute(message, ("core", "zl"), [owner_of(n, k) for n in range(8)])
+        for k, message in enumerate(messages)
+    ]
     slab = exchange(spread, COL)
-    grouped, own, kept, sent = call(
-        regroup_kernel, (shape(NR, GROUP * VECS, LANES), piece, piece, piece), 1
-    )(slab)
-    received = lax.ppermute(sent, "core", [(0, 1), (1, 0)])
+    grouped, own, owned, owned_energies = call(
+        regroup_kernel,
+        (shape(NR, GROUP * VECS, LANES), piece, piece, shape(2, LANES, dtype=F32)),
+        3,
+    )(slab, *received)
     fields = exchange(grouped, ROW)
     partial = call(
         functools.partial(tiles_kernel, True),
@@ -393,7 +406,7 @@
         1,
     )(exchange(partial, PIECE))
     residual = call(solve_kernel, shape(NR, 2 * VECS, LANES), 4)(
-        exchange(by_owner, OWNER), back, kept, received
+        exchange(by_owner, OWNER), back, owned, owned_energies
     )
 
     grouped = call(regroup_back_kernel, shape(PIECES, 3 * VECS, LANES), 1)(exchange(residual, OWNER))

time: 168 us -> 169 us (level)
  starting transfers between devices: 5.7 us -> 18 us
  blocking collectives: 140 us -> 129 us
    all_to_all x7, blocking collectives: 140 us -> 129 us  [exchange(): return lax.all_to_all(value, axis, split_axis=0, concat_axis=0, tiled=True)]
    all_to_all x1, starting transfers between devices: 3.52 us -> 12.9 us  [exchange(): return lax.all_to_all(value, axis, split_axis=0, concat_axis=0, tiled=True)]
    ppermute x1 -> x2, starting transfers between devices: 2.19 us -> 5.05 us  [shards(): lax.ppermute(message, ('core', 'zl'), [owner_of(n, k) for n in range(8)])]
  transfers between devices with their start and end apart: 2 -> 3, of which waited for: 2 -> 2; matrix products, arithmetic and copies ran while one was open for 0% -> 0% of each run, Pallas kernels for 0% -> 0%
where the time goes in v6:
time: 169 us; the launch traced here: 167 us
  blocking collectives  129 us (76%)
  starting transfers between devices  18 us (11%)
  Pallas kernels  9.96 us (6%)
  waiting for transfers between devices  7.47 us (4%)
    all_to_all x7, blocking collectives, exchange(): return lax.all_to_all(value, axis, split_axis=0, concat_axis=0, tiled=True)  129 us
    all_to_all x1, starting transfers between devices, exchange(): return lax.all_to_all(value, axis, split_axis=0, concat_axis=0, tiled=True)  12.9 us
    all_to_all x1, waiting for transfers between devices, exchange(): return lax.all_to_all(value, axis, split_axis=0, concat_axis=0, tiled=True)  5.23 us
    ppermute x2, starting transfers between devices, shards(): lax.ppermute(message, ('core', 'zl'), [owner_of(n, k) for n in range(8)])  5.05 us
  transfers between devices with their start and end apart: 3, of which 2 were waited for; matrix products, arithmetic and copies ran while one was open for 0% of the time, Pallas kernels for 0%

profile of v6, /device:TPU:6, one launch (start us, length us, event | category | flops | bytes accessed | tf_op | source)
XLA Modules:
  0.0 166.8 jit_solution(1597761656165732664)
XLA Ops:
  0.6 0.0 copy-start
  1.4 1.5 shard_map.68
  2.9 12.9 %all-to-all-start = ((bf16[32,32,128]{2,1,0:T(8,128)(2,1)}), bf16[32,32,128]{2,1,0:T(8,128)(2,1)S(1)}, u32[]{:S(2)}, u32[]{:S(2)}) async-start(bf16[32,32,128]{2,1,0:T(8,128)(2,1)} %get-tuple-element.18), calls=%async_computation | async-start | bytes 524288 | tf_op jit(solution)/shard_map/all_to_all | solution.py:353
  15.9 1.4 collective-permute-start
  17.2 3.7 %collective-permute-start.1 = (bf16[32,128]{1,0:T(8,128)(2,1)}, bf16[32,128]{1,0:T(8,128)(2,1)S(1)}, u32[]{:S(2)}, u32[]{:S(2)}) collective-permute-start(bf16[32,128]{1,0:T(8,128)(2,1)} %get-tuple-element.20), channel_id=1, source_target_pairs={{0,1},{1,0},{2,33},{3,32},{32,3},{33,2},{34,35},{35,34},{4,5},{5,4... | collective-permute-start | bytes 24584 | tf_op jit(solution)/shard_map/ppermute | solution.py:386
  20.9 0.0 collective-permute-done.even_ref
  20.9 2.2 %collective-permute-done.1.odd_ref = bf16[32,128]{1,0:T(8,128)(2,1)S(1)} collective-permute-done((bf16[32,128]{1,0:T(8,128)(2,1)}, bf16[32,128]{1,0:T(8,128)(2,1)S(1)}, u32[]{:S(2)}, u32[]{:S(2)}) %collective-permute-start.1) | collective-permute-done | bytes 8224 | tf_op jit(solution)/shard_map/ppermute | solution.py:386
  23.2 5.2 %all-to-all-done.in_ref = bf16[32,32,128]{2,1,0:T(8,128)(2,1)S(1)} async-done(((bf16[32,32,128]{2,1,0:T(8,128)(2,1)}), bf16[32,32,128]{2,1,0:T(8,128)(2,1)S(1)}, u32[]{:S(2)}, u32[]{:S(2)}) %all-to-all-start) | async-done | bytes 262176 | tf_op jit(solution)/shard_map/all_to_all | solution.py:353
  28.4 0.0 copy-start.2
  28.4 22.8 %all_to_all.40.refs_1_ = bf16[16,96,128]{2,1,0:T(8,128)(2,1)S(1)} all-to-all(bf16[16,96,128]{2,1,0:T(8,128)(2,1)S(1)} %get-tuple-element.21), channel_id=1, replica_groups=mesh['zh'=2,'x'=4,'core'=2,'y'=8,'zl'=4] {'x','core','zh'}, dimensions={0} | all-to-all | bytes 786432 | tf_op jit(solution)/shard_map/all_to_all | solution.py:353
  51.2 0.0 copy-start.1
  51.2 0.0 copy-done
  51.2 0.0 copy-done.2
  51.2 0.7 copy-done.1
  51.9 3.1 %shard_map.70 = bf16[32,56,128]{2,1,0:T(8,128)(2,1)S(1)} custom-call(s32[2,128]{1,0:T(2,128)S(1)} %copy-done.2, bf16[16,96,128]{2,1,0:T(8,128)(2,1)S(1)} %all_to_all.40.refs_1_, bf16[64,64,128]{2,1,0:T(8,128)(2,1)S(1)} %bitcast.1, bf16[2,16,128]{2,1,0:T(8,128)(2,1)S(1)} %get-tuple-element.22.refs_3_, f32[2,128]{1,0:T(2,128)S(1)} %copy-done.1), custom_call_target="tpu_custom_call" | custom-call | tf_op jit(solution)/shard_map/pallas_call | solution.py:396
  55.0 22.4 %all_to_all.41.in_ref = bf16[32,56,128]{2,1,0:T(8,128)(2,1)S(1)} all-to-all(bf16[32,56,128]{2,1,0:T(8,128)(2,1)S(1)} %shard_map.70), channel_id=1, replica_groups=mesh['zh'=2,'x'=4,'core'=2,'y'=8,'zl'=4] {'x','zh','zl'}, dimensions={0} | all-to-all | bytes 917504 | tf_op jit(solution)/shard_map/all_to_all | solution.py:353
  77.4 0.3 shard_map.71
  77.7 13.3 %all_to_all.42.in_ref = bf16[16,40,128]{2,1,0:T(8,128)(2,1)S(1)} all-to-all(bf16[16,40,128]{2,1,0:T(8,128)(2,1)S(1)} %get-tuple-element.24), channel_id=1, replica_groups=mesh['zh'=2,'x'=4,'core'=2,'y'=8,'zl'=4] {'y','core'}, dimensions={0} | all-to-all | bytes 327680 | tf_op jit(solution)/shard_map/all_to_all | solution.py:353
  91.0 1.5 shard_map.72
  92.6 11.8 %all_to_all.43.in_ref = bf16[16,32,128]{2,1,0:T(8,128)(2,1)S(1)} all-to-all(bf16[16,32,128]{2,1,0:T(8,128)(2,1)S(1)} %shard_map.72), channel_id=1, replica_groups=mesh['zh'=2,'x'=4,'core'=2,'y'=8,'zl'=4] {'y','core'}, dimensions={0} | all-to-all | bytes 262144 | tf_op jit(solution)/shard_map/all_to_all | solution.py:353
  104.3 0.1 shard_map.73
  104.4 21.1 %all_to_all.44.refs_1_ = bf16[32,48,128]{2,1,0:T(8,128)(2,1)S(1)} all-to-all(bf16[32,48,128]{2,1,0:T(8,128)(2,1)S(1)} %shard_map.73), channel_id=1, replica_groups=mesh['zh'=2,'x'=4,'core'=2,'y'=8,'zl'=4] {'x','zh','zl'}, dimensions={0} | all-to-all | bytes 786432 | tf_op jit(solution)/shard_map/all_to_all | solution.py:353
  125.5 2.7 %shard_map.74 = (bf16[16,96,128]{2,1,0:T(8,128)(2,1)S(1)}, bf16[2,16,128]{2,1,0:T(8,128)(2,1)S(1)}) custom-call(s32[2,128]{1,0:T(2,128)S(1)} %copy-done.2, bf16[32,48,128]{2,1,0:T(8,128)(2,1)S(1)} %all_to_all.44.refs_1_, bf16[64,64,128]{2,1,0:T(8,128)(2,1)S(1)} %bitcast.2), custom_call_target="tpu_custom_call" | custom-call | tf_op jit(solution)/shard_map/pallas_call | solution.py:413
  128.2 17.6 %all_to_all.45.in_ref = bf16[16,96,128]{2,1,0:T(8,128)(2,1)S(1)} all-to-all(bf16[16,96,128]{2,1,0:T(8,128)(2,1)S(1)} %get-tuple-element.28), channel_id=1, replica_groups=mesh['zh'=2,'x'=4,'core'=2,'y'=8,'zl'=4] {'x','core','zh'}, dimensions={0} | all-to-all | bytes 786432 | tf_op jit(solution)/shard_map/all_to_all | solution.py:353
  145.9 20.3 %all_to_all.46.in_ref = bf16[32,32,128]{2,1,0:T(8,128)(2,1)S(1)} all-to-all(bf16[32,32,128]{2,1,0:T(8,128)(2,1)S(1)} %get-tuple-element.29), channel_id=1, replica_groups=mesh['zh'=2,'x'=4,'core'=2,'y'=8,'zl'=4] {'zl','y'}, dimensions={0} | all-to-all | bytes 524288 | tf_op jit(solution)/shard_map/all_to_all | solution.py:353
  166.1 0.7 shard_map.76
  (2 shorter events, 0.1 us)
Async XLA Ops:
  0.6 50.6 %copy-start = (bf16[1,64,64,128]{3,2,1,0:T(8,128)(2,1)S(1)}, bf16[1,64,64,128]{3,2,1,0:T(8,128)(2,1)}, u32[]{:S(2)}) copy-start(bf16[1,64,64,128]{3,2,1,0:T(8,128)(2,1)} %param.6) | copy-start | bytes 3145732
  2.9 25.5 %all-to-all-start = ((bf16[32,32,128]{2,1,0:T(8,128)(2,1)}), bf16[32,32,128]{2,1,0:T(8,128)(2,1)S(1)}, u32[]{:S(2)}, u32[]{:S(2)}) async-start(bf16[32,32,128]{2,1,0:T(8,128)(2,1)} %get-tuple-element.18), calls=%async_computation | async-start | bytes 524288 | tf_op jit(solution)/shard_map/all_to_all | solution.py:353
  15.9 5.1 %collective-permute-start = (bf16[32,128]{1,0:T(8,128)(2,1)}, bf16[32,128]{1,0:T(8,128)(2,1)S(1)}, u32[]{:S(2)}, u32[]{:S(2)}) collective-permute-start(bf16[32,128]{1,0:T(8,128)(2,1)} %get-tuple-element.19), channel_id=1, source_target_pairs={{0,0},{1,1},{2,32},{3,33},{32,2},{33,3},{34,34},{35,35},{4,4},{5,5... | collective-permute-start | bytes 24584 | tf_op jit(solution)/shard_map/ppermute | solution.py:386
  17.2 5.9 %collective-permute-start.1 = (bf16[32,128]{1,0:T(8,128)(2,1)}, bf16[32,128]{1,0:T(8,128)(2,1)S(1)}, u32[]{:S(2)}, u32[]{:S(2)}) collective-permute-start(bf16[32,128]{1,0:T(8,128)(2,1)} %get-tuple-element.20), channel_id=1, source_target_pairs={{0,1},{1,0},{2,33},{3,32},{32,3},{33,2},{34,35},{35,34},{4,5},{5,4... | collective-permute-start | bytes 24584 | tf_op jit(solution)/shard_map/ppermute | solution.py:386
  28.4 22.8 %copy-start.2 = (s32[2,128]{1,0:T(2,128)S(1)}, s32[2,128]{1,0:T(2,128)}, u32[]{:S(2)}) copy-start(s32[2,128]{1,0:T(2,128)} %get-tuple-element.17.refs_0_) | copy-start | bytes 3076
  51.2 0.7 copy-start.1

commit v7 on v6

--- a/solution.py
+++ b/solution.py
@@ -86,11 +86,8 @@
 INNER = [(zh, core, j) for zh in range(2) for core in range(2) for j in range(2)]
 
 
-def spread_kernel(
-    x_hbm, coords_hbm, counts_hbm, e_hbm, out_ref, index_ref, energy_ref, *refs
-):
-    messages, (x_ref, coords_ref, counts_ref, sems) = refs[:2], refs[2:]
-    pairs = ((x_hbm, x_ref), (coords_hbm, coords_ref), (counts_hbm, counts_ref), (e_hbm, energy_ref))
+def spread_kernel(x_hbm, e_hbm, out_ref, even_ref, odd_ref, x_ref, e_ref, sems):
+    pairs = ((x_hbm, x_ref), (e_hbm, e_ref))
     copies = [pltpu.make_async_copy(a, b, sems.at[n]) for n, (a, b) in enumerate(pairs)]
     for copy in copies:
         copy.start()
@@ -102,12 +99,15 @@
             out_ref[c, j * VECS : (j + 1) * VECS] = value
     odd = lax.rem(lax.axis_index("zl"), 2)
     row = lax.broadcasted_iota(jnp.int32, (VECS, LANES), 0)
-    for k, message in enumerate(messages):
+    for k, message in enumerate((even_ref, odd_ref)):
         message[:VECS] = jnp.where(odd == k, x_ref[:, 0, :], x_ref[:, 1, :])
         terms = jnp.zeros((VECS, LANES), F32)
-        for n, term in enumerate(split3(jnp.where(odd == k, energy_ref[0:1], energy_ref[1:2]))):
+        for n, term in enumerate(split3(jnp.where(odd == k, e_ref[0:1], e_ref[1:2]))):
             terms = jnp.where(row == n, term.astype(F32), terms)
         message[VECS:] = terms.astype(BF16)
+
+
+def index_kernel(coords_ref, counts_ref, e_ref, index_ref, energy_ref):
     live = lax.broadcasted_iota(jnp.int32, (1, SLOTS), 1) < counts_ref[0, 0]
     for n, dead in ((0, ROW_DEAD), (1, COL_DEAD)):
         coords = coords_ref[n]
@@ -116,9 +116,14 @@
         if n == 0:
             piece = piece * 2 + ((coords >> 1) & 1)
         index_ref[n : n + 1] = jnp.where(live, piece * 2 + (coords & 1), dead)
-
-
-def regroup_kernel(in_ref, even_ref, odd_ref, out_ref, own_ref, owned_ref, energy_ref):
+    energy_ref[...] = e_ref[...]
+
+
+def regroup_kernel(
+    in_ref, even_ref, odd_ref, index_in, e_in, out_ref, own_ref, owned_ref, energy_ref, index_out, e_out
+):
+    index_out[...] = index_in[...]
+    e_out[...] = e_in[...]
     wide = 2 * VECS
     y, zl = lax.axis_index("y"), lax.axis_index("zl")
     own = in_ref[zl * 8 + y]
@@ -362,36 +367,33 @@
         pltpu.VMEM((ROW_DEAD + 1, VECS, LANES), F32),
         pltpu.VMEM((COL_DEAD + 1, VECS, LANES), F32),
     ]
-    spread, index, energies, *messages = call(
+    index_shape, energy_shape = shape(2, SLOTS, dtype=jnp.int32), shape(2, LANES, dtype=F32)
+    message = shape(2 * VECS, LANES)
+    spread, *messages = call(
         spread_kernel,
-        (
-            shape(NC, 2 * VECS, LANES),
-            shape(2, SLOTS, dtype=jnp.int32),
-            shape(2, LANES, dtype=F32),
-            shape(2 * VECS, LANES),
-            shape(2 * VECS, LANES),
-        ),
-        4,
+        (shape(NC, 2 * VECS, LANES), message, message),
+        2,
         [
             pltpu.VMEM((VECS, 2, LANES), BF16),
-            pltpu.VMEM((2, 1, SLOTS), jnp.int32),
-            pltpu.SMEM((1, 1), jnp.int32),
-            pltpu.SemaphoreType.DMA((4,)),
+            pltpu.VMEM((2, LANES), F32),
+            pltpu.SemaphoreType.DMA((2,)),
         ],
         first=pl.BlockSpec(memory_space=pl.ANY),
         limit=60,
-    )(vectors, tile_coords, tile_counts, energies)
-
+    )(vectors, energies)
     received = [
         lax.ppermute(message, ("core", "zl"), [owner_of(n, k) for n in range(8)])
         for k, message in enumerate(messages)
     ]
     slab = exchange(spread, COL)
-    grouped, own, owned, owned_energies = call(
+    index, energies = call(index_kernel, (index_shape, energy_shape), 3, scalars=(1,))(
+        tile_coords, tile_counts, energies
+    )
+    grouped, own, owned, owned_energies, index, energies = call(
         regroup_kernel,
-        (shape(NR, GROUP * VECS, LANES), piece, piece, shape(2, LANES, dtype=F32)),
-        3,
-    )(slab, *received)
+        (shape(NR, GROUP * VECS, LANES), piece, piece, energy_shape, index_shape, energy_shape),
+        5,
+    )(slab, *received, index, energies)
     fields = exchange(grouped, ROW)
     partial = call(
         functools.partial(tiles_kernel, True),

time: 169 us -> 167 us (0.988)
  waiting for transfers between devices: 7.47 us -> 5.45 us
    ppermute x2, waiting for transfers between devices: 2.24 us -> 0.22 us  [shards(): lax.ppermute(message, ('core', 'zl'), [owner_of(n, k) for n in range(8)])]
where the time goes in v7:
time: 167 us; the launch traced here: 164 us
  blocking collectives  128 us (77%)
  starting transfers between devices  18 us (11%)
  Pallas kernels  10.1 us (6%)
  waiting for transfers between devices  5.45 us (3%)
    all_to_all x7, blocking collectives, exchange(): return lax.all_to_all(value, axis, split_axis=0, concat_axis=0, tiled=True)  128 us
    all_to_all x1, starting transfers between devices, exchange(): return lax.all_to_all(value, axis, split_axis=0, concat_axis=0, tiled=True)  12.9 us
    all_to_all x1, waiting for transfers between devices, exchange(): return lax.all_to_all(value, axis, split_axis=0, concat_axis=0, tiled=True)  5.23 us
    ppermute x2, starting transfers between devices, shards(): lax.ppermute(message, ('core', 'zl'), [owner_of(n, k) for n in range(8)])  5.05 us
  transfers between devices with their start and end apart: 3, of which 2 were waited for; matrix products, arithmetic and copies ran while one was open for 0% of the time, Pallas kernels for 0%

profile of v7, /device:TPU:6, one launch (start us, length us, event | category | flops | bytes accessed | tf_op | source)
XLA Modules:
  0.0 164.4 jit_solution(14452214115500164686)
XLA Ops:
  0.6 0.0 copy-start
  0.6 1.6 shard_map.68
  2.2 12.9 %all-to-all-start = ((bf16[32,32,128]{2,1,0:T(8,128)(2,1)}), bf16[32,32,128]{2,1,0:T(8,128)(2,1)S(1)}, u32[]{:S(2)}, u32[]{:S(2)}) async-start(bf16[32,32,128]{2,1,0:T(8,128)(2,1)} %get-tuple-element.19), calls=%async_computation | async-start | bytes 524288 | tf_op jit(solution)/shard_map/all_to_all | solution.py:358
  15.2 1.4 collective-permute-start
  16.5 3.7 %collective-permute-start.1 = (bf16[32,128]{1,0:T(8,128)(2,1)}, bf16[32,128]{1,0:T(8,128)(2,1)S(1)}, u32[]{:S(2)}, u32[]{:S(2)}) collective-permute-start(bf16[32,128]{1,0:T(8,128)(2,1)} %get-tuple-element.21), channel_id=1, source_target_pairs={{0,1},{1,0},{2,33},{3,32},{32,3},{33,2},{34,35},{35,34},{4,5},{5,4... | collective-permute-start | bytes 24584 | tf_op jit(solution)/shard_map/ppermute | solution.py:385
  20.9 0.0 copy-start.1
  20.9 0.7 copy-done.1
  21.6 0.0 copy-start.2
  21.6 0.7 copy-done.2
  22.3 0.0 collective-permute-done.even_ref
  22.3 0.2 collective-permute-done.1.odd_ref
  22.5 5.2 %all-to-all-done.in_ref = bf16[32,32,128]{2,1,0:T(8,128)(2,1)S(1)} async-done(((bf16[32,32,128]{2,1,0:T(8,128)(2,1)}), bf16[32,32,128]{2,1,0:T(8,128)(2,1)S(1)}, u32[]{:S(2)}, u32[]{:S(2)}) %all-to-all-start) | async-done | bytes 262176 | tf_op jit(solution)/shard_map/all_to_all | solution.py:358
  27.8 22.8 %all_to_all.40.refs_1_ = bf16[16,96,128]{2,1,0:T(8,128)(2,1)S(1)} all-to-all(bf16[16,96,128]{2,1,0:T(8,128)(2,1)S(1)} %get-tuple-element.25), channel_id=1, replica_groups=mesh['zh'=2,'x'=4,'core'=2,'y'=8,'zl'=4] {'x','core','zh'}, dimensions={0} | all-to-all | bytes 786432 | tf_op jit(solution)/shard_map/all_to_all | solution.py:358
  50.5 0.0 copy-done
  50.5 3.1 %shard_map.71 = bf16[32,56,128]{2,1,0:T(8,128)(2,1)S(1)} custom-call(s32[2,128]{1,0:T(2,128)S(1)} %get-tuple-element.24.refs_0_, bf16[16,96,128]{2,1,0:T(8,128)(2,1)S(1)} %all_to_all.40.refs_1_, bf16[64,64,128]{2,1,0:T(8,128)(2,1)S(1)} %bitcast.1, bf16[2,16,128]{2,1,0:T(8,128)(2,1)S(1)} %get-tuple-element.26.refs_3_, ...), custom_call_target="tpu_custom_call" | custom-call | tf_op jit(solution)/shard_map/pallas_call | solution.py:398
  53.7 22.4 %all_to_all.41.in_ref = bf16[32,56,128]{2,1,0:T(8,128)(2,1)S(1)} all-to-all(bf16[32,56,128]{2,1,0:T(8,128)(2,1)S(1)} %shard_map.71), channel_id=1, replica_groups=mesh['zh'=2,'x'=4,'core'=2,'y'=8,'zl'=4] {'x','zh','zl'}, dimensions={0} | all-to-all | bytes 917504 | tf_op jit(solution)/shard_map/all_to_all | solution.py:358
  76.0 0.3 shard_map.72
  76.3 13.3 %all_to_all.42.in_ref = bf16[16,40,128]{2,1,0:T(8,128)(2,1)S(1)} all-to-all(bf16[16,40,128]{2,1,0:T(8,128)(2,1)S(1)} %get-tuple-element.28), channel_id=1, replica_groups=mesh['zh'=2,'x'=4,'core'=2,'y'=8,'zl'=4] {'y','core'}, dimensions={0} | all-to-all | bytes 327680 | tf_op jit(solution)/shard_map/all_to_all | solution.py:358
  89.7 1.5 shard_map.73
  91.2 11.8 %all_to_all.43.in_ref = bf16[16,32,128]{2,1,0:T(8,128)(2,1)S(1)} all-to-all(bf16[16,32,128]{2,1,0:T(8,128)(2,1)S(1)} %shard_map.73), channel_id=1, replica_groups=mesh['zh'=2,'x'=4,'core'=2,'y'=8,'zl'=4] {'y','core'}, dimensions={0} | all-to-all | bytes 262144 | tf_op jit(solution)/shard_map/all_to_all | solution.py:358
  103.0 0.1 shard_map.74
  103.0 20.1 %all_to_all.44.refs_1_ = bf16[32,48,128]{2,1,0:T(8,128)(2,1)S(1)} all-to-all(bf16[32,48,128]{2,1,0:T(8,128)(2,1)S(1)} %shard_map.74), channel_id=1, replica_groups=mesh['zh'=2,'x'=4,'core'=2,'y'=8,'zl'=4] {'x','zh','zl'}, dimensions={0} | all-to-all | bytes 786432 | tf_op jit(solution)/shard_map/all_to_all | solution.py:358
  123.1 2.7 %shard_map.75 = (bf16[16,96,128]{2,1,0:T(8,128)(2,1)S(1)}, bf16[2,16,128]{2,1,0:T(8,128)(2,1)S(1)}) custom-call(s32[2,128]{1,0:T(2,128)S(1)} %get-tuple-element.24.refs_0_, bf16[32,48,128]{2,1,0:T(8,128)(2,1)S(1)} %all_to_all.44.refs_1_, bf16[64,64,128]{2,1,0:T(8,128)(2,1)S(1)} %bitcast.2), custom_call_target="tpu_custom_call" | custom-call | tf_op jit(solution)/shard_map/pallas_call | solution.py:415
  125.8 17.6 %all_to_all.45.in_ref = bf16[16,96,128]{2,1,0:T(8,128)(2,1)S(1)} all-to-all(bf16[16,96,128]{2,1,0:T(8,128)(2,1)S(1)} %get-tuple-element.32), channel_id=1, replica_groups=mesh['zh'=2,'x'=4,'core'=2,'y'=8,'zl'=4] {'x','core','zh'}, dimensions={0} | all-to-all | bytes 786432 | tf_op jit(solution)/shard_map/all_to_all | solution.py:358
  143.4 20.3 %all_to_all.46.in_ref = bf16[32,32,128]{2,1,0:T(8,128)(2,1)S(1)} all-to-all(bf16[32,32,128]{2,1,0:T(8,128)(2,1)S(1)} %get-tuple-element.33), channel_id=1, replica_groups=mesh['zh'=2,'x'=4,'core'=2,'y'=8,'zl'=4] {'zl','y'}, dimensions={0} | all-to-all | bytes 524288 | tf_op jit(solution)/shard_map/all_to_all | solution.py:358
  163.7 0.7 shard_map.77
  (3 shorter events, 0.1 us)
Async XLA Ops:
  0.6 49.9 %copy-start = (bf16[1,64,64,128]{3,2,1,0:T(8,128)(2,1)S(1)}, bf16[1,64,64,128]{3,2,1,0:T(8,128)(2,1)}, u32[]{:S(2)}) copy-start(bf16[1,64,64,128]{3,2,1,0:T(8,128)(2,1)} %param.6) | copy-start | bytes 3145732
  2.2 25.5 %all-to-all-start = ((bf16[32,32,128]{2,1,0:T(8,128)(2,1)}), bf16[32,32,128]{2,1,0:T(8,128)(2,1)S(1)}, u32[]{:S(2)}, u32[]{:S(2)}) async-start(bf16[32,32,128]{2,1,0:T(8,128)(2,1)} %get-tuple-element.19), calls=%async_computation | async-start | bytes 524288 | tf_op jit(solution)/shard_map/all_to_all | solution.py:358
  15.2 7.1 %collective-permute-start = (bf16[32,128]{1,0:T(8,128)(2,1)}, bf16[32,128]{1,0:T(8,128)(2,1)S(1)}, u32[]{:S(2)}, u32[]{:S(2)}) collective-permute-start(bf16[32,128]{1,0:T(8,128)(2,1)} %get-tuple-element.20), channel_id=1, source_target_pairs={{0,0},{1,1},{2,32},{3,33},{32,2},{33,3},{34,34},{35,35},{4,4},{5,5... | collective-permute-start | bytes 24584 | tf_op jit(solution)/shard_map/ppermute | solution.py:385
  16.5 5.9 %collective-permute-start.1 = (bf16[32,128]{1,0:T(8,128)(2,1)}, bf16[32,128]{1,0:T(8,128)(2,1)S(1)}, u32[]{:S(2)}, u32[]{:S(2)}) collective-permute-start(bf16[32,128]{1,0:T(8,128)(2,1)} %get-tuple-element.21), channel_id=1, source_target_pairs={{0,1},{1,0},{2,33},{3,32},{32,3},{33,2},{34,35},{35,34},{4,5},{5,4... | collective-permute-start | bytes 24584 | tf_op jit(solution)/shard_map/ppermute | solution.py:385
  20.9 0.7 copy-start.1
  21.6 0.7 copy-start.2

commit v8 on v7

--- a/solution.py
+++ b/solution.py
@@ -19,10 +19,10 @@
 GROUP = 6
 PIECES = 32
 SLOTS = 128
-UNROLL = 16
+UNROLL = 32
 ROW_DEAD = NR * 8
 COL_DEAD = NR * 4
-ROW = ("x", "core", "zh")
+ROW = ("core", "x", "zh")
 COL = ("zl", "y")
 PIECE = ("x", "zh", "zl")
 OWNER = ("y", "core")
@@ -32,7 +32,7 @@
 
 
 def row_at(r):
-    return (r % 8) * 2 + r // 8
+    return (r % 2) * 8 + (r // 2 % 4) * 2 + r // 8
 
 
 def col_at(c):
@@ -79,7 +79,7 @@
 def locate(by_row, x, zh, core, j, slot):
     if by_row:
         place = slot * 2 + j if slot < 2 else 4 + j
-        return x * 4 + core * 2 + zh, slice(place * VECS, (place + 1) * VECS)
+        return core * 8 + x * 2 + zh, slice(place * VECS, (place + 1) * VECS)
     return piece_at(x, zh, core, j), slice(slot * VECS, (slot + 1) * VECS)
 
 
@@ -154,10 +154,12 @@
 
 def tiles_kernel(first, *refs):
     if first:
-        idx_ref, x_ref, w_ref, own_ref, e_ref, out_ref, *scratch = refs
+        index_ref, x_ref, w_ref, own_ref, e_ref, out_ref, *scratch = refs
     else:
-        idx_ref, x_ref, w_ref, out_ref, own_ref, *scratch = refs
-    field_row, field_col, acc_row, acc_col = scratch[:4]
+        index_ref, x_ref, w_ref, out_ref, own_ref, *scratch = refs
+    field_row, field_col, acc_row, acc_col, idx_ref, sem = scratch[:6]
+    fetch = pltpu.make_async_copy(index_ref, idx_ref, sem)
+    fetch.start()
     low_half = lane_index() < HALF
     zero = jnp.zeros((VECS, LANES), F32)
     half_mask = [low_half, jnp.logical_not(low_half)]
@@ -208,6 +210,7 @@
                 acc_col[cols[k]] += jnp.where(half_mask[k % 2], backward[part(k)], 0.0)
         return carry
 
+    fetch.wait()
     lax.fori_loop(0, SLOTS // 4 // UNROLL, block, 0)
 
     def folded(piece, slot):
@@ -224,7 +227,7 @@
                 out_ref[chunk, rows] = total.astype(BF16)
                 if first and slot == 2:
                     for n, term in enumerate(split3(total)):
-                        scratch[4][n, piece] = term
+                        scratch[6][n, piece] = term
         return carry
 
     if not first:
@@ -234,7 +237,7 @@
         return
 
     lax.fori_loop(0, 4, pack, 0)
-    terms = scratch[4]
+    terms = scratch[6]
     left = jnp.concatenate(
         [jnp.concatenate([terms[n, p] for p in range(PIECES)], axis=1) for n in range(3)], axis=0
     )
@@ -366,6 +369,8 @@
         pltpu.VMEM((COL_DEAD + 1, VECS, LANES), BF16),
         pltpu.VMEM((ROW_DEAD + 1, VECS, LANES), F32),
         pltpu.VMEM((COL_DEAD + 1, VECS, LANES), F32),
+        pltpu.SMEM((2, SLOTS), jnp.int32),
+        pltpu.SemaphoreType.DMA,
     ]
     index_shape, energy_shape = shape(2, SLOTS, dtype=jnp.int32), shape(2, LANES, dtype=F32)
     message = shape(2 * VECS, LANES)
@@ -400,7 +405,6 @@
         shape(PIECES, 3 * VECS + MESSAGE, LANES),
         5,
         scratch + [pltpu.VMEM((3, PIECES, VECS, LANES), BF16)],
-        scalars=(0,),
     )(index, fields, tiles, own, energies)
     by_owner, back = call(
         collect_owner_kernel,
@@ -417,7 +421,6 @@
         (shape(NR, GROUP * VECS, LANES), piece),
         3,
         scratch,
-        scalars=(0,),
     )(index, exchange(grouped, PIECE), tiles)
     by_block, back = call(
         collect_kernel, (shape(NC, 2 * VECS, LANES), shape(2, VECS, LANES, dtype=F32)), 1

time: 167 us -> 165 us (0.988)
  no operation moved by 1% of the time
where the time goes in v8:
time: 165 us; the launch traced here: 163 us
  blocking collectives  128 us (78%)
  starting transfers between devices  18 us (11%)
  Pallas kernels  9.1 us (6%)
  waiting for transfers between devices  5.45 us (3%)
    all_to_all x7, blocking collectives, exchange(): return lax.all_to_all(value, axis, split_axis=0, concat_axis=0, tiled=True)  128 us
    all_to_all x1, starting transfers between devices, exchange(): return lax.all_to_all(value, axis, split_axis=0, concat_axis=0, tiled=True)  12.9 us
    all_to_all x1, waiting for transfers between devices, exchange(): return lax.all_to_all(value, axis, split_axis=0, concat_axis=0, tiled=True)  5.23 us
    ppermute x2, starting transfers between devices, shards(): lax.ppermute(message, ('core', 'zl'), [owner_of(n, k) for n in range(8)])  5.05 us
  transfers between devices with their start and end apart: 3, of which 2 were waited for; matrix products, arithmetic and copies ran while one was open for 0% of the time, Pallas kernels for 0%

profile of v8, /device:TPU:6, one launch (start us, length us, event | category | flops | bytes accessed | tf_op | source)
XLA Modules:
  0.0 163.3 jit_solution(10746344400981135287)
XLA Ops:
  0.6 0.0 copy-start
  0.6 1.6 shard_map.68
  2.2 12.9 %all-to-all-start = ((bf16[32,32,128]{2,1,0:T(8,128)(2,1)}), bf16[32,32,128]{2,1,0:T(8,128)(2,1)S(1)}, u32[]{:S(2)}, u32[]{:S(2)}) async-start(bf16[32,32,128]{2,1,0:T(8,128)(2,1)} %get-tuple-element.19), calls=%async_computation | async-start | bytes 524288 | tf_op jit(solution)/shard_map/all_to_all | solution.py:361
  15.2 1.4 collective-permute-start
  16.5 3.7 %collective-permute-start.1 = (bf16[32,128]{1,0:T(8,128)(2,1)}, bf16[32,128]{1,0:T(8,128)(2,1)S(1)}, u32[]{:S(2)}, u32[]{:S(2)}) collective-permute-start(bf16[32,128]{1,0:T(8,128)(2,1)} %get-tuple-element.21), channel_id=1, source_target_pairs={{0,1},{1,0},{2,33},{3,32},{32,3},{33,2},{34,35},{35,34},{4,5},{5,4... | collective-permute-start | bytes 24584 | tf_op jit(solution)/shard_map/ppermute | solution.py:390
  20.9 0.0 copy-start.1
  20.9 0.7 copy-done.1
  21.6 0.0 copy-start.2
  21.6 0.7 copy-done.2
  22.3 0.0 collective-permute-done.even_ref
  22.3 0.2 collective-permute-done.1.odd_ref
  22.5 5.2 %all-to-all-done.in_ref = bf16[32,32,128]{2,1,0:T(8,128)(2,1)S(1)} async-done(((bf16[32,32,128]{2,1,0:T(8,128)(2,1)}), bf16[32,32,128]{2,1,0:T(8,128)(2,1)S(1)}, u32[]{:S(2)}, u32[]{:S(2)}) %all-to-all-start) | async-done | bytes 262176 | tf_op jit(solution)/shard_map/all_to_all | solution.py:361
  27.8 22.8 %all_to_all.40.refs_1_ = bf16[16,96,128]{2,1,0:T(8,128)(2,1)S(1)} all-to-all(bf16[16,96,128]{2,1,0:T(8,128)(2,1)S(1)} %get-tuple-element.25), channel_id=1, replica_groups=mesh['zh'=2,'x'=4,'core'=2,'y'=8,'zl'=4] {'core','x','zh'}, dimensions={0} | all-to-all | bytes 786432 | tf_op jit(solution)/shard_map/all_to_all | solution.py:361
  50.5 0.0 copy-done
  50.5 2.8 %shard_map.71 = bf16[32,56,128]{2,1,0:T(8,128)(2,1)S(1)} custom-call(s32[2,128]{1,0:T(2,128)S(1)} %get-tuple-element.24.refs_0_, bf16[16,96,128]{2,1,0:T(8,128)(2,1)S(1)} %all_to_all.40.refs_1_, bf16[64,64,128]{2,1,0:T(8,128)(2,1)S(1)} %bitcast.1, bf16[2,16,128]{2,1,0:T(8,128)(2,1)S(1)} %get-tuple-element.26.refs_3_, ...), custom_call_target="tpu_custom_call" | custom-call | tf_op jit(solution)/shard_map/pallas_call | solution.py:403
  53.3 21.9 %all_to_all.41.in_ref = bf16[32,56,128]{2,1,0:T(8,128)(2,1)S(1)} all-to-all(bf16[32,56,128]{2,1,0:T(8,128)(2,1)S(1)} %shard_map.71), channel_id=1, replica_groups=mesh['zh'=2,'x'=4,'core'=2,'y'=8,'zl'=4] {'x','zh','zl'}, dimensions={0} | all-to-all | bytes 917504 | tf_op jit(solution)/shard_map/all_to_all | solution.py:361
  75.2 0.3 shard_map.72
  75.5 13.4 %all_to_all.42.in_ref = bf16[16,40,128]{2,1,0:T(8,128)(2,1)S(1)} all-to-all(bf16[16,40,128]{2,1,0:T(8,128)(2,1)S(1)} %get-tuple-element.28), channel_id=1, replica_groups=mesh['zh'=2,'x'=4,'core'=2,'y'=8,'zl'=4] {'y','core'}, dimensions={0} | all-to-all | bytes 327680 | tf_op jit(solution)/shard_map/all_to_all | solution.py:361
  88.9 1.5 shard_map.73
  90.4 11.8 %all_to_all.43.in_ref = bf16[16,32,128]{2,1,0:T(8,128)(2,1)S(1)} all-to-all(bf16[16,32,128]{2,1,0:T(8,128)(2,1)S(1)} %shard_map.73), channel_id=1, replica_groups=mesh['zh'=2,'x'=4,'core'=2,'y'=8,'zl'=4] {'y','core'}, dimensions={0} | all-to-all | bytes 262144 | tf_op jit(solution)/shard_map/all_to_all | solution.py:361
  102.2 0.1 shard_map.74
  102.2 20.3 %all_to_all.44.refs_1_ = bf16[32,48,128]{2,1,0:T(8,128)(2,1)S(1)} all-to-all(bf16[32,48,128]{2,1,0:T(8,128)(2,1)S(1)} %shard_map.74), channel_id=1, replica_groups=mesh['zh'=2,'x'=4,'core'=2,'y'=8,'zl'=4] {'x','zh','zl'}, dimensions={0} | all-to-all | bytes 786432 | tf_op jit(solution)/shard_map/all_to_all | solution.py:361
  122.5 2.1 %shard_map.75 = (bf16[16,96,128]{2,1,0:T(8,128)(2,1)S(1)}, bf16[2,16,128]{2,1,0:T(8,128)(2,1)S(1)}) custom-call(s32[2,128]{1,0:T(2,128)S(1)} %get-tuple-element.24.refs_0_, bf16[32,48,128]{2,1,0:T(8,128)(2,1)S(1)} %all_to_all.44.refs_1_, bf16[64,64,128]{2,1,0:T(8,128)(2,1)S(1)} %bitcast.2), custom_call_target="tpu_custom_call" | custom-call | tf_op jit(solution)/shard_map/pallas_call | solution.py:419
  124.6 17.5 %all_to_all.45.in_ref = bf16[16,96,128]{2,1,0:T(8,128)(2,1)S(1)} all-to-all(bf16[16,96,128]{2,1,0:T(8,128)(2,1)S(1)} %get-tuple-element.32), channel_id=1, replica_groups=mesh['zh'=2,'x'=4,'core'=2,'y'=8,'zl'=4] {'core','x','zh'}, dimensions={0} | all-to-all | bytes 786432 | tf_op jit(solution)/shard_map/all_to_all | solution.py:361
  142.1 20.5 %all_to_all.46.in_ref = bf16[32,32,128]{2,1,0:T(8,128)(2,1)S(1)} all-to-all(bf16[32,32,128]{2,1,0:T(8,128)(2,1)S(1)} %get-tuple-element.33), channel_id=1, replica_groups=mesh['zh'=2,'x'=4,'core'=2,'y'=8,'zl'=4] {'zl','y'}, dimensions={0} | all-to-all | bytes 524288 | tf_op jit(solution)/shard_map/all_to_all | solution.py:361
  162.6 0.7 shard_map.77
  (3 shorter events, 0.1 us)
Async XLA Ops:
  0.6 49.9 %copy-start = (bf16[1,64,64,128]{3,2,1,0:T(8,128)(2,1)S(1)}, bf16[1,64,64,128]{3,2,1,0:T(8,128)(2,1)}, u32[]{:S(2)}) copy-start(bf16[1,64,64,128]{3,2,1,0:T(8,128)(2,1)} %param.6) | copy-start | bytes 3145732
  2.2 25.5 %all-to-all-start = ((bf16[32,32,128]{2,1,0:T(8,128)(2,1)}), bf16[32,32,128]{2,1,0:T(8,128)(2,1)S(1)}, u32[]{:S(2)}, u32[]{:S(2)}) async-start(bf16[32,32,128]{2,1,0:T(8,128)(2,1)} %get-tuple-element.19), calls=%async_computation | async-start | bytes 524288 | tf_op jit(solution)/shard_map/all_to_all | solution.py:361
  15.2 7.1 %collective-permute-start = (bf16[32,128]{1,0:T(8,128)(2,1)}, bf16[32,128]{1,0:T(8,128)(2,1)S(1)}, u32[]{:S(2)}, u32[]{:S(2)}) collective-permute-start(bf16[32,128]{1,0:T(8,128)(2,1)} %get-tuple-element.20), channel_id=1, source_target_pairs={{0,0},{1,1},{2,32},{3,33},{32,2},{33,3},{34,34},{35,35},{4,4},{5,5... | collective-permute-start | bytes 24584 | tf_op jit(solution)/shard_map/ppermute | solution.py:390
  16.5 5.9 %collective-permute-start.1 = (bf16[32,128]{1,0:T(8,128)(2,1)}, bf16[32,128]{1,0:T(8,128)(2,1)S(1)}, u32[]{:S(2)}, u32[]{:S(2)}) collective-permute-start(bf16[32,128]{1,0:T(8,128)(2,1)} %get-tuple-element.21), channel_id=1, source_target_pairs={{0,1},{1,0},{2,33},{3,32},{32,3},{33,2},{34,35},{35,34},{4,5},{5,4... | collective-permute-start | bytes 24584 | tf_op jit(solution)/shard_map/ppermute | solution.py:390
  20.9 0.7 copy-start.1
  21.6 0.7 copy-start.2

commit v9 on v8

--- a/solution.py
+++ b/solution.py
@@ -107,7 +107,16 @@
         message[VECS:] = terms.astype(BF16)
 
 
-def index_kernel(coords_ref, counts_ref, e_ref, index_ref, energy_ref):
+def index_kernel(coords_ref, counts_ref, e_ref, x_ref, index_ref, energy_ref, gram_ref, cross_ref):
+    gram = jnp.zeros((VECS, VECS), F32)
+    cross = jnp.zeros((VECS, VECS), F32)
+    for j in range(2):
+        own = x_ref[:, j, :]
+        gram = gram + lax.dot_general(own, own, NT_DIMS, preferred_element_type=F32)
+        for term in split3(own.astype(F32) * (0.5 * e_ref[j : j + 1, :])):
+            cross = cross + lax.dot_general(term, own, NT_DIMS, preferred_element_type=F32)
+    gram_ref[...] = widen(gram)
+    cross_ref[...] = widen(cross)
     live = lax.broadcasted_iota(jnp.int32, (1, SLOTS), 1) < counts_ref[0, 0]
     for n, dead in ((0, ROW_DEAD), (1, COL_DEAD)):
         coords = coords_ref[n]
@@ -120,7 +129,7 @@
 
 
 def regroup_kernel(
-    in_ref, even_ref, odd_ref, index_in, e_in, out_ref, own_ref, owned_ref, energy_ref, index_out, e_out
+    in_ref, even_ref, odd_ref, index_in, e_in, out_ref, owned_ref, energy_ref, index_out, e_out
 ):
     index_out[...] = index_in[...]
     e_out[...] = e_in[...]
@@ -129,7 +138,6 @@
     own = in_ref[zl * 8 + y]
     odd = lax.rem(zl, 2)
     for j in range(2):
-        own_ref[j] = own[j * VECS : (j + 1) * VECS]
         message = jnp.where(odd == j, even_ref[...], odd_ref[...])
         owned_ref[j] = message[:VECS]
         terms = message[VECS:].astype(F32)
@@ -154,7 +162,7 @@
 
 def tiles_kernel(first, *refs):
     if first:
-        index_ref, x_ref, w_ref, own_ref, e_ref, out_ref, *scratch = refs
+        index_ref, x_ref, w_ref, gram_ref, cross_ref, out_ref, *scratch = refs
     else:
         index_ref, x_ref, w_ref, out_ref, own_ref, *scratch = refs
     field_row, field_col, acc_row, acc_col, idx_ref, sem = scratch[:6]
@@ -250,13 +258,7 @@
         left, jnp.concatenate(pieces, axis=1), NT_DIMS, preferred_element_type=F32
     )
     cross = crosses[:VECS] + crosses[VECS : 2 * VECS] + crosses[2 * VECS :]
-    gram = jnp.zeros((VECS, VECS), F32)
-    for j in range(2):
-        own = own_ref[j]
-        gram = gram + lax.dot_general(own, own, NT_DIMS, preferred_element_type=F32)
-        for term in split3(own.astype(F32) * (0.5 * e_ref[j : j + 1, :])):
-            cross = cross + lax.dot_general(term, own, NT_DIMS, preferred_element_type=F32)
-    message = message_of(widen(gram), widen(cross))
+    message = message_of(gram_ref[...], cross_ref[...] + widen(cross))
     for p in range(PIECES):
         out_ref[p, 3 * VECS :] = message
 
@@ -319,17 +321,19 @@
     wide = jnp.concatenate([cross, jnp.zeros((LANES - VECS, LANES), F32)], axis=0)
     cross = cross + jnp.transpose(wide)[:VECS]
     state = jnp.concatenate([gram, cross], axis=0)
-    lane = lax.broadcasted_iota(jnp.int32, (2 * VECS, LANES), 1)
+    columns = [jnp.broadcast_to(state[:, p : p + 1], (2 * VECS, LANES)) for p in range(VECS)]
     for p in range(VECS):
-        column = state[:, p : p + 1] * (1.0 / state[p : p + 1, p : p + 1])
-        state = jnp.where(lane == p, column, state - column * state[p : p + 1])
-    mix = state[VECS:]
+        scaled = columns[p] * (1.0 / columns[p][p : p + 1])
+        columns = [
+            scaled if q == p else column - scaled * column[p : p + 1]
+            for q, column in enumerate(columns)
+        ]
     for s in range(2):
         v = owned_ref[s].astype(F32)
         product = sum_over(in_ref, s * VECS, VECS) + back_ref[s] + e_ref[s : s + 1, :] * v
         shifted = jnp.zeros((VECS, LANES), F32)
         for k in range(VECS):
-            shifted = shifted + mix[:, k : k + 1] * v[k : k + 1, :]
+            shifted = shifted + columns[k][VECS:] * v[k : k + 1, :]
         value = (product - shifted).astype(BF16)
         for n in range(2 * 8):
             out_ref[n, s * VECS : (s + 1) * VECS] = value
@@ -391,12 +395,13 @@
         for k, message in enumerate(messages)
     ]
     slab = exchange(spread, COL)
-    index, energies = call(index_kernel, (index_shape, energy_shape), 3, scalars=(1,))(
-        tile_coords, tile_counts, energies
-    )
-    grouped, own, owned, owned_energies, index, energies = call(
+    sums = shape(VECS, LANES, dtype=F32)
+    index, energies, gram, cross = call(
+        index_kernel, (index_shape, energy_shape, sums, sums), 4, scalars=(1,)
+    )(tile_coords, tile_counts, energies, vectors)
+    grouped, owned, owned_energies, index, energies = call(
         regroup_kernel,
-        (shape(NR, GROUP * VECS, LANES), piece, piece, energy_shape, index_shape, energy_shape),
+        (shape(NR, GROUP * VECS, LANES), piece, energy_shape, index_shape, energy_shape),
         5,
     )(slab, *received, index, energies)
     fields = exchange(grouped, ROW)
@@ -405,7 +410,7 @@
         shape(PIECES, 3 * VECS + MESSAGE, LANES),
         5,
         scratch + [pltpu.VMEM((3, PIECES, VECS, LANES), BF16)],
-    )(index, fields, tiles, own, energies)
+    )(index, fields, tiles, gram, cross)
     by_owner, back = call(
         collect_owner_kernel,
         (shape(NR, 2 * VECS + MESSAGE, LANES), shape(2, VECS, LANES, dtype=F32)),

time: 165 us -> 165 us (level)
  transfers between devices with their start and end apart: 3 -> 3, of which waited for: 2 -> 1; matrix products, arithmetic and copies ran while one was open for 0% -> 0% of each run, Pallas kernels for 0% -> 0%
where the time goes in v9:
time: 165 us; the launch traced here: 163 us
  blocking collectives  129 us (78%)
  starting transfers between devices  18 us (11%)
  Pallas kernels  8.58 us (5%)
  waiting for transfers between devices  4.6 us (3%)
  local copies, waits for them, and re-layouts  2.05 us (1%)
    all_to_all x7, blocking collectives, exchange(): return lax.all_to_all(value, axis, split_axis=0, concat_axis=0, tiled=True)  129 us
    all_to_all x1, starting transfers between devices, exchange(): return lax.all_to_all(value, axis, split_axis=0, concat_axis=0, tiled=True)  12.9 us
    ppermute x2, starting transfers between devices, shards(): lax.ppermute(message, ('core', 'zl'), [owner_of(n, k) for n in range(8)])  5.05 us
    all_to_all x1, waiting for transfers between devices, exchange(): return lax.all_to_all(value, axis, split_axis=0, concat_axis=0, tiled=True)  4.57 us
  transfers between devices with their start and end apart: 3, of which 1 were waited for; matrix products, arithmetic and copies ran while one was open for 0% of the time, Pallas kernels for 0%

profile of v9, /device:TPU:6, one launch (start us, length us, event | category | flops | bytes accessed | tf_op | source)
XLA Modules:
  0.0 163.4 jit_solution(10634817418373709863)
XLA Ops:
  0.6 0.0 copy-start
  0.6 1.6 shard_map.68
  2.2 12.9 %all-to-all-start = ((bf16[32,32,128]{2,1,0:T(8,128)(2,1)}), bf16[32,32,128]{2,1,0:T(8,128)(2,1)S(1)}, u32[]{:S(2)}, u32[]{:S(2)}) async-start(bf16[32,32,128]{2,1,0:T(8,128)(2,1)} %get-tuple-element.20), calls=%async_computation | async-start | bytes 524288 | tf_op jit(solution)/shard_map/all_to_all | solution.py:365
  15.2 1.4 collective-permute-start
  16.5 3.7 %collective-permute-start.1 = (bf16[32,128]{1,0:T(8,128)(2,1)}, bf16[32,128]{1,0:T(8,128)(2,1)S(1)}, u32[]{:S(2)}, u32[]{:S(2)}) collective-permute-start(bf16[32,128]{1,0:T(8,128)(2,1)} %get-tuple-element.22), channel_id=1, source_target_pairs={{0,1},{1,0},{2,33},{3,32},{32,3},{33,2},{34,35},{35,34},{4,5},{5,4... | collective-permute-start | bytes 24584 | tf_op jit(solution)/shard_map/ppermute | solution.py:394
  20.9 0.0 copy-start.1
  20.9 0.7 copy-done.1
  21.6 0.0 copy-start.2
  21.6 0.7 copy-done.2
  22.3 0.0 copy-start.3
  22.3 0.7 copy-done.3
  22.9 0.2 shard_map.69
  23.1 0.0 collective-permute-done.even_ref
  23.1 0.0 collective-permute-done.1.odd_ref
  23.1 4.6 %all-to-all-done.in_ref = bf16[32,32,128]{2,1,0:T(8,128)(2,1)S(1)} async-done(((bf16[32,32,128]{2,1,0:T(8,128)(2,1)}), bf16[32,32,128]{2,1,0:T(8,128)(2,1)S(1)}, u32[]{:S(2)}, u32[]{:S(2)}) %all-to-all-start) | async-done | bytes 262176 | tf_op jit(solution)/shard_map/all_to_all | solution.py:365
  27.7 22.8 %all_to_all.40.refs_1_ = bf16[16,96,128]{2,1,0:T(8,128)(2,1)S(1)} all-to-all(bf16[16,96,128]{2,1,0:T(8,128)(2,1)S(1)} %get-tuple-element.26), channel_id=1, replica_groups=mesh['zh'=2,'x'=4,'core'=2,'y'=8,'zl'=4] {'core','x','zh'}, dimensions={0} | all-to-all | bytes 786432 | tf_op jit(solution)/shard_map/all_to_all | solution.py:365
  50.5 0.0 copy-done
  50.5 2.9 %shard_map.71 = bf16[32,56,128]{2,1,0:T(8,128)(2,1)S(1)} custom-call(s32[2,128]{1,0:T(2,128)S(1)} %get-tuple-element.25.refs_0_, bf16[16,96,128]{2,1,0:T(8,128)(2,1)S(1)} %all_to_all.40.refs_1_, bf16[64,64,128]{2,1,0:T(8,128)(2,1)S(1)} %bitcast.1, f32[16,128]{1,0:T(8,128)S(1)} %get-tuple-element.27.refs_3_, f32[16,128]{1,0:T(8,128)S(1)} %get-tuple-element.28.refs_4_), custom_call_target="tpu_custom_call" | custom-call | tf_op jit(solution)/shard_map/pallas_call | solution.py:408
  53.4 21.7 %all_to_all.41.in_ref = bf16[32,56,128]{2,1,0:T(8,128)(2,1)S(1)} all-to-all(bf16[32,56,128]{2,1,0:T(8,128)(2,1)S(1)} %shard_map.71), channel_id=1, replica_groups=mesh['zh'=2,'x'=4,'core'=2,'y'=8,'zl'=4] {'x','zh','zl'}, dimensions={0} | all-to-all | bytes 917504 | tf_op jit(solution)/shard_map/all_to_all | solution.py:365
  75.1 0.3 shard_map.72
  75.4 14.4 %all_to_all.42.in_ref = bf16[16,40,128]{2,1,0:T(8,128)(2,1)S(1)} all-to-all(bf16[16,40,128]{2,1,0:T(8,128)(2,1)S(1)} %get-tuple-element.29), channel_id=1, replica_groups=mesh['zh'=2,'x'=4,'core'=2,'y'=8,'zl'=4] {'y','core'}, dimensions={0} | all-to-all | bytes 327680 | tf_op jit(solution)/shard_map/all_to_all | solution.py:365
  89.9 0.6 shard_map.73
  90.5 11.8 %all_to_all.43.in_ref = bf16[16,32,128]{2,1,0:T(8,128)(2,1)S(1)} all-to-all(bf16[16,32,128]{2,1,0:T(8,128)(2,1)S(1)} %shard_map.73), channel_id=1, replica_groups=mesh['zh'=2,'x'=4,'core'=2,'y'=8,'zl'=4] {'y','core'}, dimensions={0} | all-to-all | bytes 262144 | tf_op jit(solution)/shard_map/all_to_all | solution.py:365
  102.2 0.1 shard_map.74
  102.3 20.3 %all_to_all.44.refs_1_ = bf16[32,48,128]{2,1,0:T(8,128)(2,1)S(1)} all-to-all(bf16[32,48,128]{2,1,0:T(8,128)(2,1)S(1)} %shard_map.74), channel_id=1, replica_groups=mesh['zh'=2,'x'=4,'core'=2,'y'=8,'zl'=4] {'x','zh','zl'}, dimensions={0} | all-to-all | bytes 786432 | tf_op jit(solution)/shard_map/all_to_all | solution.py:365
  122.6 2.2 %shard_map.75 = (bf16[16,96,128]{2,1,0:T(8,128)(2,1)S(1)}, bf16[2,16,128]{2,1,0:T(8,128)(2,1)S(1)}) custom-call(s32[2,128]{1,0:T(2,128)S(1)} %get-tuple-element.25.refs_0_, bf16[32,48,128]{2,1,0:T(8,128)(2,1)S(1)} %all_to_all.44.refs_1_, bf16[64,64,128]{2,1,0:T(8,128)(2,1)S(1)} %bitcast.2), custom_call_target="tpu_custom_call" | custom-call | tf_op jit(solution)/shard_map/pallas_call | solution.py:424
  124.8 17.5 %all_to_all.45.in_ref = bf16[16,96,128]{2,1,0:T(8,128)(2,1)S(1)} all-to-all(bf16[16,96,128]{2,1,0:T(8,128)(2,1)S(1)} %get-tuple-element.33), channel_id=1, replica_groups=mesh['zh'=2,'x'=4,'core'=2,'y'=8,'zl'=4] {'core','x','zh'}, dimensions={0} | all-to-all | bytes 786432 | tf_op jit(solution)/shard_map/all_to_all | solution.py:365
  142.3 20.4 %all_to_all.46.in_ref = bf16[32,32,128]{2,1,0:T(8,128)(2,1)S(1)} all-to-all(bf16[32,32,128]{2,1,0:T(8,128)(2,1)S(1)} %get-tuple-element.34), channel_id=1, replica_groups=mesh['zh'=2,'x'=4,'core'=2,'y'=8,'zl'=4] {'zl','y'}, dimensions={0} | all-to-all | bytes 524288 | tf_op jit(solution)/shard_map/all_to_all | solution.py:365
  162.7 0.7 shard_map.77
  (2 shorter events, 0.1 us)
Async XLA Ops:
  0.6 49.9 %copy-start = (bf16[1,64,64,128]{3,2,1,0:T(8,128)(2,1)S(1)}, bf16[1,64,64,128]{3,2,1,0:T(8,128)(2,1)}, u32[]{:S(2)}) copy-start(bf16[1,64,64,128]{3,2,1,0:T(8,128)(2,1)} %param.6) | copy-start | bytes 3145732
  2.2 25.5 %all-to-all-start = ((bf16[32,32,128]{2,1,0:T(8,128)(2,1)}), bf16[32,32,128]{2,1,0:T(8,128)(2,1)S(1)}, u32[]{:S(2)}, u32[]{:S(2)}) async-start(bf16[32,32,128]{2,1,0:T(8,128)(2,1)} %get-tuple-element.20), calls=%async_computation | async-start | bytes 524288 | tf_op jit(solution)/shard_map/all_to_all | solution.py:365
  15.2 7.9 %collective-permute-start = (bf16[32,128]{1,0:T(8,128)(2,1)}, bf16[32,128]{1,0:T(8,128)(2,1)S(1)}, u32[]{:S(2)}, u32[]{:S(2)}) collective-permute-start(bf16[32,128]{1,0:T(8,128)(2,1)} %get-tuple-element.21), channel_id=1, source_target_pairs={{0,0},{1,1},{2,32},{3,33},{32,2},{33,3},{34,34},{35,35},{4,4},{5,5... | collective-permute-start | bytes 24584 | tf_op jit(solution)/shard_map/ppermute | solution.py:394
  16.5 6.6 %collective-permute-start.1 = (bf16[32,128]{1,0:T(8,128)(2,1)}, bf16[32,128]{1,0:T(8,128)(2,1)S(1)}, u32[]{:S(2)}, u32[]{:S(2)}) collective-permute-start(bf16[32,128]{1,0:T(8,128)(2,1)} %get-tuple-element.22), channel_id=1, source_target_pairs={{0,1},{1,0},{2,33},{3,32},{32,3},{33,2},{34,35},{35,34},{4,5},{5,4... | collective-permute-start | bytes 24584 | tf_op jit(solution)/shard_map/ppermute | solution.py:394
  20.9 0.7 copy-start.1
  21.6 0.7 copy-start.2
  22.3 0.7 copy-start.3

commit v10 on v9

--- a/solution.py
+++ b/solution.py
@@ -149,14 +149,15 @@
         out_ref[at, 2 * wide :] = own
 
 
-def regroup_back_kernel(in_ref, out_ref):
+def regroup_back_kernel(in_ref, other_ref, out_ref):
     y, core = lax.axis_index("y"), lax.axis_index("core")
     for zl in range(4):
-        column = in_ref[y * 2 + zl // 2, (zl % 2) * VECS : (zl % 2 + 1) * VECS]
+        rows = slice((zl % 2) * VECS, (zl % 2 + 1) * VECS)
+        column = jnp.where(core == zl // 2, in_ref[y, rows], other_ref[rows])
         for block in range(8):
             zh, x = block // 4, block % 4
             at = (x * 2 + zh) * 4 + zl
-            out_ref[at, : 2 * VECS] = in_ref[block * 2 + core]
+            out_ref[at, : 2 * VECS] = in_ref[block]
             out_ref[at, 2 * VECS :] = column
 
 
@@ -316,7 +317,7 @@
         out_ref[n, wide:] = message
 
 
-def solve_kernel(in_ref, back_ref, owned_ref, e_ref, out_ref):
+def solve_kernel(in_ref, back_ref, owned_ref, e_ref, out_ref, sent_ref):
     gram, cross = read_message(sum_over(in_ref, 2 * VECS, MESSAGE))
     wide = jnp.concatenate([cross, jnp.zeros((LANES - VECS, LANES), F32)], axis=0)
     cross = cross + jnp.transpose(wide)[:VECS]
@@ -335,7 +336,8 @@
         for k in range(VECS):
             shifted = shifted + columns[k][VECS:] * v[k : k + 1, :]
         value = (product - shifted).astype(BF16)
-        for n in range(2 * 8):
+        sent_ref[s * VECS : (s + 1) * VECS] = value
+        for n in range(8):
             out_ref[n, s * VECS : (s + 1) * VECS] = value
 
 
@@ -416,11 +418,14 @@
         (shape(NR, 2 * VECS + MESSAGE, LANES), shape(2, VECS, LANES, dtype=F32)),
         1,
     )(exchange(partial, PIECE))
-    residual = call(solve_kernel, shape(NR, 2 * VECS, LANES), 4)(
+    residual, sent = call(solve_kernel, (shape(8, 2 * VECS, LANES), message), 4)(
         exchange(by_owner, OWNER), back, owned, owned_energies
     )
 
-    grouped = call(regroup_back_kernel, shape(PIECES, 3 * VECS, LANES), 1)(exchange(residual, OWNER))
+    other = lax.ppermute(sent, "core", [(0, 1), (1, 0)])
+    grouped = call(regroup_back_kernel, shape(PIECES, 3 * VECS, LANES), 2)(
+        exchange(residual, "y"), other
+    )
     partial, own = call(
         functools.partial(tiles_kernel, False),
         (shape(NR, GROUP * VECS, LANES), piece),

time: 165 us -> 166 us (level)
  blocking collectives: 129 us -> 116 us
  waiting for transfers between devices: 4.6 us -> 10.7 us
  starting transfers between devices: 18 us -> 24 us
    all_to_all x7 -> x6, blocking collectives: 129 us -> 116 us  [exchange(): return lax.all_to_all(value, axis, split_axis=0, concat_axis=0, tiled=True)]
    all_to_all x1 -> x2, waiting for transfers between devices: 4.57 us -> 9.87 us  [exchange(): return lax.all_to_all(value, axis, split_axis=0, concat_axis=0, tiled=True)]
    all_to_all x1 -> x2, starting transfers between devices: 12.9 us -> 16.3 us  [exchange(): return lax.all_to_all(value, axis, split_axis=0, concat_axis=0, tiled=True)]
    ppermute x0 -> x1, starting transfers between devices: none -> 2.71 us  [shards(): other = lax.ppermute(sent, 'core', [(0, 1), (1, 0)])]
  transfers between devices with their start and end apart: 3 -> 5, of which waited for: 1 -> 3; matrix products, arithmetic and copies ran while one was open for 0% -> 0% of each run, Pallas kernels for 0% -> 0%
where the time goes in v10:
time: 166 us; the launch traced here: 163 us
  blocking collectives  116 us (70%)
  starting transfers between devices  24 us (14%)
  waiting for transfers between devices  10.7 us (6%)
  Pallas kernels  9.15 us (6%)
  local copies, waits for them, and re-layouts  2.05 us (1%)
    all_to_all x6, blocking collectives, exchange(): return lax.all_to_all(value, axis, split_axis=0, concat_axis=0, tiled=True)  116 us
    all_to_all x2, starting transfers between devices, exchange(): return lax.all_to_all(value, axis, split_axis=0, concat_axis=0, tiled=True)  16.3 us
    all_to_all x2, waiting for transfers between devices, exchange(): return lax.all_to_all(value, axis, split_axis=0, concat_axis=0, tiled=True)  9.87 us
    ppermute x2, starting transfers between devices, shards(): lax.ppermute(message, ('core', 'zl'), [owner_of(n, k) for n in range(8)])  5.05 us
  transfers between devices with their start and end apart: 5, of which 3 were waited for; matrix products, arithmetic and copies ran while one was open for 0% of the time, Pallas kernels for 0%

profile of v10, /device:TPU:6, one launch (start us, length us, event | category | flops | bytes accessed | tf_op | source)
XLA Modules:
  0.0 163.2 jit_solution(5123310692578037925)
XLA Ops:
  0.6 0.0 copy-start
  0.6 1.6 shard_map.68
  2.2 12.9 %all-to-all-start = ((bf16[32,32,128]{2,1,0:T(8,128)(2,1)}), bf16[32,32,128]{2,1,0:T(8,128)(2,1)S(1)}, u32[]{:S(2)}, u32[]{:S(2)}) async-start(bf16[32,32,128]{2,1,0:T(8,128)(2,1)} %get-tuple-element.22), calls=%async_computation | async-start | bytes 524288 | tf_op jit(solution)/shard_map/all_to_all | solution.py:367
  15.2 1.4 collective-permute-start
  16.5 3.7 %collective-permute-start.1 = (bf16[32,128]{1,0:T(8,128)(2,1)}, bf16[32,128]{1,0:T(8,128)(2,1)S(1)}, u32[]{:S(2)}, u32[]{:S(2)}) collective-permute-start(bf16[32,128]{1,0:T(8,128)(2,1)} %get-tuple-element.24), channel_id=1, source_target_pairs={{0,1},{1,0},{2,33},{3,32},{32,3},{33,2},{34,35},{35,34},{4,5},{5,4... | collective-permute-start | bytes 24584 | tf_op jit(solution)/shard_map/ppermute | solution.py:396
  20.9 0.0 copy-start.1
  20.9 0.7 copy-done.1
  21.6 0.0 copy-start.2
  21.6 0.7 copy-done.2
  22.2 0.0 copy-start.3
  22.2 0.7 copy-done.3
  22.9 0.2 shard_map.69
  23.1 0.0 collective-permute-done.even_ref
  23.1 0.0 collective-permute-done.1.odd_ref
  23.1 4.6 %all-to-all-done.in_ref = bf16[32,32,128]{2,1,0:T(8,128)(2,1)S(1)} async-done(((bf16[32,32,128]{2,1,0:T(8,128)(2,1)}), bf16[32,32,128]{2,1,0:T(8,128)(2,1)S(1)}, u32[]{:S(2)}, u32[]{:S(2)}) %all-to-all-start) | async-done | bytes 262176 | tf_op jit(solution)/shard_map/all_to_all | solution.py:367
  27.7 22.8 %all_to_all.40.refs_1_ = bf16[16,96,128]{2,1,0:T(8,128)(2,1)S(1)} all-to-all(bf16[16,96,128]{2,1,0:T(8,128)(2,1)S(1)} %get-tuple-element.28), channel_id=1, replica_groups=mesh['zh'=2,'x'=4,'core'=2,'y'=8,'zl'=4] {'core','x','zh'}, dimensions={0} | all-to-all | bytes 786432 | tf_op jit(solution)/shard_map/all_to_all | solution.py:367
  50.5 0.0 copy-done
  50.5 2.9 %shard_map.71 = bf16[32,56,128]{2,1,0:T(8,128)(2,1)S(1)} custom-call(s32[2,128]{1,0:T(2,128)S(1)} %get-tuple-element.27.refs_0_, bf16[16,96,128]{2,1,0:T(8,128)(2,1)S(1)} %all_to_all.40.refs_1_, bf16[64,64,128]{2,1,0:T(8,128)(2,1)S(1)} %bitcast.1, f32[16,128]{1,0:T(8,128)S(1)} %get-tuple-element.29.refs_3_, f32[16,128]{1,0:T(8,128)S(1)} %get-tuple-element.30.refs_4_), custom_call_target="tpu_custom_call" | custom-call | tf_op jit(solution)/shard_map/pallas_call | solution.py:410
  53.4 21.8 %all_to_all.41.in_ref = bf16[32,56,128]{2,1,0:T(8,128)(2,1)S(1)} all-to-all(bf16[32,56,128]{2,1,0:T(8,128)(2,1)S(1)} %shard_map.71), channel_id=1, replica_groups=mesh['zh'=2,'x'=4,'core'=2,'y'=8,'zl'=4] {'x','zh','zl'}, dimensions={0} | all-to-all | bytes 917504 | tf_op jit(solution)/shard_map/all_to_all | solution.py:367
  75.2 0.3 shard_map.72
  75.6 14.3 %all_to_all.42.in_ref = bf16[16,40,128]{2,1,0:T(8,128)(2,1)S(1)} all-to-all(bf16[16,40,128]{2,1,0:T(8,128)(2,1)S(1)} %get-tuple-element.31), channel_id=1, replica_groups=mesh['zh'=2,'x'=4,'core'=2,'y'=8,'zl'=4] {'y','core'}, dimensions={0} | all-to-all | bytes 327680 | tf_op jit(solution)/shard_map/all_to_all | solution.py:367
  89.8 1.2 shard_map.73
  91.0 3.3 %all-to-all-start.4 = ((bf16[8,32,128]{2,1,0:T(8,128)(2,1)}), bf16[8,32,128]{2,1,0:T(8,128)(2,1)S(1)}, u32[]{:S(2)}, u32[]{:S(2)}) async-start(bf16[8,32,128]{2,1,0:T(8,128)(2,1)} %get-tuple-element.35), calls=%async_computation.4 | async-start | bytes 131072 | tf_op jit(solution)/shard_map/all_to_all | solution.py:367
  94.4 2.7 %collective-permute-start.2 = (bf16[32,128]{1,0:T(8,128)(2,1)S(1)}, bf16[32,128]{1,0:T(8,128)(2,1)S(1)}, u32[]{:S(2)}, u32[]{:S(2)}) collective-permute-start(bf16[32,128]{1,0:T(8,128)(2,1)S(1)} %get-tuple-element.36), channel_id=1, source_target_pairs={{0,32},{32,0},{1,33},{33,1},{2,34},{34,2},{3,35},{35,3},{4,36},{36... | collective-permute-start | bytes 24584 | tf_op jit(solution)/shard_map/ppermute | solution.py:425
  97.1 0.8 collective-permute-done.2.other_ref
  97.9 5.3 %all-to-all-done.4.in_ref = bf16[8,32,128]{2,1,0:T(8,128)(2,1)S(1)} async-done(((bf16[8,32,128]{2,1,0:T(8,128)(2,1)}), bf16[8,32,128]{2,1,0:T(8,128)(2,1)S(1)}, u32[]{:S(2)}, u32[]{:S(2)}) %all-to-all-start.4) | async-done | bytes 65568 | tf_op jit(solution)/shard_map/all_to_all | solution.py:367
  103.2 0.1 shard_map.74
  103.3 19.5 %all_to_all.43.refs_1_ = bf16[32,48,128]{2,1,0:T(8,128)(2,1)S(1)} all-to-all(bf16[32,48,128]{2,1,0:T(8,128)(2,1)S(1)} %shard_map.74), channel_id=1, replica_groups=mesh['zh'=2,'x'=4,'core'=2,'y'=8,'zl'=4] {'x','zh','zl'}, dimensions={0} | all-to-all | bytes 786432 | tf_op jit(solution)/shard_map/all_to_all | solution.py:367
  122.8 2.2 %shard_map.75 = (bf16[16,96,128]{2,1,0:T(8,128)(2,1)S(1)}, bf16[2,16,128]{2,1,0:T(8,128)(2,1)S(1)}) custom-call(s32[2,128]{1,0:T(2,128)S(1)} %get-tuple-element.27.refs_0_, bf16[32,48,128]{2,1,0:T(8,128)(2,1)S(1)} %all_to_all.43.refs_1_, bf16[64,64,128]{2,1,0:T(8,128)(2,1)S(1)} %bitcast.2), custom_call_target="tpu_custom_call" | custom-call | tf_op jit(solution)/shard_map/pallas_call | solution.py:429
  125.0 17.1 %all_to_all.44.in_ref = bf16[16,96,128]{2,1,0:T(8,128)(2,1)S(1)} all-to-all(bf16[16,96,128]{2,1,0:T(8,128)(2,1)S(1)} %get-tuple-element.37), channel_id=1, replica_groups=mesh['zh'=2,'x'=4,'core'=2,'y'=8,'zl'=4] {'core','x','zh'}, dimensions={0} | all-to-all | bytes 786432 | tf_op jit(solution)/shard_map/all_to_all | solution.py:367
  142.1 20.4 %all_to_all.45.in_ref = bf16[32,32,128]{2,1,0:T(8,128)(2,1)S(1)} all-to-all(bf16[32,32,128]{2,1,0:T(8,128)(2,1)S(1)} %get-tuple-element.38), channel_id=1, replica_groups=mesh['zh'=2,'x'=4,'core'=2,'y'=8,'zl'=4] {'zl','y'}, dimensions={0} | all-to-all | bytes 524288 | tf_op jit(solution)/shard_map/all_to_all | solution.py:367
  162.6 0.7 shard_map.77
  (2 shorter events, 0.1 us)
Async XLA Ops:
  0.6 49.9 %copy-start = (bf16[1,64,64,128]{3,2,1,0:T(8,128)(2,1)S(1)}, bf16[1,64,64,128]{3,2,1,0:T(8,128)(2,1)}, u32[]{:S(2)}) copy-start(bf16[1,64,64,128]{3,2,1,0:T(8,128)(2,1)} %param.6) | copy-start | bytes 3145732
  2.2 25.5 %all-to-all-start = ((bf16[32,32,128]{2,1,0:T(8,128)(2,1)}), bf16[32,32,128]{2,1,0:T(8,128)(2,1)S(1)}, u32[]{:S(2)}, u32[]{:S(2)}) async-start(bf16[32,32,128]{2,1,0:T(8,128)(2,1)} %get-tuple-element.22), calls=%async_computation | async-start | bytes 524288 | tf_op jit(solution)/shard_map/all_to_all | solution.py:367
  15.2 7.9 %collective-permute-start = (bf16[32,128]{1,0:T(8,128)(2,1)}, bf16[32,128]{1,0:T(8,128)(2,1)S(1)}, u32[]{:S(2)}, u32[]{:S(2)}) collective-permute-start(bf16[32,128]{1,0:T(8,128)(2,1)} %get-tuple-element.23), channel_id=1, source_target_pairs={{0,0},{1,1},{2,32},{3,33},{32,2},{33,3},{34,34},{35,35},{4,4},{5,5... | collective-permute-start | bytes 24584 | tf_op jit(solution)/shard_map/ppermute | solution.py:396
  16.5 6.6 %collective-permute-start.1 = (bf16[32,128]{1,0:T(8,128)(2,1)}, bf16[32,128]{1,0:T(8,128)(2,1)S(1)}, u32[]{:S(2)}, u32[]{:S(2)}) collective-permute-start(bf16[32,128]{1,0:T(8,128)(2,1)} %get-tuple-element.24), channel_id=1, source_target_pairs={{0,1},{1,0},{2,33},{3,32},{32,3},{33,2},{34,35},{35,34},{4,5},{5,4... | collective-permute-start | bytes 24584 | tf_op jit(solution)/shard_map/ppermute | solution.py:396
  20.9 0.7 copy-start.1
  21.6 0.7 copy-start.2
  22.2 0.7 copy-start.3
  91.0 12.2 %all-to-all-start.4 = ((bf16[8,32,128]{2,1,0:T(8,128)(2,1)}), bf16[8,32,128]{2,1,0:T(8,128)(2,1)S(1)}, u32[]{:S(2)}, u32[]{:S(2)}) async-start(bf16[8,32,128]{2,1,0:T(8,128)(2,1)} %get-tuple-element.35), calls=%async_computation.4 | async-start | bytes 131072 | tf_op jit(solution)/shard_map/all_to_all | solution.py:367
  94.4 3.5 %collective-permute-start.2 = (bf16[32,128]{1,0:T(8,128)(2,1)S(1)}, bf16[32,128]{1,0:T(8,128)(2,1)S(1)}, u32[]{:S(2)}, u32[]{:S(2)}) collective-permute-start(bf16[32,128]{1,0:T(8,128)(2,1)S(1)} %get-tuple-element.36), channel_id=1, source_target_pairs={{0,32},{32,0},{1,33},{33,1},{2,34},{34,2},{3,35},{35,3},{4,36},{36... | collective-permute-start | bytes 24584 | tf_op jit(solution)/shard_map/ppermute | solution.py:425

commit v11 on v9

--- a/solution.py
+++ b/solution.py
@@ -43,13 +43,13 @@
     return jax.ShapeDtypeStruct(dims, dtype)
 
 
-def call(kernel, outs, n_in, scratch=(), scalars=(), first=VMEM, limit=32):
+def call(kernel, outs, n_in, scratch=(), scalars=(), first=VMEM, last=VMEM, limit=32):
     specs = [SMEM if n in scalars else first for n in range(n_in)]
     return pl.pallas_call(
         kernel,
         out_shape=outs,
         in_specs=specs,
-        out_specs=jax.tree.map(lambda _: VMEM, outs),
+        out_specs=jax.tree.map(lambda _: last, outs),
         scratch_shapes=list(scratch),
         compiler_params=pltpu.CompilerParams(vmem_limit_bytes=limit * 1024 * 1024),
     )
@@ -86,25 +86,32 @@
 INNER = [(zh, core, j) for zh in range(2) for core in range(2) for j in range(2)]
 
 
-def spread_kernel(x_hbm, e_hbm, out_ref, even_ref, odd_ref, x_ref, e_ref, sems):
-    pairs = ((x_hbm, x_ref), (e_hbm, e_ref))
-    copies = [pltpu.make_async_copy(a, b, sems.at[n]) for n, (a, b) in enumerate(pairs)]
+def spread_kernel(x_hbm, e_hbm, out_hbm, even_hbm, odd_hbm, x_ref, e_ref, block_ref, even_ref, odd_ref, sems):
+    fetches = [
+        pltpu.make_async_copy(x_hbm, x_ref, sems.at[NC + 2]),
+        pltpu.make_async_copy(e_hbm, e_ref, sems.at[NC + 3]),
+    ]
+    for fetch in fetches:
+        fetch.start()
+    fetches[0].wait()
+    for j in range(2):
+        block_ref[j * VECS : (j + 1) * VECS] = x_ref[:, j, :]
+    copies = [pltpu.make_async_copy(block_ref, out_hbm.at[c], sems.at[c]) for c in range(NC)]
     for copy in copies:
         copy.start()
-    for copy in copies:
-        copy.wait()
-    for j in range(2):
-        value = x_ref[:, j, :]
-        for c in range(NC):
-            out_ref[c, j * VECS : (j + 1) * VECS] = value
+    fetches[1].wait()
     odd = lax.rem(lax.axis_index("zl"), 2)
     row = lax.broadcasted_iota(jnp.int32, (VECS, LANES), 0)
-    for k, message in enumerate((even_ref, odd_ref)):
+    for k, (message, target) in enumerate(((even_ref, even_hbm), (odd_ref, odd_hbm))):
         message[:VECS] = jnp.where(odd == k, x_ref[:, 0, :], x_ref[:, 1, :])
         terms = jnp.zeros((VECS, LANES), F32)
         for n, term in enumerate(split3(jnp.where(odd == k, e_ref[0:1], e_ref[1:2]))):
             terms = jnp.where(row == n, term.astype(F32), terms)
         message[VECS:] = terms.astype(BF16)
+        copies.append(pltpu.make_async_copy(message, target, sems.at[NC + k]))
+        copies[-1].start()
+    for copy in copies:
+        copy.wait()
 
 
 def index_kernel(coords_ref, counts_ref, e_ref, x_ref, index_ref, energy_ref, gram_ref, cross_ref):
@@ -195,7 +202,7 @@
                 acc[at + 1] = zero
         return carry
 
-    lax.fori_loop(0, 4, duplicate, 0)
+    lax.fori_loop(0, 4, duplicate, 0, unroll=2)
     for field, acc, dead in ((field_row, acc_row, ROW_DEAD), (field_col, acc_col, COL_DEAD)):
         field[dead] = zero.astype(BF16)
         acc[dead] = zero
@@ -234,20 +241,20 @@
                 chunk, rows = locate(not first, x, zh, core, j, slot)
                 out_ref[chunk, rows] = total.astype(BF16)
                 if first and slot == 2:
-                    for n, term in enumerate(split3(total)):
+                    for n, term in enumerate(split2(total)):
                         scratch[6][n, piece] = term
         return carry
 
     if not first:
-        lax.fori_loop(0, 4, pack, 0)
+        lax.fori_loop(0, 4, pack, 0, unroll=2)
         for j in range(2):
             own_ref[j] = x_ref[own_piece + j, part(2)]
         return
 
-    lax.fori_loop(0, 4, pack, 0)
+    lax.fori_loop(0, 4, pack, 0, unroll=2)
     terms = scratch[6]
     left = jnp.concatenate(
-        [jnp.concatenate([terms[n, p] for p in range(PIECES)], axis=1) for n in range(3)], axis=0
+        [jnp.concatenate([terms[n, p] for p in range(PIECES)], axis=1) for n in range(2)], axis=0
     )
     pieces = []
     for x in range(4):
@@ -257,7 +264,7 @@
     crosses = lax.dot_general(
         left, jnp.concatenate(pieces, axis=1), NT_DIMS, preferred_element_type=F32
     )
-    cross = crosses[:VECS] + crosses[VECS : 2 * VECS] + crosses[2 * VECS :]
+    cross = crosses[:VECS] + crosses[VECS:]
     message = message_of(gram_ref[...], cross_ref[...] + widen(cross))
     for p in range(PIECES):
         out_ref[p, 3 * VECS :] = message
@@ -385,9 +392,13 @@
         [
             pltpu.VMEM((VECS, 2, LANES), BF16),
             pltpu.VMEM((2, LANES), F32),
-            pltpu.SemaphoreType.DMA((2,)),
+            pltpu.VMEM((2 * VECS, LANES), BF16),
+            pltpu.VMEM((2 * VECS, LANES), BF16),
+            pltpu.VMEM((2 * VECS, LANES), BF16),
+            pltpu.SemaphoreType.DMA((NC + 4,)),
         ],
         first=pl.BlockSpec(memory_space=pl.ANY),
+        last=pl.BlockSpec(memory_space=pl.ANY),
         limit=60,
     )(vectors, energies)
     received = [
@@ -409,7 +420,7 @@
         functools.partial(tiles_kernel, True),
         shape(PIECES, 3 * VECS + MESSAGE, LANES),
         5,
-        scratch + [pltpu.VMEM((3, PIECES, VECS, LANES), BF16)],
+        scratch + [pltpu.VMEM((2, PIECES, VECS, LANES), BF16)],
     )(index, fields, tiles, gram, cross)
     by_owner, back = call(
         collect_owner_kernel,

time: 165 us -> 165 us (level)
  no operation moved by 1% of the time
where the time goes in v11:
time: 165 us; the launch traced here: 163 us
  blocking collectives  129 us (78%)
  starting transfers between devices  18 us (11%)
  Pallas kernels  8.29 us (5%)
  waiting for transfers between devices  4.6 us (3%)
  local copies, waits for them, and re-layouts  2.05 us (1%)
    all_to_all x7, blocking collectives, exchange(): return lax.all_to_all(value, axis, split_axis=0, concat_axis=0, tiled=True)  129 us
    all_to_all x1, starting transfers between devices, exchange(): return lax.all_to_all(value, axis, split_axis=0, concat_axis=0, tiled=True)  12.9 us
    ppermute x2, starting transfers between devices, shards(): lax.ppermute(message, ('core', 'zl'), [owner_of(n, k) for n in range(8)])  5.05 us
    all_to_all x1, waiting for transfers between devices, exchange(): return lax.all_to_all(value, axis, split_axis=0, concat_axis=0, tiled=True)  4.57 us
  transfers between devices with their start and end apart: 3, of which 1 were waited for; matrix products, arithmetic and copies ran while one was open for 0% of the time, Pallas kernels for 0%

profile of v11, /device:TPU:6, one launch (start us, length us, event | category | flops | bytes accessed | tf_op | source)
XLA Modules:
  0.0 163.1 jit_solution(302715446218777601)
XLA Ops:
  0.6 0.0 copy-start
  0.6 1.9 %shard_map.68 = (bf16[32,32,128]{2,1,0:T(8,128)(2,1)}, bf16[32,128]{1,0:T(8,128)(2,1)}, bf16[32,128]{1,0:T(8,128)(2,1)}) custom-call(bf16[16,2,128]{2,1,0:T(2,128)(2,1)} %x_ref.1, f32[2,128]{1,0:T(2,128)} %e_ref.1), custom_call_target="tpu_custom_call" | custom-call | tf_op jit(solution)/shard_map/pallas_call | solution.py:388
  2.5 12.9 %all-to-all-start = ((bf16[32,32,128]{2,1,0:T(8,128)(2,1)}), bf16[32,32,128]{2,1,0:T(8,128)(2,1)S(1)}, u32[]{:S(2)}, u32[]{:S(2)}) async-start(bf16[32,32,128]{2,1,0:T(8,128)(2,1)} %get-tuple-element.20), calls=%async_computation | async-start | bytes 524288 | tf_op jit(solution)/shard_map/all_to_all | solution.py:372
  15.4 1.4 collective-permute-start
  16.8 3.7 %collective-permute-start.1 = (bf16[32,128]{1,0:T(8,128)(2,1)}, bf16[32,128]{1,0:T(8,128)(2,1)S(1)}, u32[]{:S(2)}, u32[]{:S(2)}) collective-permute-start(bf16[32,128]{1,0:T(8,128)(2,1)} %get-tuple-element.22), channel_id=1, source_target_pairs={{0,1},{1,0},{2,33},{3,32},{32,3},{33,2},{34,35},{35,34},{4,5},{5,4... | collective-permute-start | bytes 24584 | tf_op jit(solution)/shard_map/ppermute | solution.py:405
  21.1 0.0 copy-start.1
  21.2 0.7 copy-done.1
  21.8 0.0 copy-start.2
  21.8 0.7 copy-done.2
  22.5 0.0 copy-start.3
  22.5 0.7 copy-done.3
  23.2 0.2 shard_map.69
  23.4 0.0 collective-permute-done.even_ref
  23.4 0.0 collective-permute-done.1.odd_ref
  23.4 4.6 %all-to-all-done.in_ref = bf16[32,32,128]{2,1,0:T(8,128)(2,1)S(1)} async-done(((bf16[32,32,128]{2,1,0:T(8,128)(2,1)}), bf16[32,32,128]{2,1,0:T(8,128)(2,1)S(1)}, u32[]{:S(2)}, u32[]{:S(2)}) %all-to-all-start) | async-done | bytes 262176 | tf_op jit(solution)/shard_map/all_to_all | solution.py:372
  28.0 22.8 %all_to_all.40.refs_1_ = bf16[16,96,128]{2,1,0:T(8,128)(2,1)S(1)} all-to-all(bf16[16,96,128]{2,1,0:T(8,128)(2,1)S(1)} %get-tuple-element.26), channel_id=1, replica_groups=mesh['zh'=2,'x'=4,'core'=2,'y'=8,'zl'=4] {'core','x','zh'}, dimensions={0} | all-to-all | bytes 786432 | tf_op jit(solution)/shard_map/all_to_all | solution.py:372
  50.8 0.0 copy-done
  50.8 2.6 %shard_map.71 = bf16[32,56,128]{2,1,0:T(8,128)(2,1)S(1)} custom-call(s32[2,128]{1,0:T(2,128)S(1)} %get-tuple-element.25.refs_0_, bf16[16,96,128]{2,1,0:T(8,128)(2,1)S(1)} %all_to_all.40.refs_1_, bf16[64,64,128]{2,1,0:T(8,128)(2,1)S(1)} %bitcast.1, f32[16,128]{1,0:T(8,128)S(1)} %get-tuple-element.27.refs_3_, f32[16,128]{1,0:T(8,128)S(1)} %get-tuple-element.28.refs_4_), custom_call_target="tpu_custom_call" | custom-call | tf_op jit(solution)/shard_map/pallas_call | solution.py:419
  53.3 21.9 %all_to_all.41.in_ref = bf16[32,56,128]{2,1,0:T(8,128)(2,1)S(1)} all-to-all(bf16[32,56,128]{2,1,0:T(8,128)(2,1)S(1)} %shard_map.71), channel_id=1, replica_groups=mesh['zh'=2,'x'=4,'core'=2,'y'=8,'zl'=4] {'x','zh','zl'}, dimensions={0} | all-to-all | bytes 917504 | tf_op jit(solution)/shard_map/all_to_all | solution.py:372
  75.3 0.3 shard_map.72
  75.6 14.2 %all_to_all.42.in_ref = bf16[16,40,128]{2,1,0:T(8,128)(2,1)S(1)} all-to-all(bf16[16,40,128]{2,1,0:T(8,128)(2,1)S(1)} %get-tuple-element.29), channel_id=1, replica_groups=mesh['zh'=2,'x'=4,'core'=2,'y'=8,'zl'=4] {'y','core'}, dimensions={0} | all-to-all | bytes 327680 | tf_op jit(solution)/shard_map/all_to_all | solution.py:372
  89.8 0.6 shard_map.73
  90.4 11.8 %all_to_all.43.in_ref = bf16[16,32,128]{2,1,0:T(8,128)(2,1)S(1)} all-to-all(bf16[16,32,128]{2,1,0:T(8,128)(2,1)S(1)} %shard_map.73), channel_id=1, replica_groups=mesh['zh'=2,'x'=4,'core'=2,'y'=8,'zl'=4] {'y','core'}, dimensions={0} | all-to-all | bytes 262144 | tf_op jit(solution)/shard_map/all_to_all | solution.py:372
  102.1 0.1 shard_map.74
  102.2 20.3 %all_to_all.44.refs_1_ = bf16[32,48,128]{2,1,0:T(8,128)(2,1)S(1)} all-to-all(bf16[32,48,128]{2,1,0:T(8,128)(2,1)S(1)} %shard_map.74), channel_id=1, replica_groups=mesh['zh'=2,'x'=4,'core'=2,'y'=8,'zl'=4] {'x','zh','zl'}, dimensions={0} | all-to-all | bytes 786432 | tf_op jit(solution)/shard_map/all_to_all | solution.py:372
  122.4 2.0 %shard_map.75 = (bf16[16,96,128]{2,1,0:T(8,128)(2,1)S(1)}, bf16[2,16,128]{2,1,0:T(8,128)(2,1)S(1)}) custom-call(s32[2,128]{1,0:T(2,128)S(1)} %get-tuple-element.25.refs_0_, bf16[32,48,128]{2,1,0:T(8,128)(2,1)S(1)} %all_to_all.44.refs_1_, bf16[64,64,128]{2,1,0:T(8,128)(2,1)S(1)} %bitcast.2), custom_call_target="tpu_custom_call" | custom-call | tf_op jit(solution)/shard_map/pallas_call | solution.py:435
  124.5 17.4 %all_to_all.45.in_ref = bf16[16,96,128]{2,1,0:T(8,128)(2,1)S(1)} all-to-all(bf16[16,96,128]{2,1,0:T(8,128)(2,1)S(1)} %get-tuple-element.33), channel_id=1, replica_groups=mesh['zh'=2,'x'=4,'core'=2,'y'=8,'zl'=4] {'core','x','zh'}, dimensions={0} | all-to-all | bytes 786432 | tf_op jit(solution)/shard_map/all_to_all | solution.py:372
  141.9 20.5 %all_to_all.46.in_ref = bf16[32,32,128]{2,1,0:T(8,128)(2,1)S(1)} all-to-all(bf16[32,32,128]{2,1,0:T(8,128)(2,1)S(1)} %get-tuple-element.34), channel_id=1, replica_groups=mesh['zh'=2,'x'=4,'core'=2,'y'=8,'zl'=4] {'zl','y'}, dimensions={0} | all-to-all | bytes 524288 | tf_op jit(solution)/shard_map/all_to_all | solution.py:372
  162.4 0.7 shard_map.77
  (2 shorter events, 0.1 us)
Async XLA Ops:
  0.6 50.1 %copy-start = (bf16[1,64,64,128]{3,2,1,0:T(8,128)(2,1)S(1)}, bf16[1,64,64,128]{3,2,1,0:T(8,128)(2,1)}, u32[]{:S(2)}) copy-start(bf16[1,64,64,128]{3,2,1,0:T(8,128)(2,1)} %param.6) | copy-start | bytes 3145732
  2.5 25.5 %all-to-all-start = ((bf16[32,32,128]{2,1,0:T(8,128)(2,1)}), bf16[32,32,128]{2,1,0:T(8,128)(2,1)S(1)}, u32[]{:S(2)}, u32[]{:S(2)}) async-start(bf16[32,32,128]{2,1,0:T(8,128)(2,1)} %get-tuple-element.20), calls=%async_computation | async-start | bytes 524288 | tf_op jit(solution)/shard_map/all_to_all | solution.py:372
  15.4 7.9 %collective-permute-start = (bf16[32,128]{1,0:T(8,128)(2,1)}, bf16[32,128]{1,0:T(8,128)(2,1)S(1)}, u32[]{:S(2)}, u32[]{:S(2)}) collective-permute-start(bf16[32,128]{1,0:T(8,128)(2,1)} %get-tuple-element.21), channel_id=1, source_target_pairs={{0,0},{1,1},{2,32},{3,33},{32,2},{33,3},{34,34},{35,35},{4,4},{5,5... | collective-permute-start | bytes 24584 | tf_op jit(solution)/shard_map/ppermute | solution.py:405
  16.8 6.6 %collective-permute-start.1 = (bf16[32,128]{1,0:T(8,128)(2,1)}, bf16[32,128]{1,0:T(8,128)(2,1)S(1)}, u32[]{:S(2)}, u32[]{:S(2)}) collective-permute-start(bf16[32,128]{1,0:T(8,128)(2,1)} %get-tuple-element.22), channel_id=1, source_target_pairs={{0,1},{1,0},{2,33},{3,32},{32,3},{33,2},{34,35},{35,34},{4,5},{5,4... | collective-permute-start | bytes 24584 | tf_op jit(solution)/shard_map/ppermute | solution.py:405
  21.1 0.7 copy-start.1
  21.8 0.7 copy-start.2
  22.5 0.7 copy-start.3

commit v12 on v9

--- a/solution.py
+++ b/solution.py
@@ -195,7 +195,7 @@
                 acc[at + 1] = zero
         return carry
 
-    lax.fori_loop(0, 4, duplicate, 0)
+    lax.fori_loop(0, 4, duplicate, 0, unroll=2)
     for field, acc, dead in ((field_row, acc_row, ROW_DEAD), (field_col, acc_col, COL_DEAD)):
         field[dead] = zero.astype(BF16)
         acc[dead] = zero
@@ -234,20 +234,20 @@
                 chunk, rows = locate(not first, x, zh, core, j, slot)
                 out_ref[chunk, rows] = total.astype(BF16)
                 if first and slot == 2:
-                    for n, term in enumerate(split3(total)):
+                    for n, term in enumerate(split2(total)):
                         scratch[6][n, piece] = term
         return carry
 
     if not first:
-        lax.fori_loop(0, 4, pack, 0)
+        lax.fori_loop(0, 4, pack, 0, unroll=2)
         for j in range(2):
             own_ref[j] = x_ref[own_piece + j, part(2)]
         return
 
-    lax.fori_loop(0, 4, pack, 0)
+    lax.fori_loop(0, 4, pack, 0, unroll=2)
     terms = scratch[6]
     left = jnp.concatenate(
-        [jnp.concatenate([terms[n, p] for p in range(PIECES)], axis=1) for n in range(3)], axis=0
+        [jnp.concatenate([terms[n, p] for p in range(PIECES)], axis=1) for n in range(2)], axis=0
     )
     pieces = []
     for x in range(4):
@@ -257,7 +257,7 @@
     crosses = lax.dot_general(
         left, jnp.concatenate(pieces, axis=1), NT_DIMS, preferred_element_type=F32
     )
-    cross = crosses[:VECS] + crosses[VECS : 2 * VECS] + crosses[2 * VECS :]
+    cross = crosses[:VECS] + crosses[VECS:]
     message = message_of(gram_ref[...], cross_ref[...] + widen(cross))
     for p in range(PIECES):
         out_ref[p, 3 * VECS :] = message
@@ -409,7 +409,7 @@
         functools.partial(tiles_kernel, True),
         shape(PIECES, 3 * VECS + MESSAGE, LANES),
         5,
-        scratch + [pltpu.VMEM((3, PIECES, VECS, LANES), BF16)],
+        scratch + [pltpu.VMEM((2, PIECES, VECS, LANES), BF16)],
     )(index, fields, tiles, gram, cross)
     by_owner, back = call(
         collect_owner_kernel,

time: 165 us -> 165 us (level)
  no operation moved by 1% of the time
where the time goes in v12:
time: 165 us; the launch traced here: 163 us
  blocking collectives  129 us (78%)
  starting transfers between devices  18 us (11%)
  Pallas kernels  7.98 us (5%)
  waiting for transfers between devices  4.6 us (3%)
  local copies, waits for them, and re-layouts  2.05 us (1%)
    all_to_all x7, blocking collectives, exchange(): return lax.all_to_all(value, axis, split_axis=0, concat_axis=0, tiled=True)  129 us
    all_to_all x1, starting transfers between devices, exchange(): return lax.all_to_all(value, axis, split_axis=0, concat_axis=0, tiled=True)  12.9 us
    ppermute x2, starting transfers between devices, shards(): lax.ppermute(message, ('core', 'zl'), [owner_of(n, k) for n in range(8)])  5.05 us
    all_to_all x1, waiting for transfers between devices, exchange(): return lax.all_to_all(value, axis, split_axis=0, concat_axis=0, tiled=True)  4.57 us
  transfers between devices with their start and end apart: 3, of which 1 were waited for; matrix products, arithmetic and copies ran while one was open for 0% of the time, Pallas kernels for 0%

profile of v12, /device:TPU:6, one launch (start us, length us, event | category | flops | bytes accessed | tf_op | source)
XLA Modules:
  0.0 163.2 jit_solution(7902048799632220574)
XLA Ops:
  0.6 0.0 copy-start
  0.6 1.6 shard_map.68
  2.2 12.9 %all-to-all-start = ((bf16[32,32,128]{2,1,0:T(8,128)(2,1)}), bf16[32,32,128]{2,1,0:T(8,128)(2,1)S(1)}, u32[]{:S(2)}, u32[]{:S(2)}) async-start(bf16[32,32,128]{2,1,0:T(8,128)(2,1)} %get-tuple-element.20), calls=%async_computation | async-start | bytes 524288 | tf_op jit(solution)/shard_map/all_to_all | solution.py:365
  15.2 1.4 collective-permute-start
  16.5 3.7 %collective-permute-start.1 = (bf16[32,128]{1,0:T(8,128)(2,1)}, bf16[32,128]{1,0:T(8,128)(2,1)S(1)}, u32[]{:S(2)}, u32[]{:S(2)}) collective-permute-start(bf16[32,128]{1,0:T(8,128)(2,1)} %get-tuple-element.22), channel_id=1, source_target_pairs={{0,1},{1,0},{2,33},{3,32},{32,3},{33,2},{34,35},{35,34},{4,5},{5,4... | collective-permute-start | bytes 24584 | tf_op jit(solution)/shard_map/ppermute | solution.py:394
  20.9 0.0 copy-start.1
  20.9 0.7 copy-done.1
  21.6 0.0 copy-start.2
  21.6 0.7 copy-done.2
  22.3 0.0 copy-start.3
  22.3 0.7 copy-done.3
  22.9 0.2 shard_map.69
  23.1 0.0 collective-permute-done.even_ref
  23.1 0.0 collective-permute-done.1.odd_ref
  23.1 4.6 %all-to-all-done.in_ref = bf16[32,32,128]{2,1,0:T(8,128)(2,1)S(1)} async-done(((bf16[32,32,128]{2,1,0:T(8,128)(2,1)}), bf16[32,32,128]{2,1,0:T(8,128)(2,1)S(1)}, u32[]{:S(2)}, u32[]{:S(2)}) %all-to-all-start) | async-done | bytes 262176 | tf_op jit(solution)/shard_map/all_to_all | solution.py:365
  27.7 22.8 %all_to_all.40.refs_1_ = bf16[16,96,128]{2,1,0:T(8,128)(2,1)S(1)} all-to-all(bf16[16,96,128]{2,1,0:T(8,128)(2,1)S(1)} %get-tuple-element.26), channel_id=1, replica_groups=mesh['zh'=2,'x'=4,'core'=2,'y'=8,'zl'=4] {'core','x','zh'}, dimensions={0} | all-to-all | bytes 786432 | tf_op jit(solution)/shard_map/all_to_all | solution.py:365
  50.5 0.0 copy-done
  50.5 2.5 %shard_map.71 = bf16[32,56,128]{2,1,0:T(8,128)(2,1)S(1)} custom-call(s32[2,128]{1,0:T(2,128)S(1)} %get-tuple-element.25.refs_0_, bf16[16,96,128]{2,1,0:T(8,128)(2,1)S(1)} %all_to_all.40.refs_1_, bf16[64,64,128]{2,1,0:T(8,128)(2,1)S(1)} %bitcast.1, f32[16,128]{1,0:T(8,128)S(1)} %get-tuple-element.27.refs_3_, f32[16,128]{1,0:T(8,128)S(1)} %get-tuple-element.28.refs_4_), custom_call_target="tpu_custom_call" | custom-call | tf_op jit(solution)/shard_map/pallas_call | solution.py:408
  53.0 21.9 %all_to_all.41.in_ref = bf16[32,56,128]{2,1,0:T(8,128)(2,1)S(1)} all-to-all(bf16[32,56,128]{2,1,0:T(8,128)(2,1)S(1)} %shard_map.71), channel_id=1, replica_groups=mesh['zh'=2,'x'=4,'core'=2,'y'=8,'zl'=4] {'x','zh','zl'}, dimensions={0} | all-to-all | bytes 917504 | tf_op jit(solution)/shard_map/all_to_all | solution.py:365
  74.9 0.3 shard_map.72
  75.2 14.3 %all_to_all.42.in_ref = bf16[16,40,128]{2,1,0:T(8,128)(2,1)S(1)} all-to-all(bf16[16,40,128]{2,1,0:T(8,128)(2,1)S(1)} %get-tuple-element.29), channel_id=1, replica_groups=mesh['zh'=2,'x'=4,'core'=2,'y'=8,'zl'=4] {'y','core'}, dimensions={0} | all-to-all | bytes 327680 | tf_op jit(solution)/shard_map/all_to_all | solution.py:365
  89.6 0.6 shard_map.73
  90.2 11.8 %all_to_all.43.in_ref = bf16[16,32,128]{2,1,0:T(8,128)(2,1)S(1)} all-to-all(bf16[16,32,128]{2,1,0:T(8,128)(2,1)S(1)} %shard_map.73), channel_id=1, replica_groups=mesh['zh'=2,'x'=4,'core'=2,'y'=8,'zl'=4] {'y','core'}, dimensions={0} | all-to-all | bytes 262144 | tf_op jit(solution)/shard_map/all_to_all | solution.py:365
  101.9 0.1 shard_map.74
  102.0 20.3 %all_to_all.44.refs_1_ = bf16[32,48,128]{2,1,0:T(8,128)(2,1)S(1)} all-to-all(bf16[32,48,128]{2,1,0:T(8,128)(2,1)S(1)} %shard_map.74), channel_id=1, replica_groups=mesh['zh'=2,'x'=4,'core'=2,'y'=8,'zl'=4] {'x','zh','zl'}, dimensions={0} | all-to-all | bytes 786432 | tf_op jit(solution)/shard_map/all_to_all | solution.py:365
  122.3 2.0 %shard_map.75 = (bf16[16,96,128]{2,1,0:T(8,128)(2,1)S(1)}, bf16[2,16,128]{2,1,0:T(8,128)(2,1)S(1)}) custom-call(s32[2,128]{1,0:T(2,128)S(1)} %get-tuple-element.25.refs_0_, bf16[32,48,128]{2,1,0:T(8,128)(2,1)S(1)} %all_to_all.44.refs_1_, bf16[64,64,128]{2,1,0:T(8,128)(2,1)S(1)} %bitcast.2), custom_call_target="tpu_custom_call" | custom-call | tf_op jit(solution)/shard_map/pallas_call | solution.py:424
  124.3 17.5 %all_to_all.45.in_ref = bf16[16,96,128]{2,1,0:T(8,128)(2,1)S(1)} all-to-all(bf16[16,96,128]{2,1,0:T(8,128)(2,1)S(1)} %get-tuple-element.33), channel_id=1, replica_groups=mesh['zh'=2,'x'=4,'core'=2,'y'=8,'zl'=4] {'core','x','zh'}, dimensions={0} | all-to-all | bytes 786432 | tf_op jit(solution)/shard_map/all_to_all | solution.py:365
  141.8 20.8 %all_to_all.46.in_ref = bf16[32,32,128]{2,1,0:T(8,128)(2,1)S(1)} all-to-all(bf16[32,32,128]{2,1,0:T(8,128)(2,1)S(1)} %get-tuple-element.34), channel_id=1, replica_groups=mesh['zh'=2,'x'=4,'core'=2,'y'=8,'zl'=4] {'zl','y'}, dimensions={0} | all-to-all | bytes 524288 | tf_op jit(solution)/shard_map/all_to_all | solution.py:365
  162.5 0.7 shard_map.77
  (2 shorter events, 0.1 us)
Async XLA Ops:
  0.6 49.9 %copy-start = (bf16[1,64,64,128]{3,2,1,0:T(8,128)(2,1)S(1)}, bf16[1,64,64,128]{3,2,1,0:T(8,128)(2,1)}, u32[]{:S(2)}) copy-start(bf16[1,64,64,128]{3,2,1,0:T(8,128)(2,1)} %param.6) | copy-start | bytes 3145732
  2.2 25.5 %all-to-all-start = ((bf16[32,32,128]{2,1,0:T(8,128)(2,1)}), bf16[32,32,128]{2,1,0:T(8,128)(2,1)S(1)}, u32[]{:S(2)}, u32[]{:S(2)}) async-start(bf16[32,32,128]{2,1,0:T(8,128)(2,1)} %get-tuple-element.20), calls=%async_computation | async-start | bytes 524288 | tf_op jit(solution)/shard_map/all_to_all | solution.py:365
  15.2 7.9 %collective-permute-start = (bf16[32,128]{1,0:T(8,128)(2,1)}, bf16[32,128]{1,0:T(8,128)(2,1)S(1)}, u32[]{:S(2)}, u32[]{:S(2)}) collective-permute-start(bf16[32,128]{1,0:T(8,128)(2,1)} %get-tuple-element.21), channel_id=1, source_target_pairs={{0,0},{1,1},{2,32},{3,33},{32,2},{33,3},{34,34},{35,35},{4,4},{5,5... | collective-permute-start | bytes 24584 | tf_op jit(solution)/shard_map/ppermute | solution.py:394
  16.5 6.6 %collective-permute-start.1 = (bf16[32,128]{1,0:T(8,128)(2,1)}, bf16[32,128]{1,0:T(8,128)(2,1)S(1)}, u32[]{:S(2)}, u32[]{:S(2)}) collective-permute-start(bf16[32,128]{1,0:T(8,128)(2,1)} %get-tuple-element.22), channel_id=1, source_target_pairs={{0,1},{1,0},{2,33},{3,32},{32,3},{33,2},{34,35},{35,34},{4,5},{5,4... | collective-permute-start | bytes 24584 | tf_op jit(solution)/shard_map/ppermute | solution.py:394
  20.9 0.7 copy-start.1
  21.6 0.7 copy-start.2
  22.3 0.7 copy-start.3

commit v13 on v8

--- a/solution.py
+++ b/solution.py
@@ -187,7 +187,7 @@
                 acc[at + 1] = zero
         return carry
 
-    lax.fori_loop(0, 4, duplicate, 0)
+    lax.fori_loop(0, 4, duplicate, 0, unroll=2)
     for field, acc, dead in ((field_row, acc_row, ROW_DEAD), (field_col, acc_col, COL_DEAD)):
         field[dead] = zero.astype(BF16)
         acc[dead] = zero
@@ -226,20 +226,20 @@
                 chunk, rows = locate(not first, x, zh, core, j, slot)
                 out_ref[chunk, rows] = total.astype(BF16)
                 if first and slot == 2:
-                    for n, term in enumerate(split3(total)):
+                    for n, term in enumerate(split2(total)):
                         scratch[6][n, piece] = term
         return carry
 
     if not first:
-        lax.fori_loop(0, 4, pack, 0)
+        lax.fori_loop(0, 4, pack, 0, unroll=2)
         for j in range(2):
             own_ref[j] = x_ref[own_piece + j, part(2)]
         return
 
-    lax.fori_loop(0, 4, pack, 0)
+    lax.fori_loop(0, 4, pack, 0, unroll=2)
     terms = scratch[6]
     left = jnp.concatenate(
-        [jnp.concatenate([terms[n, p] for p in range(PIECES)], axis=1) for n in range(3)], axis=0
+        [jnp.concatenate([terms[n, p] for p in range(PIECES)], axis=1) for n in range(2)], axis=0
     )
     pieces = []
     for x in range(4):
@@ -249,7 +249,7 @@
     crosses = lax.dot_general(
         left, jnp.concatenate(pieces, axis=1), NT_DIMS, preferred_element_type=F32
     )
-    cross = crosses[:VECS] + crosses[VECS : 2 * VECS] + crosses[2 * VECS :]
+    cross = crosses[:VECS] + crosses[VECS:]
     gram = jnp.zeros((VECS, VECS), F32)
     for j in range(2):
         own = own_ref[j]
@@ -319,17 +319,19 @@
     wide = jnp.concatenate([cross, jnp.zeros((LANES - VECS, LANES), F32)], axis=0)
     cross = cross + jnp.transpose(wide)[:VECS]
     state = jnp.concatenate([gram, cross], axis=0)
-    lane = lax.broadcasted_iota(jnp.int32, (2 * VECS, LANES), 1)
+    columns = [jnp.broadcast_to(state[:, p : p + 1], (2 * VECS, LANES)) for p in range(VECS)]
     for p in range(VECS):
-        column = state[:, p : p + 1] * (1.0 / state[p : p + 1, p : p + 1])
-        state = jnp.where(lane == p, column, state - column * state[p : p + 1])
-    mix = state[VECS:]
+        scaled = columns[p] * (1.0 / columns[p][p : p + 1])
+        columns = [
+            scaled if q == p else column - scaled * column[p : p + 1]
+            for q, column in enumerate(columns)
+        ]
     for s in range(2):
         v = owned_ref[s].astype(F32)
         product = sum_over(in_ref, s * VECS, VECS) + back_ref[s] + e_ref[s : s + 1, :] * v
         shifted = jnp.zeros((VECS, LANES), F32)
         for k in range(VECS):
-            shifted = shifted + mix[:, k : k + 1] * v[k : k + 1, :]
+            shifted = shifted + columns[k][VECS:] * v[k : k + 1, :]
         value = (product - shifted).astype(BF16)
         for n in range(2 * 8):
             out_ref[n, s * VECS : (s + 1) * VECS] = value
@@ -404,7 +406,7 @@
         functools.partial(tiles_kernel, True),
         shape(PIECES, 3 * VECS + MESSAGE, LANES),
         5,
-        scratch + [pltpu.VMEM((3, PIECES, VECS, LANES), BF16)],
+        scratch + [pltpu.VMEM((2, PIECES, VECS, LANES), BF16)],
     )(index, fields, tiles, own, energies)
     by_owner, back = call(
         collect_owner_kernel,

time: 165 us -> 164 us (level)
  no operation moved by 1% of the time
where the time goes in v13:
time: 164 us; the launch traced here: 162 us
  blocking collectives  128 us (78%)
  starting transfers between devices  18 us (11%)
  Pallas kernels  7.76 us (5%)
  waiting for transfers between devices  5.45 us (3%)
    all_to_all x7, blocking collectives, exchange(): return lax.all_to_all(value, axis, split_axis=0, concat_axis=0, tiled=True)  128 us
    all_to_all x1, starting transfers between devices, exchange(): return lax.all_to_all(value, axis, split_axis=0, concat_axis=0, tiled=True)  12.9 us
    all_to_all x1, waiting for transfers between devices, exchange(): return lax.all_to_all(value, axis, split_axis=0, concat_axis=0, tiled=True)  5.23 us
    ppermute x2, starting transfers between devices, shards(): lax.ppermute(message, ('core', 'zl'), [owner_of(n, k) for n in range(8)])  5.05 us
  transfers between devices with their start and end apart: 3, of which 2 were waited for; matrix products, arithmetic and copies ran while one was open for 0% of the time, Pallas kernels for 0%

profile of v13, /device:TPU:6, one launch (start us, length us, event | category | flops | bytes accessed | tf_op | source)
XLA Modules:
  0.0 162.1 jit_solution(12343521503366131912)
XLA Ops:
  0.6 0.0 copy-start
  0.6 1.6 shard_map.68
  2.2 12.9 %all-to-all-start = ((bf16[32,32,128]{2,1,0:T(8,128)(2,1)}), bf16[32,32,128]{2,1,0:T(8,128)(2,1)S(1)}, u32[]{:S(2)}, u32[]{:S(2)}) async-start(bf16[32,32,128]{2,1,0:T(8,128)(2,1)} %get-tuple-element.19), calls=%async_computation | async-start | bytes 524288 | tf_op jit(solution)/shard_map/all_to_all | solution.py:363
  15.2 1.4 collective-permute-start
  16.5 3.7 %collective-permute-start.1 = (bf16[32,128]{1,0:T(8,128)(2,1)}, bf16[32,128]{1,0:T(8,128)(2,1)S(1)}, u32[]{:S(2)}, u32[]{:S(2)}) collective-permute-start(bf16[32,128]{1,0:T(8,128)(2,1)} %get-tuple-element.21), channel_id=1, source_target_pairs={{0,1},{1,0},{2,33},{3,32},{32,3},{33,2},{34,35},{35,34},{4,5},{5,4... | collective-permute-start | bytes 24584 | tf_op jit(solution)/shard_map/ppermute | solution.py:392
  20.9 0.0 copy-start.1
  20.9 0.7 copy-done.1
  21.6 0.0 copy-start.2
  21.6 0.7 copy-done.2
  22.3 0.0 collective-permute-done.even_ref
  22.3 0.2 collective-permute-done.1.odd_ref
  22.5 5.2 %all-to-all-done.in_ref = bf16[32,32,128]{2,1,0:T(8,128)(2,1)S(1)} async-done(((bf16[32,32,128]{2,1,0:T(8,128)(2,1)}), bf16[32,32,128]{2,1,0:T(8,128)(2,1)S(1)}, u32[]{:S(2)}, u32[]{:S(2)}) %all-to-all-start) | async-done | bytes 262176 | tf_op jit(solution)/shard_map/all_to_all | solution.py:363
  27.8 22.8 %all_to_all.40.refs_1_ = bf16[16,96,128]{2,1,0:T(8,128)(2,1)S(1)} all-to-all(bf16[16,96,128]{2,1,0:T(8,128)(2,1)S(1)} %get-tuple-element.25), channel_id=1, replica_groups=mesh['zh'=2,'x'=4,'core'=2,'y'=8,'zl'=4] {'core','x','zh'}, dimensions={0} | all-to-all | bytes 786432 | tf_op jit(solution)/shard_map/all_to_all | solution.py:363
  50.5 0.0 copy-done
  50.5 2.5 %shard_map.71 = bf16[32,56,128]{2,1,0:T(8,128)(2,1)S(1)} custom-call(s32[2,128]{1,0:T(2,128)S(1)} %get-tuple-element.24.refs_0_, bf16[16,96,128]{2,1,0:T(8,128)(2,1)S(1)} %all_to_all.40.refs_1_, bf16[64,64,128]{2,1,0:T(8,128)(2,1)S(1)} %bitcast.1, bf16[2,16,128]{2,1,0:T(8,128)(2,1)S(1)} %get-tuple-element.26.refs_3_, ...), custom_call_target="tpu_custom_call" | custom-call | tf_op jit(solution)/shard_map/pallas_call | solution.py:405
  53.0 22.0 %all_to_all.41.in_ref = bf16[32,56,128]{2,1,0:T(8,128)(2,1)S(1)} all-to-all(bf16[32,56,128]{2,1,0:T(8,128)(2,1)S(1)} %shard_map.71), channel_id=1, replica_groups=mesh['zh'=2,'x'=4,'core'=2,'y'=8,'zl'=4] {'x','zh','zl'}, dimensions={0} | all-to-all | bytes 917504 | tf_op jit(solution)/shard_map/all_to_all | solution.py:363
  75.0 0.3 shard_map.72
  75.3 13.2 %all_to_all.42.in_ref = bf16[16,40,128]{2,1,0:T(8,128)(2,1)S(1)} all-to-all(bf16[16,40,128]{2,1,0:T(8,128)(2,1)S(1)} %get-tuple-element.28), channel_id=1, replica_groups=mesh['zh'=2,'x'=4,'core'=2,'y'=8,'zl'=4] {'y','core'}, dimensions={0} | all-to-all | bytes 327680 | tf_op jit(solution)/shard_map/all_to_all | solution.py:363
  88.5 0.6 shard_map.73
  89.1 11.8 %all_to_all.43.in_ref = bf16[16,32,128]{2,1,0:T(8,128)(2,1)S(1)} all-to-all(bf16[16,32,128]{2,1,0:T(8,128)(2,1)S(1)} %shard_map.73), channel_id=1, replica_groups=mesh['zh'=2,'x'=4,'core'=2,'y'=8,'zl'=4] {'y','core'}, dimensions={0} | all-to-all | bytes 262144 | tf_op jit(solution)/shard_map/all_to_all | solution.py:363
  100.9 0.1 shard_map.74
  100.9 20.3 %all_to_all.44.refs_1_ = bf16[32,48,128]{2,1,0:T(8,128)(2,1)S(1)} all-to-all(bf16[32,48,128]{2,1,0:T(8,128)(2,1)S(1)} %shard_map.74), channel_id=1, replica_groups=mesh['zh'=2,'x'=4,'core'=2,'y'=8,'zl'=4] {'x','zh','zl'}, dimensions={0} | all-to-all | bytes 786432 | tf_op jit(solution)/shard_map/all_to_all | solution.py:363
  121.2 1.9 %shard_map.75 = (bf16[16,96,128]{2,1,0:T(8,128)(2,1)S(1)}, bf16[2,16,128]{2,1,0:T(8,128)(2,1)S(1)}) custom-call(s32[2,128]{1,0:T(2,128)S(1)} %get-tuple-element.24.refs_0_, bf16[32,48,128]{2,1,0:T(8,128)(2,1)S(1)} %all_to_all.44.refs_1_, bf16[64,64,128]{2,1,0:T(8,128)(2,1)S(1)} %bitcast.2), custom_call_target="tpu_custom_call" | custom-call | tf_op jit(solution)/shard_map/pallas_call | solution.py:421
  123.1 17.5 %all_to_all.45.in_ref = bf16[16,96,128]{2,1,0:T(8,128)(2,1)S(1)} all-to-all(bf16[16,96,128]{2,1,0:T(8,128)(2,1)S(1)} %get-tuple-element.32), channel_id=1, replica_groups=mesh['zh'=2,'x'=4,'core'=2,'y'=8,'zl'=4] {'core','x','zh'}, dimensions={0} | all-to-all | bytes 786432 | tf_op jit(solution)/shard_map/all_to_all | solution.py:363
  140.7 20.8 %all_to_all.46.in_ref = bf16[32,32,128]{2,1,0:T(8,128)(2,1)S(1)} all-to-all(bf16[32,32,128]{2,1,0:T(8,128)(2,1)S(1)} %get-tuple-element.33), channel_id=1, replica_groups=mesh['zh'=2,'x'=4,'core'=2,'y'=8,'zl'=4] {'zl','y'}, dimensions={0} | all-to-all | bytes 524288 | tf_op jit(solution)/shard_map/all_to_all | solution.py:363
  161.5 0.7 shard_map.77
  (3 shorter events, 0.1 us)
Async XLA Ops:
  0.6 49.9 %copy-start = (bf16[1,64,64,128]{3,2,1,0:T(8,128)(2,1)S(1)}, bf16[1,64,64,128]{3,2,1,0:T(8,128)(2,1)}, u32[]{:S(2)}) copy-start(bf16[1,64,64,128]{3,2,1,0:T(8,128)(2,1)} %param.6) | copy-start | bytes 3145732
  2.2 25.5 %all-to-all-start = ((bf16[32,32,128]{2,1,0:T(8,128)(2,1)}), bf16[32,32,128]{2,1,0:T(8,128)(2,1)S(1)}, u32[]{:S(2)}, u32[]{:S(2)}) async-start(bf16[32,32,128]{2,1,0:T(8,128)(2,1)} %get-tuple-element.19), calls=%async_computation | async-start | bytes 524288 | tf_op jit(solution)/shard_map/all_to_all | solution.py:363
  15.2 7.1 %collective-permute-start = (bf16[32,128]{1,0:T(8,128)(2,1)}, bf16[32,128]{1,0:T(8,128)(2,1)S(1)}, u32[]{:S(2)}, u32[]{:S(2)}) collective-permute-start(bf16[32,128]{1,0:T(8,128)(2,1)} %get-tuple-element.20), channel_id=1, source_target_pairs={{0,0},{1,1},{2,32},{3,33},{32,2},{33,3},{34,34},{35,35},{4,4},{5,5... | collective-permute-start | bytes 24584 | tf_op jit(solution)/shard_map/ppermute | solution.py:392
  16.5 5.9 %collective-permute-start.1 = (bf16[32,128]{1,0:T(8,128)(2,1)}, bf16[32,128]{1,0:T(8,128)(2,1)S(1)}, u32[]{:S(2)}, u32[]{:S(2)}) collective-permute-start(bf16[32,128]{1,0:T(8,128)(2,1)} %get-tuple-element.21), channel_id=1, source_target_pairs={{0,1},{1,0},{2,33},{3,32},{32,3},{33,2},{34,35},{35,34},{4,5},{5,4... | collective-permute-start | bytes 24584 | tf_op jit(solution)/shard_map/ppermute | solution.py:392
  20.9 0.7 copy-start.1
  21.6 0.7 copy-start.2
